TPU v7x, 32 devices: a whole 2x2x4 slice. The times are simulated.
32 devices in a mesh: ind: 8 (over y, x, core), snp: 4 (over z).
Axes of the slice: x: 2, y: 2, z: 4, core: 2. Of those that a mesh axis runs over, the one named last changes fastest.
Arguments:
- genotypes: int32 [8192, 4096], P('ind', 'snp'), may hold values from 0 to 2, as said below
- ancestry: float32 [16, 8192], P(None, ('ind', 'snp')), may hold values from 0 to 1, as said below
- freqs: float32 [16, 4096], P(None, ('snp', 'ind')), may hold values from 0.05 to 0.95
Outputs:
- ancestry_new: float32 [16, 8192], P(None, ('ind', 'snp'))
- freqs_new: float32 [16, 4096], P(None, ('snp', 'ind'))
Inputs may be any that keep to these rules, and one draw needn't show every extreme that they name: `genotypes`: each count is 0, 1 or 2. `ancestry`: all entries are positive and each column sums to one.
All inputs are finite; a program needn't handle non-finite values.
Results may differ from a plain program's by a relative error of at most 0.0001.
Values sent between devices are 32-bit elements; how exact they have to be, the bound alone decides.
No kernel may reach another device: no remote copies, remote signals or barrier semaphores. Data moves between devices by JAX's collectives and lax.ppermute only.
A program may use at most 64 MiB of HBM per device.

v0:
```python
import jax
import jax.numpy as jnp
from jax import lax
from jax.sharding import PartitionSpec as P

ITERS = 4


def fetch_ancestry(shard):
    return lax.all_gather(shard, "snp", axis=1, tiled=True)


def fetch_freqs(shard):
    return lax.all_gather(shard, "ind", axis=1, tiled=True)


def body(genotypes, ancestry, freqs):
    g_val = genotypes.astype(jnp.float32)
    snp_count = genotypes.shape[1] * lax.axis_size("snp")
    q_own = ancestry
    p_own = freqs
    q_full = fetch_ancestry(q_own)
    p_full = fetch_freqs(p_own)
    for step in range(ITERS):
        if step > 0:
            q_full = fetch_ancestry(q_own)
            p_full = fetch_freqs(p_own)
        expected = lax.dot_general(
            q_full, p_full, (((0,), (0,)), ((), ())), precision=lax.Precision.HIGHEST
        )
        ratio_one = g_val / expected
        ratio_two = (2.0 - g_val) / (1.0 - expected)
        q_sum = lax.dot_general(
            p_full, ratio_one - ratio_two, (((1,), (1,)), ((), ())), precision=lax.Precision.HIGHEST
        )
        q_sum = q_sum + jnp.sum(ratio_two, axis=1)[None, :]
        p_one = jnp.dot(q_full, ratio_one, precision=lax.Precision.HIGHEST)
        p_two = jnp.dot(q_full, ratio_two, precision=lax.Precision.HIGHEST)
        q_part = lax.psum_scatter(q_sum, "snp", scatter_dimension=1, tiled=True)
        q_own = q_own * q_part / (2.0 * snp_count)
        one_part, two_part = (
            lax.psum_scatter(p_one, "ind", scatter_dimension=1, tiled=True),
            lax.psum_scatter(p_two, "ind", scatter_dimension=1, tiled=True),
        )
        p_own = p_own * one_part / (p_own * one_part + (1.0 - p_own) * two_part)
    return (q_own, p_own)


def solution(mesh):
    in_specs = (P("ind", "snp"), P(None, ("ind", "snp")), P(None, ("snp", "ind")))
    out_specs = (P(None, ("ind", "snp")), P(None, ("snp", "ind")))
    return jax.shard_map(body, mesh=mesh, in_specs=in_specs, out_specs=out_specs, check_vma=False)
```

profile of v0, /device:TPU:0, one launch (start us, length us, event | category | flops | bytes accessed | tf_op | source)
XLA Modules:
  0.0 495.7 jit_solution(11370205347376229034)
XLA Ops:
  7.2 15.1 %all_gather.24 = f32[16,1024]{1,0:T(8,128)S(1)} all-gather(f32[16,256]{1,0:T(8,128)} %param.4), channel_id=1, replica_groups=mesh['ind'=8,'snp'=4] {'snp'}, dimensions={1}, use_global_device_ids=true | all-gather | bytes 81920 | tf_op jit(solution)/shard_map/all_gather | solution.py:10
  22.3 9.2 %all_gather.25 = f32[16,1024]{1,0:T(8,128)S(1)} all-gather(f32[16,128]{1,0:T(8,128)} %param.5), channel_id=1, replica_groups=mesh['ind'=8,'snp'=4] {'ind'}, dimensions={1}, use_global_device_ids=true | all-gather | bytes 73728 | tf_op jit(solution)/shard_map/all_gather | solution.py:14
  36.9 9.9 %fusion.29 = (f32[1024]{0:T(1024)S(1)}, f32[1024,1024]{0,1:T(8,128)S(1)}, f32[1024,1024]{0,1:T(8,128)}) fusion(s32[1024,1024]{0,1:T(8,128)} %copy.5, f32[16,1024]{1,0:T(8,128)S(1)} %all_gather.24, f32[16,1024]{1,0:T(8,128)S(1)} %all_gather.25), kind=kOutput, calls=%fused_computation.38 | convolution fusion | flops 206568448 | bytes 12718080 | tf_op jit(solution)/shard_map/dot_general | solution.py:28
  53.1 8.2 %convolution_bitcast_fusion.1 = f32[16,1024]{1,0:T(8,128)} fusion(f32[16,1024]{1,0:T(8,128)S(1)} %all_gather.24, f32[1024,1024]{0,1:T(8,128)} %get-tuple-element.10, s32[1024,1024]{0,1:T(8,128)} %copy.5), kind=kOutput, calls=%fused_computation.23 | convolution fusion | flops 203423744 | bytes 8519680 | tf_op jit(solution)/shard_map/dot_general | solution.py:37
  61.8 8.2 %fusion.11 = f32[16,1024]{1,0:T(8,128)} fusion(f32[16,1024]{1,0:T(8,128)S(1)} %all_gather.25, f32[1024,1024]{0,1:T(8,128)} %copy-done.1, f32[1024]{0:T(1024)S(1)} %get-tuple-element.8, f32[1024,1024]{0,1:T(8,128)} %get-tuple-element.10, s32[1024,1024]{0,1:T(8,128)} %copy.5), kind=kOutput, calls=%fused_computation.18 | convolution fusion | flops 204488704 | bytes 12718080 | tf_op jit(solution)/shard_map/dot_general | solution.py:33
  70.1 14.5 %reduce-scatter.17.cloned.1.call-done = f32[16,128]{1,0:T(8,128)} async-done(((f32[16,1024]{1,0:T(8,128)}), f32[16,128]{1,0:T(8,128)}) %reduce-scatter.17.cloned.1.call-update) | async-done | bytes 8208 | tf_op jit(solution)/shard_map/reduce_scatter | solution.py:43
  84.6 34.8 %reduce-scatter.15.cloned.1.call-done = f32[16,128]{1,0:T(8,128)} async-done(((f32[16,1024]{1,0:T(8,128)}), f32[16,128]{1,0:T(8,128)}) %reduce-scatter.15.cloned.1.call-update) | async-done | bytes 8208 | tf_op jit(solution)/shard_map/reduce_scatter | solution.py:42
  120.1 9.0 %all_gather.26 = f32[16,1024]{1,0:T(8,128)S(1)} all-gather(f32[16,128]{1,0:T(8,128)S(1)} %add_divide_fusion.3), channel_id=1, replica_groups=mesh['ind'=8,'snp'=4] {'ind'}, dimensions={1}, use_global_device_ids=true | all-gather | bytes 73728 | tf_op jit(solution)/shard_map/all_gather | solution.py:14
  129.1 11.5 %reduce-scatter.13.cloned.1.call-done = f32[16,256]{1,0:T(8,128)} async-done(((f32[16,1024]{1,0:T(8,128)}), f32[16,256]{1,0:T(8,128)}) %reduce-scatter.13.cloned.1.call-update) | async-done | bytes 16400 | tf_op jit(solution)/shard_map/reduce_scatter | solution.py:39
  141.4 13.1 %all_gather.27 = f32[16,1024]{1,0:T(8,128)S(1)} all-gather(f32[16,256]{1,0:T(8,128)S(1)} %multiply_multiply_fusion.3), channel_id=1, replica_groups=mesh['ind'=8,'snp'=4] {'snp'}, dimensions={1}, use_global_device_ids=true | all-gather | bytes 81920 | tf_op jit(solution)/shard_map/all_gather | solution.py:10
  154.5 9.9 %fusion.28 = (f32[1024]{0:T(1024)S(1)}, f32[1024,1024]{0,1:T(8,128)S(1)}, f32[1024,1024]{0,1:T(8,128)}) fusion(s32[1024,1024]{0,1:T(8,128)} %copy.5, f32[16,1024]{1,0:T(8,128)S(1)} %all_gather.27, f32[16,1024]{1,0:T(8,128)S(1)} %all_gather.26), kind=kOutput, calls=%fused_computation.37 | convolution fusion | flops 206568448 | bytes 12718080 | tf_op jit(solution)/shard_map/dot_general | solution.py:28
  170.9 7.7 %fusion.23 = f32[16,1024]{1,0:T(8,128)} fusion(f32[16,1024]{1,0:T(8,128)S(1)} %all_gather.27, f32[1024,1024]{0,1:T(8,128)} %get-tuple-element.11, s32[1024,1024]{0,1:T(8,128)} %copy.5), kind=kOutput, calls=%fused_computation.32 | convolution fusion | flops 203423744 | bytes 8519680 | tf_op jit(solution)/shard_map/dot_general | solution.py:37
  178.6 8.0 %fusion.14 = f32[16,1024]{1,0:T(8,128)} fusion(f32[16,1024]{1,0:T(8,128)S(1)} %all_gather.26, f32[1024,1024]{0,1:T(8,128)} %copy-done.2, f32[1024]{0:T(1024)S(1)} %get-tuple-element.6, f32[1024,1024]{0,1:T(8,128)} %get-tuple-element.11, s32[1024,1024]{0,1:T(8,128)} %copy.5), kind=kOutput, calls=%fused_computation.19 | convolution fusion | flops 204488704 | bytes 12718080 | tf_op jit(solution)/shard_map/dot_general | solution.py:33
  186.7 13.7 %reduce-scatter.23.cloned.1.call-done = f32[16,128]{1,0:T(8,128)} async-done(((f32[16,1024]{1,0:T(8,128)}), f32[16,128]{1,0:T(8,128)}) %reduce-scatter.23.cloned.1.call-update) | async-done | bytes 8208 | tf_op jit(solution)/shard_map/reduce_scatter | solution.py:43
  200.4 34.3 %reduce-scatter.21.cloned.1.call-done = f32[16,128]{1,0:T(8,128)} async-done(((f32[16,1024]{1,0:T(8,128)}), f32[16,128]{1,0:T(8,128)}) %reduce-scatter.21.cloned.1.call-update) | async-done | bytes 8208 | tf_op jit(solution)/shard_map/reduce_scatter | solution.py:42
  235.4 9.0 %all_gather.28 = f32[16,1024]{1,0:T(8,128)S(1)} all-gather(f32[16,128]{1,0:T(8,128)S(1)} %add_divide_fusion.2), channel_id=1, replica_groups=mesh['ind'=8,'snp'=4] {'ind'}, dimensions={1}, use_global_device_ids=true | all-gather | bytes 73728 | tf_op jit(solution)/shard_map/all_gather | solution.py:14
  244.4 11.5 %reduce-scatter.19.cloned.1.call-done = f32[16,256]{1,0:T(8,128)} async-done(((f32[16,1024]{1,0:T(8,128)}), f32[16,256]{1,0:T(8,128)}) %reduce-scatter.19.cloned.1.call-update) | async-done | bytes 16400 | tf_op jit(solution)/shard_map/reduce_scatter | solution.py:39
  256.6 13.1 %all_gather.29 = f32[16,1024]{1,0:T(8,128)S(1)} all-gather(f32[16,256]{1,0:T(8,128)S(1)} %multiply_multiply_fusion.2), channel_id=1, replica_groups=mesh['ind'=8,'snp'=4] {'snp'}, dimensions={1}, use_global_device_ids=true | all-gather | bytes 81920 | tf_op jit(solution)/shard_map/all_gather | solution.py:10
  269.7 9.9 %fusion.27 = (f32[1024]{0:T(1024)S(1)}, f32[1024,1024]{0,1:T(8,128)S(1)}, f32[1024,1024]{0,1:T(8,128)}) fusion(s32[1024,1024]{0,1:T(8,128)} %copy.5, f32[16,1024]{1,0:T(8,128)S(1)} %all_gather.29, f32[16,1024]{1,0:T(8,128)S(1)} %all_gather.28), kind=kOutput, calls=%fused_computation.36 | convolution fusion | flops 206568448 | bytes 12718080 | tf_op jit(solution)/shard_map/dot_general | solution.py:28
  286.1 7.7 %fusion.24 = f32[16,1024]{1,0:T(8,128)} fusion(f32[16,1024]{1,0:T(8,128)S(1)} %all_gather.29, f32[1024,1024]{0,1:T(8,128)} %get-tuple-element.12, s32[1024,1024]{0,1:T(8,128)} %copy.5), kind=kOutput, calls=%fused_computation.33 | convolution fusion | flops 203423744 | bytes 8519680 | tf_op jit(solution)/shard_map/dot_general | solution.py:37
  293.9 8.0 %fusion.17 = f32[16,1024]{1,0:T(8,128)} fusion(f32[16,1024]{1,0:T(8,128)S(1)} %all_gather.28, f32[1024,1024]{0,1:T(8,128)} %copy-done.3, f32[1024]{0:T(1024)S(1)} %get-tuple-element.4, f32[1024,1024]{0,1:T(8,128)} %get-tuple-element.12, s32[1024,1024]{0,1:T(8,128)} %copy.5), kind=kOutput, calls=%fused_computation.20 | convolution fusion | flops 204488704 | bytes 12718080 | tf_op jit(solution)/shard_map/dot_general | solution.py:33
  302.0 13.7 %reduce-scatter.29.cloned.1.call-done = f32[16,128]{1,0:T(8,128)} async-done(((f32[16,1024]{1,0:T(8,128)}), f32[16,128]{1,0:T(8,128)}) %reduce-scatter.29.cloned.1.call-update) | async-done | bytes 8208 | tf_op jit(solution)/shard_map/reduce_scatter | solution.py:43
  315.7 34.8 %reduce-scatter.27.cloned.1.call-done = f32[16,128]{1,0:T(8,128)} async-done(((f32[16,1024]{1,0:T(8,128)}), f32[16,128]{1,0:T(8,128)}) %reduce-scatter.27.cloned.1.call-update) | async-done | bytes 8208 | tf_op jit(solution)/shard_map/reduce_scatter | solution.py:42
  351.2 9.0 %all_gather.30 = f32[16,1024]{1,0:T(8,128)S(1)} all-gather(f32[16,128]{1,0:T(8,128)S(1)} %add_divide_fusion.1), channel_id=1, replica_groups=mesh['ind'=8,'snp'=4] {'ind'}, dimensions={1}, use_global_device_ids=true | all-gather | bytes 73728 | tf_op jit(solution)/shard_map/all_gather | solution.py:14
  360.2 11.5 %reduce-scatter.25.cloned.1.call-done = f32[16,256]{1,0:T(8,128)} async-done(((f32[16,1024]{1,0:T(8,128)}), f32[16,256]{1,0:T(8,128)}) %reduce-scatter.25.cloned.1.call-update) | async-done | bytes 16400 | tf_op jit(solution)/shard_map/reduce_scatter | solution.py:39
  372.4 13.1 %all_gather.31 = f32[16,1024]{1,0:T(8,128)S(1)} all-gather(f32[16,256]{1,0:T(8,128)S(1)} %multiply_multiply_fusion.1), channel_id=1, replica_groups=mesh['ind'=8,'snp'=4] {'snp'}, dimensions={1}, use_global_device_ids=true | all-gather | bytes 81920 | tf_op jit(solution)/shard_map/all_gather | solution.py:10
  385.5 9.9 %fusion.26 = (f32[1024]{0:T(1024)S(1)}, f32[1024,1024]{0,1:T(8,128)S(1)}, f32[1024,1024]{0,1:T(8,128)}) fusion(s32[1024,1024]{0,1:T(8,128)} %copy.5, f32[16,1024]{1,0:T(8,128)S(1)} %all_gather.31, f32[16,1024]{1,0:T(8,128)S(1)} %all_gather.30), kind=kOutput, calls=%fused_computation.35 | convolution fusion | flops 206568448 | bytes 12718080 | tf_op jit(solution)/shard_map/dot_general | solution.py:28
  401.9 7.7 %fusion.25 = f32[16,1024]{1,0:T(8,128)} fusion(f32[16,1024]{1,0:T(8,128)S(1)} %all_gather.31, f32[1024,1024]{0,1:T(8,128)} %get-tuple-element.13, s32[1024,1024]{0,1:T(8,128)} %copy.5), kind=kOutput, calls=%fused_computation.34 | convolution fusion | flops 203423744 | bytes 8519680 | tf_op jit(solution)/shard_map/dot_general | solution.py:37
  409.7 8.0 %fusion.20 = f32[16,1024]{1,0:T(8,128)} fusion(f32[16,1024]{1,0:T(8,128)S(1)} %all_gather.30, f32[1024,1024]{0,1:T(8,128)} %copy-done, f32[1024]{0:T(1024)S(1)} %get-tuple-element.2, f32[1024,1024]{0,1:T(8,128)} %get-tuple-element.13, s32[1024,1024]{0,1:T(8,128)} %copy.5), kind=kOutput, calls=%fused_computation.21 | convolution fusion | flops 204488704 | bytes 12718080 | tf_op jit(solution)/shard_map/dot_general | solution.py:33
  417.8 13.6 %reduce-scatter.35.cloned.1.call-done = f32[16,128]{1,0:T(8,128)} async-done(((f32[16,1024]{1,0:T(8,128)}), f32[16,128]{1,0:T(8,128)}) %reduce-scatter.35.cloned.1.call-update) | async-done | bytes 8208 | tf_op jit(solution)/shard_map/reduce_scatter | solution.py:43
  431.4 34.4 %reduce-scatter.33.cloned.1.call-done = f32[16,128]{1,0:T(8,128)} async-done(((f32[16,1024]{1,0:T(8,128)}), f32[16,128]{1,0:T(8,128)}) %reduce-scatter.33.cloned.1.call-update) | async-done | bytes 8208 | tf_op jit(solution)/shard_map/reduce_scatter | solution.py:42
  467.2 19.9 %reduce-scatter.31.cloned.1.call-done = f32[16,256]{1,0:T(8,128)} async-done(((f32[16,1024]{1,0:T(8,128)}), f32[16,256]{1,0:T(8,128)}) %reduce-scatter.31.cloned.1.call-update) | async-done | bytes 16400 | tf_op jit(solution)/shard_map/reduce_scatter | solution.py:39
  (49 shorter events, 38.9 us)
Async XLA Ops:
  7.2 77.5 %reduce-scatter.17.cloned.1.call-start = ((), (), s32[]{:S(2)}) async-start(), calls=%async_computation.14 | async-start | bytes 73728 | tf_op jit(solution)/shard_map/reduce_scatter | solution.py:43
  46.8 2.0 copy-start.1
  53.0 66.4 %reduce-scatter.15.cloned.1.call-start = ((), (), s32[]{:S(2)}) async-start(), calls=%async_computation.13 | async-start | bytes 73728 | tf_op jit(solution)/shard_map/reduce_scatter | solution.py:42
  61.3 79.4 %reduce-scatter.13.cloned.1.call-start = ((), (), s32[]{:S(2)}) async-start(), calls=%async_computation.12 | async-start | bytes 81920 | tf_op jit(solution)/shard_map/reduce_scatter | solution.py:39
  61.8 57.6 %copy-start.5 = (f32[16,128]{1,0:T(8,128)S(1)}, f32[16,128]{1,0:T(8,128)}, u32[]{:S(2)}) copy-start(f32[16,128]{1,0:T(8,128)} %param.5) | copy-start | bytes 24580
  61.8 78.9 %copy-start.4 = (f32[16,256]{1,0:T(8,128)S(1)}, f32[16,256]{1,0:T(8,128)}, u32[]{:S(2)}) copy-start(f32[16,256]{1,0:T(8,128)} %param.4) | copy-start | bytes 49156
  70.1 130.4 %reduce-scatter.23.cloned.1.call-start = ((), (), s32[]{:S(2)}) async-start(), calls=%async_computation.17 | async-start | bytes 73728 | tf_op jit(solution)/shard_map/reduce_scatter | solution.py:43
  164.4 2.0 copy-start.2
  170.6 64.1 %reduce-scatter.21.cloned.1.call-start = ((), (), s32[]{:S(2)}) async-start(), calls=%async_computation.16 | async-start | bytes 73728 | tf_op jit(solution)/shard_map/reduce_scatter | solution.py:42
  178.6 77.3 %reduce-scatter.19.cloned.1.call-start = ((), (), s32[]{:S(2)}) async-start(), calls=%async_computation.15 | async-start | bytes 81920 | tf_op jit(solution)/shard_map/reduce_scatter | solution.py:39
  186.7 129.0 %reduce-scatter.29.cloned.1.call-start = ((), (), s32[]{:S(2)}) async-start(), calls=%async_computation.20 | async-start | bytes 73728 | tf_op jit(solution)/shard_map/reduce_scatter | solution.py:43
  279.6 2.0 copy-start.3
  285.8 64.6 %reduce-scatter.27.cloned.1.call-start = ((), (), s32[]{:S(2)}) async-start(), calls=%async_computation.19 | async-start | bytes 73728 | tf_op jit(solution)/shard_map/reduce_scatter | solution.py:42
  293.8 77.9 %reduce-scatter.25.cloned.1.call-start = ((), (), s32[]{:S(2)}) async-start(), calls=%async_computation.18 | async-start | bytes 81920 | tf_op jit(solution)/shard_map/reduce_scatter | solution.py:39
  301.9 129.5 %reduce-scatter.35.cloned.1.call-start = ((), (), s32[]{:S(2)}) async-start(), calls=%async_computation.23 | async-start | bytes 73728 | tf_op jit(solution)/shard_map/reduce_scatter | solution.py:43
  395.4 2.0 copy-start
  401.6 64.2 %reduce-scatter.33.cloned.1.call-start = ((), (), s32[]{:S(2)}) async-start(), calls=%async_computation.22 | async-start | bytes 73728 | tf_op jit(solution)/shard_map/reduce_scatter | solution.py:42
  409.7 77.4 %reduce-scatter.31.cloned.1.call-start = ((), (), s32[]{:S(2)}) async-start(), calls=%async_computation.21 | async-start | bytes 81920 | tf_op jit(solution)/shard_map/reduce_scatter | solution.py:39
Sparse Core Ops, SparseCore 0:
  53.1 31.4 reduce-scatter.16
  87.9 31.4 reduce-scatter.14
  121.6 19.0 reduce-scatter.12
  170.7 29.6 reduce-scatter.22
  203.3 31.3 reduce-scatter.20
  236.9 18.9 reduce-scatter.18
  285.9 29.7 reduce-scatter.28
  319.0 31.4 reduce-scatter.26
  352.7 18.9 reduce-scatter.24
  401.8 29.6 reduce-scatter.34
  434.4 31.3 reduce-scatter.32
  468.0 18.9 reduce-scatter.30
where the time goes:
time: 504 us; the launch traced here: 496 us
  waiting for transfers between devices  248 us (49%)
  matrix products  120 us (24%)
  blocking collectives  90.7 us (18%)
  between operations  14.7 us (3%)
  local copies, waits for them, and re-layouts  13.3 us (3%)
  other arithmetic  6.98 us (1%)
    reduce_scatter x4, waiting for transfers between devices, body(): lax.psum_scatter(p_one, 'ind', scatter_dimension=1, tiled=True)  138 us
    reduce_scatter x4, waiting for transfers between devices, body(): lax.psum_scatter(p_two, 'ind', scatter_dimension=1, tiled=True)  55.6 us
    all_gather x4, blocking collectives, fetch_ancestry(): return lax.all_gather(shard, 'snp', axis=1, tiled=True)  54.5 us
    reduce_scatter x4, waiting for transfers between devices, body(): q_part = lax.psum_scatter(q_sum, 'snp', scatter_dimension=1, tiled=True)  54.4 us
    dot_general x4, matrix products, body(): lax.dot_general(q_full, p_full, (((0,), (0,)), ((), ())), precision=lax.P...  39.6 us
    all_gather x4, blocking collectives, fetch_freqs(): return lax.all_gather(shard, 'ind', axis=1, tiled=True)  36.3 us
    dot_general x4, matrix products, body(): lax.dot_general(p_full, ratio_one - ratio_two, (((1,), (1,)), ((), ())),...  32.3 us
    dot_general x4, matrix products, body(): p_one = jnp.dot(q_full, ratio_one, precision=lax.Precision.HIGHEST)  31.3 us
  transfers between devices with their start and end apart: 12, of which 12 were waited for; matrix products, arithmetic and copies ran while one was open for 14% of the time, Pallas kernels for 0%

commit v1 on v0

v1 whole, which is shorter than its diff:
```python
import functools

import jax
import jax.numpy as jnp
from jax import lax
from jax.experimental import pallas as pl
from jax.experimental.pallas import tpu as pltpu
from jax.sharding import PartitionSpec as P

ITERS = 4
AXES = ("ind", "snp")


def split3(x):
    one = x.astype(jnp.bfloat16)
    rest = x - one.astype(jnp.float32)
    two = rest.astype(jnp.bfloat16)
    three = (rest - two.astype(jnp.float32)).astype(jnp.bfloat16)
    return one, two, three


def fold3(x):
    k = x.shape[0] // 3
    return x[:k] + x[k : 2 * k] + x[2 * k :]


def em_kernel(first, rows, snps_all, core_ref, g_ref, q_ref, keep_ref, got_ref, mine_ref, send_ref, q_out, p_out, qs_ref, ql_ref, ps_ref, pr_ref, acc_ref):
    core = core_ref[0]
    keep, got = keep_ref[...], got_ref[...]
    p = jnp.where(core == 0, keep, got)
    a_sum = jnp.where(core == 0, got, keep)
    if first:
        q = a_sum
    else:
        q_old = q_ref[...]
        rest = 2.0 * snps_all - jnp.sum(q_old * a_sum, axis=0, keepdims=True)
        q = q_old * (a_sum + rest) * (1.0 / (2.0 * snps_all))
    q_out[...] = q
    p_out[...] = p
    k = q.shape[0]
    q1, q2, q3 = split3(q)
    p1, p2, p3 = split3(p)
    qs_ref[...] = jnp.concatenate([q1, q2, q3], axis=0)
    ps_ref[...] = jnp.concatenate([p1, p2, p3], axis=0)
    ql_ref[...] = jnp.concatenate([q1, q2, q1, q2, q3, q1], axis=0).T
    pr_ref[...] = jnp.concatenate([p1, p1, p2, p2, p1, p3], axis=0)
    acc_ref[...] = jnp.zeros_like(acc_ref)
    qsum_ref, other_ref = (send_ref, mine_ref)

    def block(b, _):
        at = pl.ds(pl.multiple_of(b * rows, rows), rows)
        e = jnp.dot(ql_ref[at, :], pr_ref[...], preferred_element_type=jnp.float32)
        g = g_ref[at, :].astype(jnp.float32)
        d = e * (1.0 - e)
        inv = pl.reciprocal(d, approx=True)
        inv = inv * (2.0 - d * inv)
        diff = (g - 2.0 * e) * inv
        two = ((2.0 - g) * e) * inv
        dh = diff.astype(jnp.bfloat16)
        dl = (diff - dh.astype(jnp.float32)).astype(jnp.bfloat16)
        th = two.astype(jnp.bfloat16)
        tl = (two - th.astype(jnp.float32)).astype(jnp.bfloat16)
        nt = (((1,), (1,)), ((), ()))
        a = lax.dot_general(ps_ref[...], dh, nt, preferred_element_type=jnp.float32)
        a = a + lax.dot_general(ps_ref[...], dl, nt, preferred_element_type=jnp.float32)
        a = fold3(a)
        mine_ref[k:, at] = a
        qb = qs_ref[:, at]
        pd = jnp.dot(qb, dh, preferred_element_type=jnp.float32) + jnp.dot(qb, dl, preferred_element_type=jnp.float32)
        pt = jnp.dot(qb, th, preferred_element_type=jnp.float32) + jnp.dot(qb, tl, preferred_element_type=jnp.float32)
        pt = fold3(pt)
        acc_ref[:k] += fold3(pd) + pt
        acc_ref[k:] += pt
        return 0

    lax.fori_loop(0, g_ref.shape[0] // rows, block, 0)
    a = mine_ref[k:, :]
    acc = acc_ref[...]

    @pl.when(core == 0)
    def _():
        send_ref[:k] = a
        send_ref[k:] = jnp.zeros_like(a)
        mine_ref[...] = acc

    @pl.when(core == 1)
    def _():
        send_ref[...] = acc
        mine_ref[:k] = jnp.zeros_like(a)


def em_step(first, snps_all, core, g, q, keep, got):
    individuals, snps = g.shape
    k = q.shape[0]
    f32, bf16 = jnp.float32, jnp.bfloat16
    vmem = pl.BlockSpec(memory_space=pltpu.VMEM)
    return pl.pallas_call(
        functools.partial(em_kernel, first, 256, snps_all),
        out_shape=(
            jax.ShapeDtypeStruct((2 * k, snps), f32),
            jax.ShapeDtypeStruct((2 * k, snps), f32),
            jax.ShapeDtypeStruct((k, individuals), f32),
            jax.ShapeDtypeStruct((k, snps), f32),
        ),
        in_specs=[pl.BlockSpec(memory_space=pltpu.SMEM)] + [vmem] * 4,
        out_specs=(vmem,) * 4,
        scratch_shapes=[
            pltpu.VMEM((3 * k, individuals), bf16),
            pltpu.VMEM((individuals, 6 * k), bf16),
            pltpu.VMEM((3 * k, snps), bf16),
            pltpu.VMEM((6 * k, snps), bf16),
            pltpu.VMEM((2 * k, snps), f32),
        ],
        compiler_params=pltpu.CompilerParams(vmem_limit_bytes=32 * 1024 * 1024),
        cost_estimate=pl.CostEstimate(flops=2 * 20 * k * individuals * snps, bytes_accessed=4 * individuals * snps, transcendentals=individuals * snps),
    )(core, g, q, keep, got)


def swap_cores(x, n_ind):
    return lax.ppermute(x, "ind", [(i, i ^ 1) for i in range(n_ind)])


def sum_groups(buf, n_ind, n_snp):
    n_chip = n_ind // 2
    base = 1
    while base < max(n_chip, n_snp):
        parts = []
        for m in (3, 2, 1):
            mask = m * base
            pairs = []
            for i in range(n_ind):
                for s in range(n_snp):
                    if i % 2 == 0 and mask < n_chip:
                        pairs.append((i * n_snp + s, (i ^ (2 * mask)) * n_snp + s))
                    if i % 2 == 1 and mask < n_snp:
                        pairs.append((i * n_snp + s, i * n_snp + (s ^ mask)))
            if pairs:
                parts.append(lax.ppermute(buf, AXES, pairs))
        for part in parts:
            buf = buf + part
        base *= 4
    return buf


def place(shard, index, count):
    width = shard.shape[1]
    full = jnp.zeros((shard.shape[0], width * count), shard.dtype)
    return lax.dynamic_update_slice_in_dim(full, shard, index * width, axis=1)


def body(genotypes, ancestry, freqs):
    n_ind, n_snp = lax.axis_size("ind"), lax.axis_size("snp")
    ind, snp = lax.axis_index("ind"), lax.axis_index("snp")
    core = ind % 2
    first_core = core == 0
    k = ancestry.shape[0]
    snps_all = genotypes.shape[1] * n_snp
    core_id = core.reshape(1).astype(jnp.int32)

    q_at = place(ancestry, snp, n_snp)
    p_at = place(freqs, ind, n_ind)
    none = jnp.zeros_like(q_at)
    mine = jnp.concatenate([jnp.where(first_core, p_at, none), jnp.where(first_core, none, q_at)])
    send = jnp.concatenate([jnp.where(first_core, q_at, p_at), none])
    q = none
    for step in range(ITERS + 1):
        buf = mine + swap_cores(send, n_ind)
        buf = sum_groups(buf, n_ind, n_snp)
        if step == 0:
            p_new = buf[:k]
        else:
            up = p * buf[:k]
            p_new = up / (up + (1.0 - p) * buf[k:])
        keep = jnp.where(first_core, p_new, buf[k:])
        got = swap_cores(jnp.where(first_core, p_new, buf[:k]), n_ind)
        if step < ITERS:
            mine, send, q, p = em_step(step == 0, snps_all, core_id, genotypes, q, keep, got)
    p = jnp.where(first_core, keep, got)
    a_sum = jnp.where(first_core, got, keep)
    rest = 2.0 * snps_all - jnp.sum(q * a_sum, axis=0, keepdims=True)
    q = q * (a_sum + rest) * (1.0 / (2.0 * snps_all))
    q_own = lax.dynamic_slice_in_dim(q, snp * ancestry.shape[1], ancestry.shape[1], axis=1)
    p_own = lax.dynamic_slice_in_dim(p, ind * freqs.shape[1], freqs.shape[1], axis=1)
    return (q_own, p_own)


def solution(mesh):
    in_specs = (P("ind", "snp"), P(None, ("ind", "snp")), P(None, ("snp", "ind")))
    out_specs = (P(None, ("ind", "snp")), P(None, ("snp", "ind")))
    return jax.shard_map(body, mesh=mesh, in_specs=in_specs, out_specs=out_specs, check_vma=False)
```

time: 504 us -> 88.9 us (0.18); the launches traced: 496 us -> 88.6 us
  waiting for transfers between devices: 248 us -> 36.8 us
  matrix products: 120 us -> 0 us
  blocking collectives: 90.7 us -> 0 us
  starting transfers between devices: 1.6 us -> 24.1 us
  Pallas kernels: 0 us -> 21.5 us
  between operations: 14.7 us -> 0.8 us
  local copies, waits for them, and re-layouts: 13.3 us -> 3.72 us
  other arithmetic: 6.98 us -> 1.62 us
    reduce_scatter x12 -> x0, waiting for transfers between devices: 248 us -> none  [the longest x4 138 us: body(): lax.psum_scatter(p_one, 'ind', scatter_dimension=1, tiled=True)]
    dot_general x16 -> x0, matrix products: 120 us -> none  [the longest x4 39.6 us: body(): lax.dot_general(q_full, p_full, (((0,), (0,)), ((), ())), precision=lax.P...]
    all_gather x8 -> x0, blocking collectives: 90.7 us -> none  [the longest x4 54.5 us: fetch_ancestry(): return lax.all_gather(shard, 'snp', axis=1, tiled=True)]
    ppermute x0 -> x25, waiting for transfers between devices: none -> 36.8 us  [the longest x15 27.2 us: sum_groups(): parts.append(lax.ppermute(buf, AXES, pairs))]
    ppermute x0 -> x25, starting transfers between devices: none -> 24.1 us  [the longest x15 18.7 us: sum_groups(): parts.append(lax.ppermute(buf, AXES, pairs))]
    pallas_call x0 -> x4, Pallas kernels: none -> 21.5 us  [em_step(): pl.pallas_call(functools.partial(em_kernel, first, 256, snps_all), out_sh...]
    unnamed x13 -> x2, local copies, waits for them, and re-layouts: 13.3 us -> 2.19 us
    div x8 -> x0, other arithmetic: 6.98 us -> none  [the longest x4 3.49 us: body(): q_own = q_own * q_part / (2.0 * snp_count)]
  transfers between devices with their start and end apart: 12 -> 25, of which waited for: 12 -> 25; matrix products, arithmetic and copies ran while one was open for 14% -> 0% of each run, Pallas kernels for 0% -> 0%
where the time goes in v1:
time: 88.9 us; the launch traced here: 88.6 us
  waiting for transfers between devices  36.8 us (41%)
  starting transfers between devices  24.1 us (27%)
  Pallas kernels  21.5 us (24%)
  local copies, waits for them, and re-layouts  3.72 us (4%)
  other arithmetic  1.62 us (2%)
    ppermute x15, waiting for transfers between devices, sum_groups(): parts.append(lax.ppermute(buf, AXES, pairs))  27.2 us
    pallas_call x4, Pallas kernels, em_step(): pl.pallas_call(functools.partial(em_kernel, first, 256, snps_all), out_sh...  21.5 us
    ppermute x15, starting transfers between devices, sum_groups(): parts.append(lax.ppermute(buf, AXES, pairs))  18.7 us
    ppermute x10, waiting for transfers between devices, swap_cores(): return lax.ppermute(x, 'ind', [(i, i ^ 1) for i in range(n_ind)])  9.6 us
    ppermute x10, starting transfers between devices, swap_cores(): return lax.ppermute(x, 'ind', [(i, i ^ 1) for i in range(n_ind)])  5.43 us
    unnamed x2, local copies, waits for them, and re-layouts  2.19 us
  transfers between devices with their start and end apart: 25, of which 25 were waited for; matrix products, arithmetic and copies ran while one was open for 0% of the time, Pallas kernels for 0%

profile of v1, /device:TPU:0, one launch (start us, length us, event | category | flops | bytes accessed | tf_op | source)
XLA Modules:
  0.0 88.6 jit_solution(1034042271799248567)
XLA Ops:
  3.7 2.9 %collective-permute-start.3 = (f32[32,1024]{1,0:T(8,128)S(1)}, f32[32,1024]{1,0:T(8,128)S(1)}, u32[]{:S(2)}, u32[]{:S(2)}) collective-permute-start(f32[32,1024]{1,0:T(8,128)S(1)} %maximum_add_fusion), channel_id=1, source_target_pairs={{0,8},{1,9},{2,10},{3,11},{4,5},{5,4},{6,7},{7,6},{8,0},{9,1},{10,... | collective-permute-start | bytes 393224 | tf_op jit(solution)/shard_map/ppermute | solution.py:138
  6.6 1.5 %collective-permute-start.2 = (f32[32,1024]{1,0:T(8,128)S(1)}, f32[32,1024]{1,0:T(8,128)S(1)}, u32[]{:S(2)}, u32[]{:S(2)}) collective-permute-start(f32[32,1024]{1,0:T(8,128)S(1)} %maximum_add_fusion), channel_id=1, source_target_pairs={{0,16},{1,17},{2,18},{3,19},{4,6},{5,7},{6,4},{7,5},{8,24},{9,25},... | collective-permute-start | bytes 393224 | tf_op jit(solution)/shard_map/ppermute | solution.py:138
  8.1 1.4 %collective-permute-done.3 = f32[32,1024]{1,0:T(8,128)S(1)} collective-permute-done((f32[32,1024]{1,0:T(8,128)S(1)}, f32[32,1024]{1,0:T(8,128)S(1)}, u32[]{:S(2)}, u32[]{:S(2)}) %collective-permute-start.3) | collective-permute-done | bytes 131104 | tf_op jit(solution)/shard_map/ppermute | solution.py:138
  9.5 2.0 %collective-permute-done.2 = f32[32,1024]{1,0:T(8,128)S(1)} collective-permute-done((f32[32,1024]{1,0:T(8,128)S(1)}, f32[32,1024]{1,0:T(8,128)S(1)}, u32[]{:S(2)}, u32[]{:S(2)}) %collective-permute-start.2) | collective-permute-done | bytes 131104 | tf_op jit(solution)/shard_map/ppermute | solution.py:138
  11.5 2.4 %collective-permute-done.1 = f32[32,1024]{1,0:T(8,128)S(1)} collective-permute-done((f32[32,1024]{1,0:T(8,128)S(1)}, f32[32,1024]{1,0:T(8,128)S(1)}, u32[]{:S(2)}, u32[]{:S(2)}) %collective-permute-start.1) | collective-permute-done | bytes 131104 | tf_op jit(solution)/shard_map/ppermute | solution.py:138
  15.6 2.2 %copy-done = s32[1024,1024]{1,0:T(8,128)S(1)} copy-done((s32[1024,1024]{1,0:T(8,128)S(1)}, s32[1024,1024]{1,0:T(8,128)}, u32[]{:S(2)}) %copy-start) | copy-done | bytes 4194328
  17.8 5.4 %shard_map.50 = (f32[32,1024]{1,0:T(8,128)S(1)}, f32[32,1024]{1,0:T(8,128)S(1)}, f32[16,1024]{1,0:T(8,128)S(1)}, f32[16,1024]{1,0:T(8,128)S(1)}) custom-call(s32[1]{0:T(128)} %bitcast.core_ref, s32[1024,1024]{1,0:T(8,128)S(1)} %copy-done, f32[16,1024]{1,0:T(8,128)S(1)} %broadcast_3_q_ref.2.q_ref, f32[16,1024]{1,0:T(8,128)S(1)} %get-tuple-element.44.keep_ref, ...), custom_call_target="tpu_custom_call" | custom-call | flops 671088640 | bytes 4194304 | tf_op jit(solution)/shard_map/pallas_call | solution.py:97
  23.6 1.0 %collective-permute-done.5 = f32[32,1024]{1,0:T(8,128)S(1)} collective-permute-done((f32[32,1024]{1,0:T(8,128)S(1)}, f32[32,1024]{1,0:T(8,128)S(1)}, u32[]{:S(2)}, u32[]{:S(2)}) %collective-permute-start.5) | collective-permute-done | bytes 131104 | tf_op jit(solution)/shard_map/ppermute | solution.py:120
  24.6 1.6 %collective-permute-start.8 = (f32[32,1024]{1,0:T(8,128)S(1)}, f32[32,1024]{1,0:T(8,128)S(1)}, u32[]{:S(2)}, u32[]{:S(2)}) collective-permute-start(f32[32,1024]{1,0:T(8,128)S(1)} %add.101), channel_id=1, source_target_pairs={{0,8},{1,9},{2,10},{3,11},{4,5},{5,4},{6,7},{7,6},{8,0},{9,1},{10,... | collective-permute-start | bytes 393224 | tf_op jit(solution)/shard_map/ppermute | solution.py:138
  26.1 1.5 %collective-permute-start.7 = (f32[32,1024]{1,0:T(8,128)S(1)}, f32[32,1024]{1,0:T(8,128)S(1)}, u32[]{:S(2)}, u32[]{:S(2)}) collective-permute-start(f32[32,1024]{1,0:T(8,128)S(1)} %add.101), channel_id=1, source_target_pairs={{0,16},{1,17},{2,18},{3,19},{4,6},{5,7},{6,4},{7,5},{8,24},{9,25},... | collective-permute-start | bytes 393224 | tf_op jit(solution)/shard_map/ppermute | solution.py:138
  28.1 1.5 %collective-permute-done.8 = f32[32,1024]{1,0:T(8,128)S(1)} collective-permute-done((f32[32,1024]{1,0:T(8,128)S(1)}, f32[32,1024]{1,0:T(8,128)S(1)}, u32[]{:S(2)}, u32[]{:S(2)}) %collective-permute-start.8) | collective-permute-done | bytes 131104 | tf_op jit(solution)/shard_map/ppermute | solution.py:138
  29.6 1.5 %collective-permute-done.7 = f32[32,1024]{1,0:T(8,128)S(1)} collective-permute-done((f32[32,1024]{1,0:T(8,128)S(1)}, f32[32,1024]{1,0:T(8,128)S(1)}, u32[]{:S(2)}, u32[]{:S(2)}) %collective-permute-start.7) | collective-permute-done | bytes 131104 | tf_op jit(solution)/shard_map/ppermute | solution.py:138
  31.1 2.4 %collective-permute-done.6 = f32[32,1024]{1,0:T(8,128)S(1)} collective-permute-done((f32[32,1024]{1,0:T(8,128)S(1)}, f32[32,1024]{1,0:T(8,128)S(1)}, u32[]{:S(2)}, u32[]{:S(2)}) %collective-permute-start.6) | collective-permute-done | bytes 131104 | tf_op jit(solution)/shard_map/ppermute | solution.py:138
  34.9 5.4 %shard_map.51 = (f32[32,1024]{1,0:T(8,128)S(1)}, f32[32,1024]{1,0:T(8,128)S(1)}, f32[16,1024]{1,0:T(8,128)S(1)}, f32[16,1024]{1,0:T(8,128)S(1)}) custom-call(s32[1]{0:T(128)} %bitcast.core_ref, s32[1024,1024]{1,0:T(8,128)S(1)} %copy-done, f32[16,1024]{1,0:T(8,128)S(1)} %get-tuple-element.18.q_ref, f32[16,1024]{1,0:T(8,128)S(1)} %get-tuple-element.42.keep_ref, ...), custom_call_target="tpu_custom_call" | custom-call | flops 671088640 | bytes 4194304 | tf_op jit(solution)/shard_map/pallas_call | solution.py:97
  40.7 1.0 %collective-permute-done.10 = f32[32,1024]{1,0:T(8,128)S(1)} collective-permute-done((f32[32,1024]{1,0:T(8,128)S(1)}, f32[32,1024]{1,0:T(8,128)S(1)}, u32[]{:S(2)}, u32[]{:S(2)}) %collective-permute-start.10) | collective-permute-done | bytes 131104 | tf_op jit(solution)/shard_map/ppermute | solution.py:120
  41.7 1.4 %collective-permute-start.13 = (f32[32,1024]{1,0:T(8,128)S(1)}, f32[32,1024]{1,0:T(8,128)S(1)}, u32[]{:S(2)}, u32[]{:S(2)}) collective-permute-start(f32[32,1024]{1,0:T(8,128)S(1)} %add.106), channel_id=1, source_target_pairs={{0,8},{1,9},{2,10},{3,11},{4,5},{5,4},{6,7},{7,6},{8,0},{9,1},{10,... | collective-permute-start | bytes 393224 | tf_op jit(solution)/shard_map/ppermute | solution.py:138
  43.1 1.5 %collective-permute-start.12 = (f32[32,1024]{1,0:T(8,128)S(1)}, f32[32,1024]{1,0:T(8,128)S(1)}, u32[]{:S(2)}, u32[]{:S(2)}) collective-permute-start(f32[32,1024]{1,0:T(8,128)S(1)} %add.106), channel_id=1, source_target_pairs={{0,16},{1,17},{2,18},{3,19},{4,6},{5,7},{6,4},{7,5},{8,24},{9,25},... | collective-permute-start | bytes 393224 | tf_op jit(solution)/shard_map/ppermute | solution.py:138
  45.3 1.5 %collective-permute-done.13 = f32[32,1024]{1,0:T(8,128)S(1)} collective-permute-done((f32[32,1024]{1,0:T(8,128)S(1)}, f32[32,1024]{1,0:T(8,128)S(1)}, u32[]{:S(2)}, u32[]{:S(2)}) %collective-permute-start.13) | collective-permute-done | bytes 131104 | tf_op jit(solution)/shard_map/ppermute | solution.py:138
  46.8 1.3 %collective-permute-done.12 = f32[32,1024]{1,0:T(8,128)S(1)} collective-permute-done((f32[32,1024]{1,0:T(8,128)S(1)}, f32[32,1024]{1,0:T(8,128)S(1)}, u32[]{:S(2)}, u32[]{:S(2)}) %collective-permute-start.12) | collective-permute-done | bytes 131104 | tf_op jit(solution)/shard_map/ppermute | solution.py:138
  48.1 2.4 %collective-permute-done.11 = f32[32,1024]{1,0:T(8,128)S(1)} collective-permute-done((f32[32,1024]{1,0:T(8,128)S(1)}, f32[32,1024]{1,0:T(8,128)S(1)}, u32[]{:S(2)}, u32[]{:S(2)}) %collective-permute-start.11) | collective-permute-done | bytes 131104 | tf_op jit(solution)/shard_map/ppermute | solution.py:138
  52.2 5.4 %shard_map.52 = (f32[32,1024]{1,0:T(8,128)S(1)}, f32[32,1024]{1,0:T(8,128)S(1)}, f32[16,1024]{1,0:T(8,128)S(1)}, f32[16,1024]{1,0:T(8,128)S(1)}) custom-call(s32[1]{0:T(128)} %bitcast.core_ref, s32[1024,1024]{1,0:T(8,128)S(1)} %copy-done, f32[16,1024]{1,0:T(8,128)S(1)} %get-tuple-element.22.q_ref, f32[16,1024]{1,0:T(8,128)S(1)} %get-tuple-element.40.keep_ref, ...), custom_call_target="tpu_custom_call" | custom-call | flops 671088640 | bytes 4194304 | tf_op jit(solution)/shard_map/pallas_call | solution.py:97
  59.1 1.5 %collective-permute-start.18 = (f32[32,1024]{1,0:T(8,128)S(1)}, f32[32,1024]{1,0:T(8,128)S(1)}, u32[]{:S(2)}, u32[]{:S(2)}) collective-permute-start(f32[32,1024]{1,0:T(8,128)S(1)} %add.111), channel_id=1, source_target_pairs={{0,8},{1,9},{2,10},{3,11},{4,5},{5,4},{6,7},{7,6},{8,0},{9,1},{10,... | collective-permute-start | bytes 393224 | tf_op jit(solution)/shard_map/ppermute | solution.py:138
  60.6 1.5 %collective-permute-start.17 = (f32[32,1024]{1,0:T(8,128)S(1)}, f32[32,1024]{1,0:T(8,128)S(1)}, u32[]{:S(2)}, u32[]{:S(2)}) collective-permute-start(f32[32,1024]{1,0:T(8,128)S(1)} %add.111), channel_id=1, source_target_pairs={{0,16},{1,17},{2,18},{3,19},{4,6},{5,7},{6,4},{7,5},{8,24},{9,25},... | collective-permute-start | bytes 393224 | tf_op jit(solution)/shard_map/ppermute | solution.py:138
  62.6 1.5 %collective-permute-done.18 = f32[32,1024]{1,0:T(8,128)S(1)} collective-permute-done((f32[32,1024]{1,0:T(8,128)S(1)}, f32[32,1024]{1,0:T(8,128)S(1)}, u32[]{:S(2)}, u32[]{:S(2)}) %collective-permute-start.18) | collective-permute-done | bytes 131104 | tf_op jit(solution)/shard_map/ppermute | solution.py:138
  64.1 1.5 %collective-permute-done.17 = f32[32,1024]{1,0:T(8,128)S(1)} collective-permute-done((f32[32,1024]{1,0:T(8,128)S(1)}, f32[32,1024]{1,0:T(8,128)S(1)}, u32[]{:S(2)}, u32[]{:S(2)}) %collective-permute-start.17) | collective-permute-done | bytes 131104 | tf_op jit(solution)/shard_map/ppermute | solution.py:138
  65.6 2.4 %collective-permute-done.16 = f32[32,1024]{1,0:T(8,128)S(1)} collective-permute-done((f32[32,1024]{1,0:T(8,128)S(1)}, f32[32,1024]{1,0:T(8,128)S(1)}, u32[]{:S(2)}, u32[]{:S(2)}) %collective-permute-start.16) | collective-permute-done | bytes 131104 | tf_op jit(solution)/shard_map/ppermute | solution.py:138
  69.7 5.4 %shard_map.53 = (f32[32,1024]{1,0:T(8,128)S(1)}, f32[32,1024]{1,0:T(8,128)S(1)}, f32[16,1024]{1,0:T(8,128)S(1)}, f32[16,1024]{1,0:T(8,128)S(1)}) custom-call(s32[1]{0:T(128)} %bitcast.core_ref, s32[1024,1024]{1,0:T(8,128)S(1)} %copy-done, f32[16,1024]{1,0:T(8,128)S(1)} %get-tuple-element.26.q_ref, f32[16,1024]{1,0:T(8,128)S(1)} %get-tuple-element.38.keep_ref, ...), custom_call_target="tpu_custom_call" | custom-call | flops 671088640 | bytes 4194304 | tf_op jit(solution)/shard_map/pallas_call | solution.py:97
  76.6 1.5 %collective-permute-start.23 = (f32[32,1024]{1,0:T(8,128)S(1)}, f32[32,1024]{1,0:T(8,128)S(1)}, u32[]{:S(2)}, u32[]{:S(2)}) collective-permute-start(f32[32,1024]{1,0:T(8,128)S(1)} %add.116), channel_id=1, source_target_pairs={{0,8},{1,9},{2,10},{3,11},{4,5},{5,4},{6,7},{7,6},{8,0},{9,1},{10,... | collective-permute-start | bytes 393224 | tf_op jit(solution)/shard_map/ppermute | solution.py:138
  78.1 1.5 %collective-permute-start.22 = (f32[32,1024]{1,0:T(8,128)S(1)}, f32[32,1024]{1,0:T(8,128)S(1)}, u32[]{:S(2)}, u32[]{:S(2)}) collective-permute-start(f32[32,1024]{1,0:T(8,128)S(1)} %add.116), channel_id=1, source_target_pairs={{0,16},{1,17},{2,18},{3,19},{4,6},{5,7},{6,4},{7,5},{8,24},{9,25},... | collective-permute-start | bytes 393224 | tf_op jit(solution)/shard_map/ppermute | solution.py:138
  80.1 1.5 %collective-permute-done.23 = f32[32,1024]{1,0:T(8,128)S(1)} collective-permute-done((f32[32,1024]{1,0:T(8,128)S(1)}, f32[32,1024]{1,0:T(8,128)S(1)}, u32[]{:S(2)}, u32[]{:S(2)}) %collective-permute-start.23) | collective-permute-done | bytes 131104 | tf_op jit(solution)/shard_map/ppermute | solution.py:138
  81.6 1.5 %collective-permute-done.22 = f32[32,1024]{1,0:T(8,128)S(1)} collective-permute-done((f32[32,1024]{1,0:T(8,128)S(1)}, f32[32,1024]{1,0:T(8,128)S(1)}, u32[]{:S(2)}, u32[]{:S(2)}) %collective-permute-start.22) | collective-permute-done | bytes 131104 | tf_op jit(solution)/shard_map/ppermute | solution.py:138
  83.1 2.4 %collective-permute-done.21 = f32[32,1024]{1,0:T(8,128)S(1)} collective-permute-done((f32[32,1024]{1,0:T(8,128)S(1)}, f32[32,1024]{1,0:T(8,128)S(1)}, u32[]{:S(2)}, u32[]{:S(2)}) %collective-permute-start.21) | collective-permute-done | bytes 131104 | tf_op jit(solution)/shard_map/ppermute | solution.py:138
  (51 shorter events, 18.2 us)
Async XLA Ops:
  2.1 1.5 %collective-permute-start = (f32[32,1024]{1,0:T(8,128)S(1)}, f32[32,1024]{1,0:T(8,128)S(1)}, u32[]{:S(2)}, u32[]{:S(2)}) collective-permute-start(f32[32,1024]{1,0:T(8,128)S(1)} %concatenate.7), channel_id=1, source_target_pairs={{0,4},{4,0},{8,12},{12,8},{16,20},{20,16},{24,28},{28,24},{1,5},{5... | collective-permute-start | bytes 393224 | tf_op jit(solution)/shard_map/ppermute | solution.py:120
  3.7 5.9 %collective-permute-start.3 = (f32[32,1024]{1,0:T(8,128)S(1)}, f32[32,1024]{1,0:T(8,128)S(1)}, u32[]{:S(2)}, u32[]{:S(2)}) collective-permute-start(f32[32,1024]{1,0:T(8,128)S(1)} %maximum_add_fusion), channel_id=1, source_target_pairs={{0,8},{1,9},{2,10},{3,11},{4,5},{5,4},{6,7},{7,6},{8,0},{9,1},{10,... | collective-permute-start | bytes 393224 | tf_op jit(solution)/shard_map/ppermute | solution.py:138
  6.6 5.0 %collective-permute-start.2 = (f32[32,1024]{1,0:T(8,128)S(1)}, f32[32,1024]{1,0:T(8,128)S(1)}, u32[]{:S(2)}, u32[]{:S(2)}) collective-permute-start(f32[32,1024]{1,0:T(8,128)S(1)} %maximum_add_fusion), channel_id=1, source_target_pairs={{0,16},{1,17},{2,18},{3,19},{4,6},{5,7},{6,4},{7,5},{8,24},{9,25},... | collective-permute-start | bytes 393224 | tf_op jit(solution)/shard_map/ppermute | solution.py:138
  8.1 5.9 %collective-permute-start.1 = (f32[32,1024]{1,0:T(8,128)S(1)}, f32[32,1024]{1,0:T(8,128)S(1)}, u32[]{:S(2)}, u32[]{:S(2)}) collective-permute-start(f32[32,1024]{1,0:T(8,128)S(1)} %maximum_add_fusion), channel_id=1, source_target_pairs={{0,24},{1,25},{2,26},{3,27},{4,7},{5,6},{6,5},{7,4},{8,16},{9,17},... | collective-permute-start | bytes 393224 | tf_op jit(solution)/shard_map/ppermute | solution.py:138
  14.0 1.6 %collective-permute-start.4 = (f32[16,1024]{1,0:T(8,128)S(1)}, f32[16,1024]{1,0:T(8,128)S(1)}, u32[]{:S(2)}, u32[]{:S(2)}) collective-permute-start(f32[16,1024]{1,0:T(8,128)S(1)} %get-tuple-element.43), channel_id=1, source_target_pairs={{0,4},{4,0},{8,12},{12,8},{16,20},{20,16},{24,28},{28,24},{1,5},{5... | collective-permute-start | bytes 196616 | tf_op jit(solution)/shard_map/ppermute | solution.py:120
  15.6 2.2 %copy-start = (s32[1024,1024]{1,0:T(8,128)S(1)}, s32[1024,1024]{1,0:T(8,128)}, u32[]{:S(2)}) copy-start(s32[1024,1024]{1,0:T(8,128)} %g_ref.7) | copy-start | bytes 12582916
  23.1 1.4 %collective-permute-start.5 = (f32[32,1024]{1,0:T(8,128)S(1)}, f32[32,1024]{1,0:T(8,128)S(1)}, u32[]{:S(2)}, u32[]{:S(2)}) collective-permute-start(f32[32,1024]{1,0:T(8,128)S(1)} %get-tuple-element.21), channel_id=1, source_target_pairs={{0,4},{4,0},{8,12},{12,8},{16,20},{20,16},{24,28},{28,24},{1,5},{5... | collective-permute-start | bytes 393224 | tf_op jit(solution)/shard_map/ppermute | solution.py:120
  24.6 5.0 %collective-permute-start.8 = (f32[32,1024]{1,0:T(8,128)S(1)}, f32[32,1024]{1,0:T(8,128)S(1)}, u32[]{:S(2)}, u32[]{:S(2)}) collective-permute-start(f32[32,1024]{1,0:T(8,128)S(1)} %add.101), channel_id=1, source_target_pairs={{0,8},{1,9},{2,10},{3,11},{4,5},{5,4},{6,7},{7,6},{8,0},{9,1},{10,... | collective-permute-start | bytes 393224 | tf_op jit(solution)/shard_map/ppermute | solution.py:138
  26.1 5.0 %collective-permute-start.7 = (f32[32,1024]{1,0:T(8,128)S(1)}, f32[32,1024]{1,0:T(8,128)S(1)}, u32[]{:S(2)}, u32[]{:S(2)}) collective-permute-start(f32[32,1024]{1,0:T(8,128)S(1)} %add.101), channel_id=1, source_target_pairs={{0,16},{1,17},{2,18},{3,19},{4,6},{5,7},{6,4},{7,5},{8,24},{9,25},... | collective-permute-start | bytes 393224 | tf_op jit(solution)/shard_map/ppermute | solution.py:138
  27.7 5.9 %collective-permute-start.6 = (f32[32,1024]{1,0:T(8,128)S(1)}, f32[32,1024]{1,0:T(8,128)S(1)}, u32[]{:S(2)}, u32[]{:S(2)}) collective-permute-start(f32[32,1024]{1,0:T(8,128)S(1)} %add.101), channel_id=1, source_target_pairs={{0,24},{1,25},{2,26},{3,27},{4,7},{5,6},{6,5},{7,4},{8,16},{9,17},... | collective-permute-start | bytes 393224 | tf_op jit(solution)/shard_map/ppermute | solution.py:138
  33.6 1.3 %collective-permute-start.9 = (f32[16,1024]{1,0:T(8,128)S(1)}, f32[16,1024]{1,0:T(8,128)S(1)}, u32[]{:S(2)}, u32[]{:S(2)}) collective-permute-start(f32[16,1024]{1,0:T(8,128)S(1)} %get-tuple-element.41), channel_id=1, source_target_pairs={{0,4},{4,0},{8,12},{12,8},{16,20},{20,16},{24,28},{28,24},{1,5},{5... | collective-permute-start | bytes 196616 | tf_op jit(solution)/shard_map/ppermute | solution.py:120
  40.3 1.4 %collective-permute-start.10 = (f32[32,1024]{1,0:T(8,128)S(1)}, f32[32,1024]{1,0:T(8,128)S(1)}, u32[]{:S(2)}, u32[]{:S(2)}) collective-permute-start(f32[32,1024]{1,0:T(8,128)S(1)} %get-tuple-element.25), channel_id=1, source_target_pairs={{0,4},{4,0},{8,12},{12,8},{16,20},{20,16},{24,28},{28,24},{1,5},{5... | collective-permute-start | bytes 393224 | tf_op jit(solution)/shard_map/ppermute | solution.py:120
  41.7 5.0 %collective-permute-start.13 = (f32[32,1024]{1,0:T(8,128)S(1)}, f32[32,1024]{1,0:T(8,128)S(1)}, u32[]{:S(2)}, u32[]{:S(2)}) collective-permute-start(f32[32,1024]{1,0:T(8,128)S(1)} %add.106), channel_id=1, source_target_pairs={{0,8},{1,9},{2,10},{3,11},{4,5},{5,4},{6,7},{7,6},{8,0},{9,1},{10,... | collective-permute-start | bytes 393224 | tf_op jit(solution)/shard_map/ppermute | solution.py:138
  43.1 5.0 %collective-permute-start.12 = (f32[32,1024]{1,0:T(8,128)S(1)}, f32[32,1024]{1,0:T(8,128)S(1)}, u32[]{:S(2)}, u32[]{:S(2)}) collective-permute-start(f32[32,1024]{1,0:T(8,128)S(1)} %add.106), channel_id=1, source_target_pairs={{0,16},{1,17},{2,18},{3,19},{4,6},{5,7},{6,4},{7,5},{8,24},{9,25},... | collective-permute-start | bytes 393224 | tf_op jit(solution)/shard_map/ppermute | solution.py:138
  44.6 5.9 %collective-permute-start.11 = (f32[32,1024]{1,0:T(8,128)S(1)}, f32[32,1024]{1,0:T(8,128)S(1)}, u32[]{:S(2)}, u32[]{:S(2)}) collective-permute-start(f32[32,1024]{1,0:T(8,128)S(1)} %add.106), channel_id=1, source_target_pairs={{0,24},{1,25},{2,26},{3,27},{4,7},{5,6},{6,5},{7,4},{8,16},{9,17},... | collective-permute-start | bytes 393224 | tf_op jit(solution)/shard_map/ppermute | solution.py:138
  50.6 1.7 %collective-permute-start.14 = (f32[16,1024]{1,0:T(8,128)S(1)}, f32[16,1024]{1,0:T(8,128)S(1)}, u32[]{:S(2)}, u32[]{:S(2)}) collective-permute-start(f32[16,1024]{1,0:T(8,128)S(1)} %get-tuple-element.39), channel_id=1, source_target_pairs={{0,4},{4,0},{8,12},{12,8},{16,20},{20,16},{24,28},{28,24},{1,5},{5... | collective-permute-start | bytes 196616 | tf_op jit(solution)/shard_map/ppermute | solution.py:120
  57.6 1.4 %collective-permute-start.15 = (f32[32,1024]{1,0:T(8,128)S(1)}, f32[32,1024]{1,0:T(8,128)S(1)}, u32[]{:S(2)}, u32[]{:S(2)}) collective-permute-start(f32[32,1024]{1,0:T(8,128)S(1)} %get-tuple-element.29), channel_id=1, source_target_pairs={{0,4},{4,0},{8,12},{12,8},{16,20},{20,16},{24,28},{28,24},{1,5},{5... | collective-permute-start | bytes 393224 | tf_op jit(solution)/shard_map/ppermute | solution.py:120
  59.1 5.0 %collective-permute-start.18 = (f32[32,1024]{1,0:T(8,128)S(1)}, f32[32,1024]{1,0:T(8,128)S(1)}, u32[]{:S(2)}, u32[]{:S(2)}) collective-permute-start(f32[32,1024]{1,0:T(8,128)S(1)} %add.111), channel_id=1, source_target_pairs={{0,8},{1,9},{2,10},{3,11},{4,5},{5,4},{6,7},{7,6},{8,0},{9,1},{10,... | collective-permute-start | bytes 393224 | tf_op jit(solution)/shard_map/ppermute | solution.py:138
  60.6 5.0 %collective-permute-start.17 = (f32[32,1024]{1,0:T(8,128)S(1)}, f32[32,1024]{1,0:T(8,128)S(1)}, u32[]{:S(2)}, u32[]{:S(2)}) collective-permute-start(f32[32,1024]{1,0:T(8,128)S(1)} %add.111), channel_id=1, source_target_pairs={{0,16},{1,17},{2,18},{3,19},{4,6},{5,7},{6,4},{7,5},{8,24},{9,25},... | collective-permute-start | bytes 393224 | tf_op jit(solution)/shard_map/ppermute | solution.py:138
  62.1 5.9 %collective-permute-start.16 = (f32[32,1024]{1,0:T(8,128)S(1)}, f32[32,1024]{1,0:T(8,128)S(1)}, u32[]{:S(2)}, u32[]{:S(2)}) collective-permute-start(f32[32,1024]{1,0:T(8,128)S(1)} %add.111), channel_id=1, source_target_pairs={{0,24},{1,25},{2,26},{3,27},{4,7},{5,6},{6,5},{7,4},{8,16},{9,17},... | collective-permute-start | bytes 393224 | tf_op jit(solution)/shard_map/ppermute | solution.py:138
  68.1 1.7 %collective-permute-start.19 = (f32[16,1024]{1,0:T(8,128)S(1)}, f32[16,1024]{1,0:T(8,128)S(1)}, u32[]{:S(2)}, u32[]{:S(2)}) collective-permute-start(f32[16,1024]{1,0:T(8,128)S(1)} %get-tuple-element.37), channel_id=1, source_target_pairs={{0,4},{4,0},{8,12},{12,8},{16,20},{20,16},{24,28},{28,24},{1,5},{5... | collective-permute-start | bytes 196616 | tf_op jit(solution)/shard_map/ppermute | solution.py:120
  75.1 1.4 %collective-permute-start.20 = (f32[32,1024]{1,0:T(8,128)S(1)}, f32[32,1024]{1,0:T(8,128)S(1)}, u32[]{:S(2)}, u32[]{:S(2)}) collective-permute-start(f32[32,1024]{1,0:T(8,128)S(1)} %get-tuple-element.33), channel_id=1, source_target_pairs={{0,4},{4,0},{8,12},{12,8},{16,20},{20,16},{24,28},{28,24},{1,5},{5... | collective-permute-start | bytes 393224 | tf_op jit(solution)/shard_map/ppermute | solution.py:120
  76.6 5.0 %collective-permute-start.23 = (f32[32,1024]{1,0:T(8,128)S(1)}, f32[32,1024]{1,0:T(8,128)S(1)}, u32[]{:S(2)}, u32[]{:S(2)}) collective-permute-start(f32[32,1024]{1,0:T(8,128)S(1)} %add.116), channel_id=1, source_target_pairs={{0,8},{1,9},{2,10},{3,11},{4,5},{5,4},{6,7},{7,6},{8,0},{9,1},{10,... | collective-permute-start | bytes 393224 | tf_op jit(solution)/shard_map/ppermute | solution.py:138
  78.1 5.0 %collective-permute-start.22 = (f32[32,1024]{1,0:T(8,128)S(1)}, f32[32,1024]{1,0:T(8,128)S(1)}, u32[]{:S(2)}, u32[]{:S(2)}) collective-permute-start(f32[32,1024]{1,0:T(8,128)S(1)} %add.116), channel_id=1, source_target_pairs={{0,16},{1,17},{2,18},{3,19},{4,6},{5,7},{6,4},{7,5},{8,24},{9,25},... | collective-permute-start | bytes 393224 | tf_op jit(solution)/shard_map/ppermute | solution.py:138
  79.6 5.9 %collective-permute-start.21 = (f32[32,1024]{1,0:T(8,128)S(1)}, f32[32,1024]{1,0:T(8,128)S(1)}, u32[]{:S(2)}, u32[]{:S(2)}) collective-permute-start(f32[32,1024]{1,0:T(8,128)S(1)} %add.116), channel_id=1, source_target_pairs={{0,24},{1,25},{2,26},{3,27},{4,7},{5,6},{6,5},{7,4},{8,16},{9,17},... | collective-permute-start | bytes 393224 | tf_op jit(solution)/shard_map/ppermute | solution.py:138
  85.6 1.7 %collective-permute-start.24 = (f32[16,1024]{1,0:T(8,128)S(1)}, f32[16,1024]{1,0:T(8,128)S(1)}, u32[]{:S(2)}, u32[]{:S(2)}) collective-permute-start(f32[16,1024]{1,0:T(8,128)S(1)} %slice_select_fusion.2), channel_id=1, source_target_pairs={{0,4},{4,0},{8,12},{12,8},{16,20},{20,16},{24,28},{28,24},{1,5},{5... | collective-permute-start | bytes 196616 | tf_op jit(solution)/shard_map/ppermute | solution.py:120

commit v2 on v1

v2 whole, which is shorter than its diff:
```python
import functools

import jax
import jax.numpy as jnp
from jax import lax
from jax.experimental import pallas as pl
from jax.experimental.pallas import tpu as pltpu
from jax.sharding import PartitionSpec as P

ITERS = 4
AXES = ("ind", "snp")
ROWS = 256
COLS = 256
NT = (((1,), (1,)), ((), ()))
SMEM = pl.BlockSpec(memory_space=pltpu.SMEM)
VMEM = pl.BlockSpec(memory_space=pltpu.VMEM)
HBM = pl.BlockSpec(memory_space=pltpu.HBM)


def split3(x):
    one = x.astype(jnp.bfloat16)
    rest = x - one.astype(jnp.float32)
    two = rest.astype(jnp.bfloat16)
    three = (rest - two.astype(jnp.float32)).astype(jnp.bfloat16)
    return one, two, three


def split2(x):
    one = x.astype(jnp.bfloat16)
    return one, (x - one.astype(jnp.float32)).astype(jnp.bfloat16)


def fold3(x):
    k = x.shape[0] // 3
    return x[:k] + x[k : 2 * k] + x[2 * k :]


def mxu(a, b, dims=(((1,), (0,)), ((), ()))):
    return lax.dot_general(a, b, dims, preferred_element_type=jnp.float32)


def new_ancestry(q, a_sum, snps_all):
    rest = snps_all - jnp.sum(q * a_sum, axis=0, keepdims=True)
    return q * (a_sum + rest) * (1.0 / snps_all)


def load_kernel(g_hbm, half_ref, buf, sems):
    n = buf.shape[0]
    rows = buf.shape[1]
    copies = [pltpu.make_async_copy(g_hbm.at[pl.ds(b * rows, rows)], buf.at[b], sems.at[b]) for b in range(n)]
    for copy in copies:
        copy.start()
    for b in range(n):
        copies[b].wait()
        half_ref[pl.ds(b * rows, rows), :] = 0.5 * buf[b].astype(jnp.float32)


def load_counts(genotypes):
    individuals, snps = genotypes.shape
    rows = 128
    n = individuals // rows
    return pl.pallas_call(
        load_kernel,
        out_shape=jax.ShapeDtypeStruct((individuals, snps), jnp.float32),
        in_specs=[HBM],
        out_specs=VMEM,
        scratch_shapes=[pltpu.VMEM((n, rows, snps), jnp.int32), pltpu.SemaphoreType.DMA((n,))],
        compiler_params=pltpu.CompilerParams(vmem_limit_bytes=16 * 1024 * 1024),
        cost_estimate=pl.CostEstimate(flops=individuals * snps, bytes_accessed=4 * individuals * snps, transcendentals=0),
    )(genotypes)


def em_kernel(first, snps_all, core_ref, g_ref, q_ref, keep_ref, got_ref, mine_ref, send_ref, q_out, p_out, qs_ref, ql_ref, ps_ref, pr_ref, dh_ref, dl_ref, th_ref, tl_ref):
    core = core_ref[0]
    keep, got = keep_ref[...], got_ref[...]
    p = jnp.where(core == 0, keep, got)
    a_sum = jnp.where(core == 0, got, keep)
    q = a_sum if first else new_ancestry(q_ref[...], a_sum, snps_all)
    q_out[...] = q
    p_out[...] = p
    k = q.shape[0]
    individuals, snps = g_ref.shape
    q1, q2, q3 = split3(q)
    p1, p2, p3 = split3(p)
    qs_ref[...] = jnp.concatenate([q1, q2, q3], axis=0)
    ps_ref[...] = jnp.concatenate([p1, p2, p3], axis=0)
    ql_ref[...] = jnp.concatenate([q1, q2, q1, q2, q3, q1], axis=0).T
    pr_ref[...] = jnp.concatenate([p1, p1, p2, p2, p1, p3], axis=0)

    def ratios(b):
        at = slice(b * ROWS, (b + 1) * ROWS)
        slot = b % 2
        for c in range(0, snps, COLS):
            to = slice(c, c + COLS)
            e = mxu(ql_ref[at, :], pr_ref[:, to])
            half = g_ref[at, to]
            d = e * (1.0 - e)
            inv = pltpu.reciprocal(d, approx=True)
            inv = inv * (2.0 - d * inv)
            diff = (half - e) * inv
            two = ((1.0 - half) * e) * inv
            dh_ref[slot, :, to], dl_ref[slot, :, to] = split2(diff)
            th_ref[slot, :, to], tl_ref[slot, :, to] = split2(two)

    pd = pt = 0.0
    blocks = individuals // ROWS
    for b in range(blocks + 1):
        if b < blocks:
            ratios(b)
        if b > 0:
            at = slice((b - 1) * ROWS, b * ROWS)
            slot = (b - 1) % 2
            dh, dl, th, tl = dh_ref[slot], dl_ref[slot], th_ref[slot], tl_ref[slot]
            mine_ref[k:, at] = fold3(mxu(ps_ref[...], dh, NT) + mxu(ps_ref[...], dl, NT))
            qb = qs_ref[:, at]
            pd = pd + fold3(mxu(qb, dh) + mxu(qb, dl))
            pt = pt + fold3(mxu(qb, th) + mxu(qb, tl))
    a = mine_ref[k:, :]
    one = pd + pt

    @pl.when(core == 0)
    def _():
        send_ref[:k] = a
        send_ref[k:] = jnp.zeros_like(a)
        mine_ref[:k] = one
        mine_ref[k:] = pt

    @pl.when(core == 1)
    def _():
        send_ref[:k] = one
        send_ref[k:] = pt
        mine_ref[:k] = jnp.zeros_like(a)


def em_step(first, snps_all, core, half, q, keep, got):
    individuals, snps = half.shape
    k = q.shape[0]
    f32, bf16 = jnp.float32, jnp.bfloat16
    return pl.pallas_call(
        functools.partial(em_kernel, first, snps_all),
        out_shape=(
            jax.ShapeDtypeStruct((2 * k, snps), f32),
            jax.ShapeDtypeStruct((2 * k, snps), f32),
            jax.ShapeDtypeStruct((k, individuals), f32),
            jax.ShapeDtypeStruct((k, snps), f32),
        ),
        in_specs=[SMEM] + [VMEM] * 4,
        out_specs=(VMEM,) * 4,
        scratch_shapes=[
            pltpu.VMEM((3 * k, individuals), bf16),
            pltpu.VMEM((individuals, 6 * k), bf16),
            pltpu.VMEM((3 * k, snps), bf16),
            pltpu.VMEM((6 * k, snps), bf16),
        ]
        + [pltpu.VMEM((2, ROWS, snps), bf16)] * 4,
        compiler_params=pltpu.CompilerParams(vmem_limit_bytes=32 * 1024 * 1024),
        cost_estimate=pl.CostEstimate(flops=2 * 20 * k * individuals * snps, bytes_accessed=4 * individuals * snps, transcendentals=individuals * snps),
    )(core, half, q, keep, got)


def swap_cores(x, n_ind):
    return lax.ppermute(x, "ind", [(i, i ^ 1) for i in range(n_ind)])


def exchange(x, mask, n_ind, n_snp):
    n_chip = n_ind // 2
    pairs = []
    for i in range(n_ind):
        for s in range(n_snp):
            if i % 2 == 0 and mask < n_chip:
                pairs.append((i * n_snp + s, (i ^ (2 * mask)) * n_snp + s))
            if i % 2 == 1 and mask < n_snp:
                pairs.append((i * n_snp + s, i * n_snp + (s ^ mask)))
    return lax.ppermute(x, AXES, pairs) if pairs else None


def sum_groups(buf, n_ind, n_snp):
    base = 1
    while base < max(n_ind // 2, n_snp):
        parts = [exchange(buf, m * base, n_ind, n_snp) for m in (1, 2, 3)]
        parts = [part for part in parts if part is not None]
        if len(parts) == 3:
            buf = (buf + parts[2]) + (parts[1] + parts[0])
        else:
            for part in parts:
                buf = buf + part
        base *= 4
    return buf


def place(shard, index, count):
    width = shard.shape[1]
    full = jnp.zeros((shard.shape[0], width * count), shard.dtype)
    return lax.dynamic_update_slice_in_dim(full, shard, index * width, axis=1)


def gather_small(core_id, index, genotypes, ancestry, freqs, n_ind, n_snp):
    k = ancestry.shape[0]
    first_core = core_id[0] == 0
    none = jnp.zeros_like(freqs)
    recv = swap_cores(jnp.where(first_core, ancestry, jnp.concatenate([none, freqs], axis=1)), n_ind)
    zeros = jnp.zeros_like(ancestry)
    mine = jnp.where(first_core, jnp.concatenate([jnp.concatenate([freqs, none], axis=1), zeros]), jnp.concatenate([zeros, ancestry]))
    mine = lax.optimization_barrier(mine)
    own = jnp.concatenate([mine[:k] + recv, mine[k:]])
    own, genotypes = lax.optimization_barrier((own, genotypes))
    half = load_counts(genotypes)
    chunks = [own] + [exchange(own, m, n_ind, n_snp) for m in range(1, n_snp)]
    *chunks, half = lax.optimization_barrier((*chunks, half))
    bit = 1
    while bit < n_snp:
        flip = (index & bit) != 0
        chunks = [jnp.where(flip, chunks[j ^ bit], chunks[j]) for j in range(n_snp)]
        bit *= 2
    full = jnp.concatenate(chunks, axis=1)
    keep = jnp.where(first_core, full[:k], full[k:])
    return half, keep, swap_cores(full[:k], n_ind)


def close_kernel(snps_all, at_ref, q_ref, p_ref, keep_ref, got_ref, q_out, p_out):
    core = at_ref[0]
    keep, got = keep_ref[...], got_ref[...]
    sums = jnp.where(core == 0, keep, got)
    a_sum = jnp.where(core == 0, got, keep)
    k, wide = q_out.shape
    width = p_out.shape[1]
    a_sum = jnp.concatenate([a_sum[:k], a_sum[k:]], axis=1)
    q = q_ref[:, pl.ds(pl.multiple_of(at_ref[1], 128), wide)]
    p = p_ref[:, pl.ds(pl.multiple_of(at_ref[2], 128), width)]
    q_out[...] = new_ancestry(q, a_sum, snps_all)
    up = p * sums[:k]
    p_out[...] = up / (up + (1.0 - p) * sums[k:])


def finish_small(snps_all, core_id, index, at, mine, send, q, p, n_ind, n_snp, shapes):
    k = q.shape[0]
    buf = mine + swap_cores(send, n_ind)
    wide = shapes[0][1]
    half = wide // 2
    chunk = lambda m: lax.dynamic_slice_in_dim(buf, (index ^ m) * wide, wide, axis=1)
    parts = [exchange(chunk(m), m, n_ind, n_snp) for m in range(1, n_snp)]
    total = chunk(0)
    for part in parts[::-1]:
        total = total + part
    first_core = core_id[0] == 0
    fold = lambda x: jnp.concatenate([x[:, :half], x[:, half:]])
    keep = jnp.where(first_core, total[:, :half], fold(total[k:]))
    got = swap_cores(jnp.where(first_core, total[:, half:], fold(total[:k])), n_ind)
    return pl.pallas_call(
        functools.partial(close_kernel, snps_all),
        out_shape=tuple(jax.ShapeDtypeStruct(s, jnp.float32) for s in shapes),
        in_specs=[SMEM] + [VMEM] * 4,
        out_specs=(VMEM, VMEM),
        compiler_params=pltpu.CompilerParams(vmem_limit_bytes=1024 * 1024),
    )(at, q, p, keep, got)


def body(genotypes, ancestry, freqs):
    n_ind, n_snp = lax.axis_size("ind"), lax.axis_size("snp")
    ind, snp = lax.axis_index("ind"), lax.axis_index("snp")
    core = ind % 2
    first_core = core == 0
    index = jnp.where(first_core, ind // 2, snp)
    k = ancestry.shape[0]
    snps_all = genotypes.shape[1] * n_snp
    core_id = core.reshape(1).astype(jnp.int32)
    at = jnp.stack([core, snp * ancestry.shape[1], ind * freqs.shape[1]]).astype(jnp.int32)
    small = n_ind == 2 * n_snp and ancestry.shape[1] == 2 * freqs.shape[1] and freqs.shape[1] % 128 == 0

    if small:
        half, keep, got = gather_small(core_id, index, genotypes, ancestry, freqs, n_ind, n_snp)
        q = keep
    else:
        half = load_counts(genotypes)
        q_at = place(ancestry, snp, n_snp)
        p_at = place(freqs, ind, n_ind)
        q = none = jnp.zeros_like(q_at)
        mine = jnp.concatenate([jnp.where(first_core, p_at, none), jnp.where(first_core, none, q_at)])
        send = jnp.concatenate([jnp.where(first_core, q_at, p_at), none])
        buf = sum_groups(mine + swap_cores(send, n_ind), n_ind, n_snp)
        keep = jnp.where(first_core, buf[:k], buf[k:])
        got = swap_cores(buf[:k], n_ind)
    for step in range(ITERS):
        mine, send, q, p = em_step(step == 0, snps_all, core_id, half, q, keep, got)
        if small and step == ITERS - 1:
            return finish_small(snps_all, core_id, index, at, mine, send, q, p, n_ind, n_snp, (ancestry.shape, freqs.shape))
        buf = sum_groups(mine + swap_cores(send, n_ind), n_ind, n_snp)
        up = p * buf[:k]
        p_new = up / (up + (1.0 - p) * buf[k:])
        keep = jnp.where(first_core, p_new, buf[k:])
        got = swap_cores(jnp.where(first_core, p_new, buf[:k]), n_ind)
    p = jnp.where(first_core, keep, got)
    q = new_ancestry(q, jnp.where(first_core, got, keep), snps_all)
    q_own = lax.dynamic_slice_in_dim(q, snp * ancestry.shape[1], ancestry.shape[1], axis=1)
    p_own = lax.dynamic_slice_in_dim(p, ind * freqs.shape[1], freqs.shape[1], axis=1)
    return (q_own, p_own)


def solution(mesh):
    in_specs = (P("ind", "snp"), P(None, ("ind", "snp")), P(None, ("snp", "ind")))
    out_specs = (P(None, ("ind", "snp")), P(None, ("snp", "ind")))
    return jax.shard_map(body, mesh=mesh, in_specs=in_specs, out_specs=out_specs, check_vma=False)
```

time: 88.9 us -> 75.3 us (0.85)
  waiting for transfers between devices: 36.8 us -> 27.4 us
  Pallas kernels: 21.5 us -> 18.1 us
  local copies, waits for them, and re-layouts: 3.72 us -> 2.21 us
    ppermute x15, waiting for transfers between devices: 27.2 us -> 19 us  [exchange(): return lax.ppermute(x, AXES, pairs) if pairs else None]
    pallas_call x4 -> x6, Pallas kernels: 21.5 us -> 18.1 us  [the longest x4 16.3 us: em_step(): pl.pallas_call(functools.partial(em_kernel, first, snps_all), out_shape=(...]
    dynamic_update_slice x2 -> x0, local copies, waits for them, and re-layouts: 1.42 us -> none  [place(): return lax.dynamic_update_slice_in_dim(full, shard, index * width, axis=1)]
    ppermute x10, waiting for transfers between devices: 9.6 us -> 8.42 us  [swap_cores(): return lax.ppermute(x, 'ind', [(i, i ^ 1) for i in range(n_ind)])]
  transfers between devices with their start and end apart: 25 -> 25, of which waited for: 25 -> 23; matrix products, arithmetic and copies ran while one was open for 0% -> 1% of each run, Pallas kernels for 0% -> 1%
where the time goes in v2:
time: 75.3 us; the launch traced here: 74.8 us
  waiting for transfers between devices  27.4 us (36%)
  starting transfers between devices  24.4 us (32%)
  Pallas kernels  18.1 us (24%)
  local copies, waits for them, and re-layouts  2.21 us (3%)
  other arithmetic  1.86 us (2%)
  between operations  0.79 us (1%)
    ppermute x15, waiting for transfers between devices, exchange(): return lax.ppermute(x, AXES, pairs) if pairs else None  19 us
    ppermute x15, starting transfers between devices, exchange(): return lax.ppermute(x, AXES, pairs) if pairs else None  18.7 us
    pallas_call x4, Pallas kernels, em_step(): pl.pallas_call(functools.partial(em_kernel, first, snps_all), out_shape=(...  16.3 us
    ppermute x10, waiting for transfers between devices, swap_cores(): return lax.ppermute(x, 'ind', [(i, i ^ 1) for i in range(n_ind)])  8.42 us
    ppermute x10, starting transfers between devices, swap_cores(): return lax.ppermute(x, 'ind', [(i, i ^ 1) for i in range(n_ind)])  5.78 us
    unnamed x2, local copies, waits for them, and re-layouts  2.19 us
  transfers between devices with their start and end apart: 25, of which 23 were waited for; matrix products, arithmetic and copies ran while one was open for 1% of the time, Pallas kernels for 1%

profile of v2, /device:TPU:0, one launch (start us, length us, event | category | flops | bytes accessed | tf_op | source)
XLA Modules:
  0.0 74.8 jit_solution(11797147622836101248)
XLA Ops:
  2.7 2.9 %collective-permute-start.1 = (f32[32,256]{1,0:T(8,128)S(1)}, f32[32,256]{1,0:T(8,128)S(1)}, u32[]{:S(2)}, u32[]{:S(2)}) collective-permute-start(f32[32,256]{1,0:T(8,128)S(1)} %pad_maximum_fusion.1), channel_id=1, source_target_pairs={{0,8},{1,9},{2,10},{3,11},{4,5},{5,4},{6,7},{7,6},{8,0},{9,1},{10,... | collective-permute-start | bytes 98312 | tf_op jit(solution)/shard_map/ppermute | solution.py:174
  5.6 1.5 %collective-permute-start.2 = (f32[32,256]{1,0:T(8,128)S(1)}, f32[32,256]{1,0:T(8,128)S(1)}, u32[]{:S(2)}, u32[]{:S(2)}) collective-permute-start(f32[32,256]{1,0:T(8,128)S(1)} %pad_maximum_fusion.1), channel_id=1, source_target_pairs={{0,16},{1,17},{2,18},{3,19},{4,6},{5,7},{6,4},{7,5},{8,24},{9,25},... | collective-permute-start | bytes 98312 | tf_op jit(solution)/shard_map/ppermute | solution.py:174
  7.1 2.2 %copy-done = s32[1024,1024]{1,0:T(8,128)S(1)} copy-done((s32[1024,1024]{1,0:T(8,128)S(1)}, s32[1024,1024]{1,0:T(8,128)}, u32[]{:S(2)}) %copy-start) | copy-done | bytes 4194328
  10.0 1.9 %collective-permute-done.3 = f32[32,256]{1,0:T(8,128)S(1)} collective-permute-done((f32[32,256]{1,0:T(8,128)S(1)}, f32[32,256]{1,0:T(8,128)S(1)}, u32[]{:S(2)}, u32[]{:S(2)}) %collective-permute-start.3) | collective-permute-done | bytes 32800 | tf_op jit(solution)/shard_map/ppermute | solution.py:174
  13.4 4.0 %shard_map.51 = (f32[32,1024]{1,0:T(8,128)S(1)}, f32[32,1024]{1,0:T(8,128)S(1)}, f32[16,1024]{1,0:T(8,128)S(1)}, f32[16,1024]{1,0:T(8,128)S(1)}) custom-call(s32[1]{0:T(128)} %bitcast.core_ref, f32[1024,1024]{1,0:T(8,128)S(1)} %shard_map.50.g_ref, f32[16,1024]{1,0:T(8,128)S(1)} %get-tuple-element.58.q_ref.keep_ref, ...), custom_call_target="tpu_custom_call" | custom-call | flops 671088640 | bytes 4194304 | tf_op jit(solution)/shard_map/pallas_call | solution.py:139
  17.9 1.0 %collective-permute-done.5 = f32[32,1024]{1,0:T(8,128)S(1)} collective-permute-done((f32[32,1024]{1,0:T(8,128)S(1)}, f32[32,1024]{1,0:T(8,128)S(1)}, u32[]{:S(2)}, u32[]{:S(2)}) %collective-permute-start.5) | collective-permute-done | bytes 131104 | tf_op jit(solution)/shard_map/ppermute | solution.py:162
  18.9 1.6 %collective-permute-start.7 = (f32[32,1024]{1,0:T(8,128)S(1)}, f32[32,1024]{1,0:T(8,128)S(1)}, u32[]{:S(2)}, u32[]{:S(2)}) collective-permute-start(f32[32,1024]{1,0:T(8,128)S(1)} %add.87), channel_id=1, source_target_pairs={{0,16},{1,17},{2,18},{3,19},{4,6},{5,7},{6,4},{7,5},{8,24},{9,25},... | collective-permute-start | bytes 393224 | tf_op jit(solution)/shard_map/ppermute | solution.py:174
  20.5 1.5 %collective-permute-start.8 = (f32[32,1024]{1,0:T(8,128)S(1)}, f32[32,1024]{1,0:T(8,128)S(1)}, u32[]{:S(2)}, u32[]{:S(2)}) collective-permute-start(f32[32,1024]{1,0:T(8,128)S(1)} %add.87), channel_id=1, source_target_pairs={{0,8},{1,9},{2,10},{3,11},{4,5},{5,4},{6,7},{7,6},{8,0},{9,1},{10,... | collective-permute-start | bytes 393224 | tf_op jit(solution)/shard_map/ppermute | solution.py:174
  22.5 1.5 %collective-permute-done.7 = f32[32,1024]{1,0:T(8,128)S(1)} collective-permute-done((f32[32,1024]{1,0:T(8,128)S(1)}, f32[32,1024]{1,0:T(8,128)S(1)}, u32[]{:S(2)}, u32[]{:S(2)}) %collective-permute-start.7) | collective-permute-done | bytes 131104 | tf_op jit(solution)/shard_map/ppermute | solution.py:174
  24.0 1.5 %collective-permute-done.8 = f32[32,1024]{1,0:T(8,128)S(1)} collective-permute-done((f32[32,1024]{1,0:T(8,128)S(1)}, f32[32,1024]{1,0:T(8,128)S(1)}, u32[]{:S(2)}, u32[]{:S(2)}) %collective-permute-start.8) | collective-permute-done | bytes 131104 | tf_op jit(solution)/shard_map/ppermute | solution.py:174
  25.5 2.4 %collective-permute-done.6 = f32[32,1024]{1,0:T(8,128)S(1)} collective-permute-done((f32[32,1024]{1,0:T(8,128)S(1)}, f32[32,1024]{1,0:T(8,128)S(1)}, u32[]{:S(2)}, u32[]{:S(2)}) %collective-permute-start.6) | collective-permute-done | bytes 131104 | tf_op jit(solution)/shard_map/ppermute | solution.py:174
  28.4 0.9 %collective-permute-done.9.got_ref = f32[16,1024]{1,0:T(8,128)S(1)} collective-permute-done((f32[16,1024]{1,0:T(8,128)S(1)}, f32[16,1024]{1,0:T(8,128)S(1)}, u32[]{:S(2)}, u32[]{:S(2)}) %collective-permute-start.9) | collective-permute-done | bytes 65568 | tf_op jit(solution)/shard_map/ppermute | solution.py:162
  29.3 4.2 %shard_map.52 = (f32[32,1024]{1,0:T(8,128)S(1)}, f32[32,1024]{1,0:T(8,128)S(1)}, f32[16,1024]{1,0:T(8,128)S(1)}, f32[16,1024]{1,0:T(8,128)S(1)}) custom-call(s32[1]{0:T(128)} %bitcast.core_ref, f32[1024,1024]{1,0:T(8,128)S(1)} %shard_map.50.g_ref, f32[16,1024]{1,0:T(8,128)S(1)} %get-tuple-element.32.q_ref, f32[16,1024]{1,0:T(8,128)S(1)} %get-tuple-element.53.keep_ref, ...), custom_call_target="tpu_custom_call" | custom-call | flops 671088640 | bytes 4194304 | tf_op jit(solution)/shard_map/pallas_call | solution.py:139
  34.0 1.0 %collective-permute-done.10 = f32[32,1024]{1,0:T(8,128)S(1)} collective-permute-done((f32[32,1024]{1,0:T(8,128)S(1)}, f32[32,1024]{1,0:T(8,128)S(1)}, u32[]{:S(2)}, u32[]{:S(2)}) %collective-permute-start.10) | collective-permute-done | bytes 131104 | tf_op jit(solution)/shard_map/ppermute | solution.py:162
  35.6 1.3 %collective-permute-start.13 = (f32[32,1024]{1,0:T(8,128)S(1)}, f32[32,1024]{1,0:T(8,128)S(1)}, u32[]{:S(2)}, u32[]{:S(2)}) collective-permute-start(f32[32,1024]{1,0:T(8,128)S(1)} %add.92), channel_id=1, source_target_pairs={{0,8},{1,9},{2,10},{3,11},{4,5},{5,4},{6,7},{7,6},{8,0},{9,1},{10,... | collective-permute-start | bytes 393224 | tf_op jit(solution)/shard_map/ppermute | solution.py:174
  36.9 1.6 %collective-permute-start.11 = (f32[32,1024]{1,0:T(8,128)S(1)}, f32[32,1024]{1,0:T(8,128)S(1)}, u32[]{:S(2)}, u32[]{:S(2)}) collective-permute-start(f32[32,1024]{1,0:T(8,128)S(1)} %add.92), channel_id=1, source_target_pairs={{0,24},{1,25},{2,26},{3,27},{4,7},{5,6},{6,5},{7,4},{8,16},{9,17},... | collective-permute-start | bytes 393224 | tf_op jit(solution)/shard_map/ppermute | solution.py:174
  38.6 1.5 %collective-permute-done.12 = f32[32,1024]{1,0:T(8,128)S(1)} collective-permute-done((f32[32,1024]{1,0:T(8,128)S(1)}, f32[32,1024]{1,0:T(8,128)S(1)}, u32[]{:S(2)}, u32[]{:S(2)}) %collective-permute-start.12) | collective-permute-done | bytes 131104 | tf_op jit(solution)/shard_map/ppermute | solution.py:174
  40.6 2.3 %collective-permute-done.11 = f32[32,1024]{1,0:T(8,128)S(1)} collective-permute-done((f32[32,1024]{1,0:T(8,128)S(1)}, f32[32,1024]{1,0:T(8,128)S(1)}, u32[]{:S(2)}, u32[]{:S(2)}) %collective-permute-start.11) | collective-permute-done | bytes 131104 | tf_op jit(solution)/shard_map/ppermute | solution.py:174
  43.0 1.0 %collective-permute-start.14 = (f32[16,1024]{1,0:T(8,128)S(1)}, f32[16,1024]{1,0:T(8,128)S(1)}, u32[]{:S(2)}, u32[]{:S(2)}) collective-permute-start(f32[16,1024]{1,0:T(8,128)S(1)} %get-tuple-element.50), channel_id=1, source_target_pairs={{0,4},{4,0},{8,12},{12,8},{16,20},{20,16},{24,28},{28,24},{1,5},{5... | collective-permute-start | bytes 196616 | tf_op jit(solution)/shard_map/ppermute | solution.py:162
  44.9 4.0 %shard_map.53 = (f32[32,1024]{1,0:T(8,128)S(1)}, f32[32,1024]{1,0:T(8,128)S(1)}, f32[16,1024]{1,0:T(8,128)S(1)}, f32[16,1024]{1,0:T(8,128)S(1)}) custom-call(s32[1]{0:T(128)} %bitcast.core_ref, f32[1024,1024]{1,0:T(8,128)S(1)} %shard_map.50.g_ref, f32[16,1024]{1,0:T(8,128)S(1)} %get-tuple-element.36.q_ref, f32[16,1024]{1,0:T(8,128)S(1)} %get-tuple-element.51.keep_ref, ...), custom_call_target="tpu_custom_call" | custom-call | flops 671088640 | bytes 4194304 | tf_op jit(solution)/shard_map/pallas_call | solution.py:139
  49.4 1.0 %collective-permute-done.15 = f32[32,1024]{1,0:T(8,128)S(1)} collective-permute-done((f32[32,1024]{1,0:T(8,128)S(1)}, f32[32,1024]{1,0:T(8,128)S(1)}, u32[]{:S(2)}, u32[]{:S(2)}) %collective-permute-start.15) | collective-permute-done | bytes 131104 | tf_op jit(solution)/shard_map/ppermute | solution.py:162
  50.9 1.1 %collective-permute-start.18 = (f32[32,1024]{1,0:T(8,128)S(1)}, f32[32,1024]{1,0:T(8,128)S(1)}, u32[]{:S(2)}, u32[]{:S(2)}) collective-permute-start(f32[32,1024]{1,0:T(8,128)S(1)} %add.97), channel_id=1, source_target_pairs={{0,8},{1,9},{2,10},{3,11},{4,5},{5,4},{6,7},{7,6},{8,0},{9,1},{10,... | collective-permute-start | bytes 393224 | tf_op jit(solution)/shard_map/ppermute | solution.py:174
  52.0 2.0 %collective-permute-start.16 = (f32[32,1024]{1,0:T(8,128)S(1)}, f32[32,1024]{1,0:T(8,128)S(1)}, u32[]{:S(2)}, u32[]{:S(2)}) collective-permute-start(f32[32,1024]{1,0:T(8,128)S(1)} %add.97), channel_id=1, source_target_pairs={{0,24},{1,25},{2,26},{3,27},{4,7},{5,6},{6,5},{7,4},{8,16},{9,17},... | collective-permute-start | bytes 393224 | tf_op jit(solution)/shard_map/ppermute | solution.py:174
  53.9 1.5 %collective-permute-done.17 = f32[32,1024]{1,0:T(8,128)S(1)} collective-permute-done((f32[32,1024]{1,0:T(8,128)S(1)}, f32[32,1024]{1,0:T(8,128)S(1)}, u32[]{:S(2)}, u32[]{:S(2)}) %collective-permute-start.17) | collective-permute-done | bytes 131104 | tf_op jit(solution)/shard_map/ppermute | solution.py:174
  55.9 2.4 %collective-permute-done.16 = f32[32,1024]{1,0:T(8,128)S(1)} collective-permute-done((f32[32,1024]{1,0:T(8,128)S(1)}, f32[32,1024]{1,0:T(8,128)S(1)}, u32[]{:S(2)}, u32[]{:S(2)}) %collective-permute-start.16) | collective-permute-done | bytes 131104 | tf_op jit(solution)/shard_map/ppermute | solution.py:174
  59.2 0.9 %collective-permute-done.19.got_ref = f32[16,1024]{1,0:T(8,128)S(1)} collective-permute-done((f32[16,1024]{1,0:T(8,128)S(1)}, f32[16,1024]{1,0:T(8,128)S(1)}, u32[]{:S(2)}, u32[]{:S(2)}) %collective-permute-start.19) | collective-permute-done | bytes 65568 | tf_op jit(solution)/shard_map/ppermute | solution.py:162
  60.1 4.0 %shard_map.54 = (f32[32,1024]{1,0:T(8,128)S(1)}, f32[32,1024]{1,0:T(8,128)S(1)}, f32[16,1024]{1,0:T(8,128)S(1)}, f32[16,1024]{1,0:T(8,128)S(1)}) custom-call(s32[1]{0:T(128)} %bitcast.core_ref, f32[1024,1024]{1,0:T(8,128)S(1)} %shard_map.50.g_ref, f32[16,1024]{1,0:T(8,128)S(1)} %get-tuple-element.40.q_ref, f32[16,1024]{1,0:T(8,128)S(1)} %get-tuple-element.49.keep_ref, ...), custom_call_target="tpu_custom_call" | custom-call | flops 671088640 | bytes 4194304 | tf_op jit(solution)/shard_map/pallas_call | solution.py:139
  64.6 1.0 %collective-permute-done.20 = f32[32,1024]{1,0:T(8,128)S(1)} collective-permute-done((f32[32,1024]{1,0:T(8,128)S(1)}, f32[32,1024]{1,0:T(8,128)S(1)}, u32[]{:S(2)}, u32[]{:S(2)}) %collective-permute-start.20) | collective-permute-done | bytes 131104 | tf_op jit(solution)/shard_map/ppermute | solution.py:162
  66.2 1.1 %collective-permute-start.22 = (f32[32,256]{1,0:T(8,128)S(1)}, f32[32,256]{1,0:T(8,128)S(1)}, u32[]{:S(2)}, u32[]{:S(2)}) collective-permute-start(f32[32,256]{1,0:T(8,128)S(1)} %get-tuple-element.56), channel_id=1, source_target_pairs={{0,16},{1,17},{2,18},{3,19},{4,6},{5,7},{6,4},{7,5},{8,24},{9,25},... | collective-permute-start | bytes 98312 | tf_op jit(solution)/shard_map/ppermute | solution.py:174
  67.3 1.8 %collective-permute-start.21 = (f32[32,256]{1,0:T(8,128)S(1)}, f32[32,256]{1,0:T(8,128)S(1)}, u32[]{:S(2)}, u32[]{:S(2)}) collective-permute-start(f32[32,256]{1,0:T(8,128)S(1)} %get-tuple-element.54), channel_id=1, source_target_pairs={{0,24},{1,25},{2,26},{3,27},{4,7},{5,6},{6,5},{7,4},{8,16},{9,17},... | collective-permute-start | bytes 98312 | tf_op jit(solution)/shard_map/ppermute | solution.py:174
  70.1 2.0 %collective-permute-done.21 = f32[32,256]{1,0:T(8,128)S(1)} collective-permute-done((f32[32,256]{1,0:T(8,128)S(1)}, f32[32,256]{1,0:T(8,128)S(1)}, u32[]{:S(2)}, u32[]{:S(2)}) %collective-permute-start.21) | collective-permute-done | bytes 32800 | tf_op jit(solution)/shard_map/ppermute | solution.py:174
  73.6 1.2 %shard_map.55 = (f32[16,256]{1,0:T(8,128)}, f32[16,128]{1,0:T(8,128)}) custom-call(s32[3]{0:T(128)S(1)} %pad_add_fusion.at_ref, f32[16,1024]{1,0:T(8,128)S(1)} %get-tuple-element.44.q_ref, f32[16,1024]{1,0:T(8,128)S(1)} %get-tuple-element.45.p_ref, f32[32,128]{1,0:T(8,128)S(1)} %get-tuple-element.64.keep_ref, f32[32,128]{1,0:T(8,128)S(1)} %collective-permute-done.24.got_ref), custom_call_target="tpu_custom_call" | custom-call | tf_op jit(solution)/shard_map/pallas_call | solution.py:249
  (48 shorter events, 14.2 us)
Async XLA Ops:
  1.4 1.3 %collective-permute-start = (f32[16,256]{1,0:T(8,128)S(1)}, f32[16,256]{1,0:T(8,128)S(1)}, u32[]{:S(2)}, u32[]{:S(2)}) collective-permute-start(f32[16,256]{1,0:T(8,128)S(1)} %pad_select_fusion.1), channel_id=1, source_target_pairs={{0,4},{4,0},{8,12},{12,8},{16,20},{20,16},{24,28},{28,24},{1,5},{5... | collective-permute-start | bytes 49160 | tf_op jit(solution)/shard_map/ppermute | solution.py:162
  2.7 7.3 %collective-permute-start.1 = (f32[32,256]{1,0:T(8,128)S(1)}, f32[32,256]{1,0:T(8,128)S(1)}, u32[]{:S(2)}, u32[]{:S(2)}) collective-permute-start(f32[32,256]{1,0:T(8,128)S(1)} %pad_maximum_fusion.1), channel_id=1, source_target_pairs={{0,8},{1,9},{2,10},{3,11},{4,5},{5,4},{6,7},{7,6},{8,0},{9,1},{10,... | collective-permute-start | bytes 98312 | tf_op jit(solution)/shard_map/ppermute | solution.py:174
  5.6 4.4 %collective-permute-start.2 = (f32[32,256]{1,0:T(8,128)S(1)}, f32[32,256]{1,0:T(8,128)S(1)}, u32[]{:S(2)}, u32[]{:S(2)}) collective-permute-start(f32[32,256]{1,0:T(8,128)S(1)} %pad_maximum_fusion.1), channel_id=1, source_target_pairs={{0,16},{1,17},{2,18},{3,19},{4,6},{5,7},{6,4},{7,5},{8,24},{9,25},... | collective-permute-start | bytes 98312 | tf_op jit(solution)/shard_map/ppermute | solution.py:174
  7.1 4.8 %collective-permute-start.3 = (f32[32,256]{1,0:T(8,128)S(1)}, f32[32,256]{1,0:T(8,128)S(1)}, u32[]{:S(2)}, u32[]{:S(2)}) collective-permute-start(f32[32,256]{1,0:T(8,128)S(1)} %pad_maximum_fusion.1), channel_id=1, source_target_pairs={{0,24},{1,25},{2,26},{3,27},{4,7},{5,6},{6,5},{7,4},{8,16},{9,17},... | collective-permute-start | bytes 98312 | tf_op jit(solution)/shard_map/ppermute | solution.py:174
  7.1 2.2 %copy-start = (s32[1024,1024]{1,0:T(8,128)S(1)}, s32[1024,1024]{1,0:T(8,128)}, u32[]{:S(2)}) copy-start(s32[1024,1024]{1,0:T(8,128)} %g_hbm) | copy-start | bytes 12582916
  12.0 1.5 %collective-permute-start.4 = (f32[16,1024]{1,0:T(8,128)S(1)}, f32[16,1024]{1,0:T(8,128)S(1)}, u32[]{:S(2)}, u32[]{:S(2)}) collective-permute-start(f32[16,1024]{1,0:T(8,128)S(1)} %get-tuple-element.57), channel_id=1, source_target_pairs={{0,4},{4,0},{8,12},{12,8},{16,20},{20,16},{24,28},{28,24},{1,5},{5... | collective-permute-start | bytes 196616 | tf_op jit(solution)/shard_map/ppermute | solution.py:162
  17.5 1.4 %collective-permute-start.5 = (f32[32,1024]{1,0:T(8,128)S(1)}, f32[32,1024]{1,0:T(8,128)S(1)}, u32[]{:S(2)}, u32[]{:S(2)}) collective-permute-start(f32[32,1024]{1,0:T(8,128)S(1)} %get-tuple-element.35), channel_id=1, source_target_pairs={{0,4},{4,0},{8,12},{12,8},{16,20},{20,16},{24,28},{28,24},{1,5},{5... | collective-permute-start | bytes 393224 | tf_op jit(solution)/shard_map/ppermute | solution.py:162
  18.9 5.0 %collective-permute-start.7 = (f32[32,1024]{1,0:T(8,128)S(1)}, f32[32,1024]{1,0:T(8,128)S(1)}, u32[]{:S(2)}, u32[]{:S(2)}) collective-permute-start(f32[32,1024]{1,0:T(8,128)S(1)} %add.87), channel_id=1, source_target_pairs={{0,16},{1,17},{2,18},{3,19},{4,6},{5,7},{6,4},{7,5},{8,24},{9,25},... | collective-permute-start | bytes 393224 | tf_op jit(solution)/shard_map/ppermute | solution.py:174
  20.5 5.0 %collective-permute-start.8 = (f32[32,1024]{1,0:T(8,128)S(1)}, f32[32,1024]{1,0:T(8,128)S(1)}, u32[]{:S(2)}, u32[]{:S(2)}) collective-permute-start(f32[32,1024]{1,0:T(8,128)S(1)} %add.87), channel_id=1, source_target_pairs={{0,8},{1,9},{2,10},{3,11},{4,5},{5,4},{6,7},{7,6},{8,0},{9,1},{10,... | collective-permute-start | bytes 393224 | tf_op jit(solution)/shard_map/ppermute | solution.py:174
  22.0 5.9 %collective-permute-start.6 = (f32[32,1024]{1,0:T(8,128)S(1)}, f32[32,1024]{1,0:T(8,128)S(1)}, u32[]{:S(2)}, u32[]{:S(2)}) collective-permute-start(f32[32,1024]{1,0:T(8,128)S(1)} %add.87), channel_id=1, source_target_pairs={{0,24},{1,25},{2,26},{3,27},{4,7},{5,6},{6,5},{7,4},{8,16},{9,17},... | collective-permute-start | bytes 393224 | tf_op jit(solution)/shard_map/ppermute | solution.py:174
  27.9 1.4 %collective-permute-start.9 = (f32[16,1024]{1,0:T(8,128)S(1)}, f32[16,1024]{1,0:T(8,128)S(1)}, u32[]{:S(2)}, u32[]{:S(2)}) collective-permute-start(f32[16,1024]{1,0:T(8,128)S(1)} %get-tuple-element.52), channel_id=1, source_target_pairs={{0,4},{4,0},{8,12},{12,8},{16,20},{20,16},{24,28},{28,24},{1,5},{5... | collective-permute-start | bytes 196616 | tf_op jit(solution)/shard_map/ppermute | solution.py:162
  33.5 1.5 %collective-permute-start.10 = (f32[32,1024]{1,0:T(8,128)S(1)}, f32[32,1024]{1,0:T(8,128)S(1)}, u32[]{:S(2)}, u32[]{:S(2)}) collective-permute-start(f32[32,1024]{1,0:T(8,128)S(1)} %get-tuple-element.39), channel_id=1, source_target_pairs={{0,4},{4,0},{8,12},{12,8},{16,20},{20,16},{24,28},{28,24},{1,5},{5... | collective-permute-start | bytes 393224 | tf_op jit(solution)/shard_map/ppermute | solution.py:162
  35.0 5.0 %collective-permute-start.12 = (f32[32,1024]{1,0:T(8,128)S(1)}, f32[32,1024]{1,0:T(8,128)S(1)}, u32[]{:S(2)}, u32[]{:S(2)}) collective-permute-start(f32[32,1024]{1,0:T(8,128)S(1)} %add.92), channel_id=1, source_target_pairs={{0,16},{1,17},{2,18},{3,19},{4,6},{5,7},{6,4},{7,5},{8,24},{9,25},... | collective-permute-start | bytes 393224 | tf_op jit(solution)/shard_map/ppermute | solution.py:174
  35.6 5.0 %collective-permute-start.13 = (f32[32,1024]{1,0:T(8,128)S(1)}, f32[32,1024]{1,0:T(8,128)S(1)}, u32[]{:S(2)}, u32[]{:S(2)}) collective-permute-start(f32[32,1024]{1,0:T(8,128)S(1)} %add.92), channel_id=1, source_target_pairs={{0,8},{1,9},{2,10},{3,11},{4,5},{5,4},{6,7},{7,6},{8,0},{9,1},{10,... | collective-permute-start | bytes 393224 | tf_op jit(solution)/shard_map/ppermute | solution.py:174
  36.9 6.0 %collective-permute-start.11 = (f32[32,1024]{1,0:T(8,128)S(1)}, f32[32,1024]{1,0:T(8,128)S(1)}, u32[]{:S(2)}, u32[]{:S(2)}) collective-permute-start(f32[32,1024]{1,0:T(8,128)S(1)} %add.92), channel_id=1, source_target_pairs={{0,24},{1,25},{2,26},{3,27},{4,7},{5,6},{6,5},{7,4},{8,16},{9,17},... | collective-permute-start | bytes 393224 | tf_op jit(solution)/shard_map/ppermute | solution.py:174
  43.0 1.9 %collective-permute-start.14 = (f32[16,1024]{1,0:T(8,128)S(1)}, f32[16,1024]{1,0:T(8,128)S(1)}, u32[]{:S(2)}, u32[]{:S(2)}) collective-permute-start(f32[16,1024]{1,0:T(8,128)S(1)} %get-tuple-element.50), channel_id=1, source_target_pairs={{0,4},{4,0},{8,12},{12,8},{16,20},{20,16},{24,28},{28,24},{1,5},{5... | collective-permute-start | bytes 196616 | tf_op jit(solution)/shard_map/ppermute | solution.py:162
  48.9 1.4 %collective-permute-start.15 = (f32[32,1024]{1,0:T(8,128)S(1)}, f32[32,1024]{1,0:T(8,128)S(1)}, u32[]{:S(2)}, u32[]{:S(2)}) collective-permute-start(f32[32,1024]{1,0:T(8,128)S(1)} %get-tuple-element.43), channel_id=1, source_target_pairs={{0,4},{4,0},{8,12},{12,8},{16,20},{20,16},{24,28},{28,24},{1,5},{5... | collective-permute-start | bytes 393224 | tf_op jit(solution)/shard_map/ppermute | solution.py:162
  50.4 5.0 %collective-permute-start.17 = (f32[32,1024]{1,0:T(8,128)S(1)}, f32[32,1024]{1,0:T(8,128)S(1)}, u32[]{:S(2)}, u32[]{:S(2)}) collective-permute-start(f32[32,1024]{1,0:T(8,128)S(1)} %add.97), channel_id=1, source_target_pairs={{0,16},{1,17},{2,18},{3,19},{4,6},{5,7},{6,4},{7,5},{8,24},{9,25},... | collective-permute-start | bytes 393224 | tf_op jit(solution)/shard_map/ppermute | solution.py:174
  50.9 5.0 %collective-permute-start.18 = (f32[32,1024]{1,0:T(8,128)S(1)}, f32[32,1024]{1,0:T(8,128)S(1)}, u32[]{:S(2)}, u32[]{:S(2)}) collective-permute-start(f32[32,1024]{1,0:T(8,128)S(1)} %add.97), channel_id=1, source_target_pairs={{0,8},{1,9},{2,10},{3,11},{4,5},{5,4},{6,7},{7,6},{8,0},{9,1},{10,... | collective-permute-start | bytes 393224 | tf_op jit(solution)/shard_map/ppermute | solution.py:174
  52.0 6.3 %collective-permute-start.16 = (f32[32,1024]{1,0:T(8,128)S(1)}, f32[32,1024]{1,0:T(8,128)S(1)}, u32[]{:S(2)}, u32[]{:S(2)}) collective-permute-start(f32[32,1024]{1,0:T(8,128)S(1)} %add.97), channel_id=1, source_target_pairs={{0,24},{1,25},{2,26},{3,27},{4,7},{5,6},{6,5},{7,4},{8,16},{9,17},... | collective-permute-start | bytes 393224 | tf_op jit(solution)/shard_map/ppermute | solution.py:174
  58.4 1.7 %collective-permute-start.19 = (f32[16,1024]{1,0:T(8,128)S(1)}, f32[16,1024]{1,0:T(8,128)S(1)}, u32[]{:S(2)}, u32[]{:S(2)}) collective-permute-start(f32[16,1024]{1,0:T(8,128)S(1)} %get-tuple-element.48), channel_id=1, source_target_pairs={{0,4},{4,0},{8,12},{12,8},{16,20},{20,16},{24,28},{28,24},{1,5},{5... | collective-permute-start | bytes 196616 | tf_op jit(solution)/shard_map/ppermute | solution.py:162
  64.1 1.4 %collective-permute-start.20 = (f32[32,1024]{1,0:T(8,128)S(1)}, f32[32,1024]{1,0:T(8,128)S(1)}, u32[]{:S(2)}, u32[]{:S(2)}) collective-permute-start(f32[32,1024]{1,0:T(8,128)S(1)} %get-tuple-element.47), channel_id=1, source_target_pairs={{0,4},{4,0},{8,12},{12,8},{16,20},{20,16},{24,28},{28,24},{1,5},{5... | collective-permute-start | bytes 393224 | tf_op jit(solution)/shard_map/ppermute | solution.py:162
  65.6 4.0 %collective-permute-start.23 = (f32[32,256]{1,0:T(8,128)S(1)}, f32[32,256]{1,0:T(8,128)S(1)}, u32[]{:S(2)}, u32[]{:S(2)}) collective-permute-start(f32[32,256]{1,0:T(8,128)S(1)} %get-tuple-element.55), channel_id=1, source_target_pairs={{0,8},{1,9},{2,10},{3,11},{4,5},{5,4},{6,7},{7,6},{8,0},{9,1},{10,... | collective-permute-start | bytes 98312 | tf_op jit(solution)/shard_map/ppermute | solution.py:174
  66.2 3.9 %collective-permute-start.22 = (f32[32,256]{1,0:T(8,128)S(1)}, f32[32,256]{1,0:T(8,128)S(1)}, u32[]{:S(2)}, u32[]{:S(2)}) collective-permute-start(f32[32,256]{1,0:T(8,128)S(1)} %get-tuple-element.56), channel_id=1, source_target_pairs={{0,16},{1,17},{2,18},{3,19},{4,6},{5,7},{6,4},{7,5},{8,24},{9,25},... | collective-permute-start | bytes 98312 | tf_op jit(solution)/shard_map/ppermute | solution.py:174
  67.3 4.8 %collective-permute-start.21 = (f32[32,256]{1,0:T(8,128)S(1)}, f32[32,256]{1,0:T(8,128)S(1)}, u32[]{:S(2)}, u32[]{:S(2)}) collective-permute-start(f32[32,256]{1,0:T(8,128)S(1)} %get-tuple-element.54), channel_id=1, source_target_pairs={{0,24},{1,25},{2,26},{3,27},{4,7},{5,6},{6,5},{7,4},{8,16},{9,17},... | collective-permute-start | bytes 98312 | tf_op jit(solution)/shard_map/ppermute | solution.py:174
  72.2 1.4 %collective-permute-start.24 = (f32[32,128]{1,0:T(8,128)S(1)}, f32[32,128]{1,0:T(8,128)S(1)}, u32[]{:S(2)}, u32[]{:S(2)}) collective-permute-start(f32[32,128]{1,0:T(8,128)S(1)} %get-tuple-element.63), channel_id=1, source_target_pairs={{0,4},{4,0},{8,12},{12,8},{16,20},{20,16},{24,28},{28,24},{1,5},{5... | collective-permute-start | bytes 49160 | tf_op jit(solution)/shard_map/ppermute | solution.py:162

commit v3 on v2

--- a/solution.py
+++ b/solution.py
@@ -12,7 +12,6 @@
 ROWS = 256
 COLS = 256
 NT = (((1,), (1,)), ((), ()))
-SMEM = pl.BlockSpec(memory_space=pltpu.SMEM)
 VMEM = pl.BlockSpec(memory_space=pltpu.VMEM)
 HBM = pl.BlockSpec(memory_space=pltpu.HBM)
 
@@ -70,8 +69,8 @@
     )(genotypes)
 
 
-def em_kernel(first, snps_all, core_ref, g_ref, q_ref, keep_ref, got_ref, mine_ref, send_ref, q_out, p_out, qs_ref, ql_ref, ps_ref, pr_ref, dh_ref, dl_ref, th_ref, tl_ref):
-    core = core_ref[0]
+def em_kernel(first, snps_all, g_ref, q_ref, keep_ref, got_ref, mine_ref, send_ref, q_out, p_out, qs_ref, ql_ref, ps_ref, pr_ref, dh_ref, dl_ref, th_ref, tl_ref):
+    core = lax.rem(lax.axis_index("ind"), 2)
     keep, got = keep_ref[...], got_ref[...]
     p = jnp.where(core == 0, keep, got)
     a_sum = jnp.where(core == 0, got, keep)
@@ -87,34 +86,43 @@
     ql_ref[...] = jnp.concatenate([q1, q2, q1, q2, q3, q1], axis=0).T
     pr_ref[...] = jnp.concatenate([p1, p1, p2, p2, p1, p3], axis=0)
 
-    def ratios(b):
-        at = slice(b * ROWS, (b + 1) * ROWS)
-        slot = b % 2
-        for c in range(0, snps, COLS):
-            to = slice(c, c + COLS)
-            e = mxu(ql_ref[at, :], pr_ref[:, to])
-            half = g_ref[at, to]
-            d = e * (1.0 - e)
-            inv = pltpu.reciprocal(d, approx=True)
-            inv = inv * (2.0 - d * inv)
-            diff = (half - e) * inv
-            two = ((1.0 - half) * e) * inv
-            dh_ref[slot, :, to], dl_ref[slot, :, to] = split2(diff)
-            th_ref[slot, :, to], tl_ref[slot, :, to] = split2(two)
-
-    pd = pt = 0.0
-    blocks = individuals // ROWS
-    for b in range(blocks + 1):
-        if b < blocks:
-            ratios(b)
-        if b > 0:
-            at = slice((b - 1) * ROWS, b * ROWS)
-            slot = (b - 1) % 2
+    def ratios(t):
+        at = slice(t // across * ROWS, (t // across + 1) * ROWS)
+        to = slice(t % across * COLS, (t % across + 1) * COLS)
+        slot = t % 2
+        e = mxu(ql_ref[at, :], pr_ref[:, to])
+        half = g_ref[at, to]
+        d = e * (1.0 - e)
+        inv = pltpu.reciprocal(d, approx=True)
+        inv = inv * (2.0 - d * inv)
+        diff = (half - e) * inv
+        two = ((1.0 - half) * e) * inv
+        dh_ref[slot], dl_ref[slot] = split2(diff)
+        th_ref[slot], tl_ref[slot] = split2(two)
+
+    across = snps // COLS
+    tiles = individuals // ROWS * across
+    pd = [0.0] * across
+    pt = [0.0] * across
+    for t in range(tiles + 1):
+        if t < tiles:
+            ratios(t)
+        if t > 0:
+            b, c = divmod(t - 1, across)
+            slot = (t - 1) % 2
+            at = slice(b * ROWS, (b + 1) * ROWS)
+            to = slice(c * COLS, (c + 1) * COLS)
             dh, dl, th, tl = dh_ref[slot], dl_ref[slot], th_ref[slot], tl_ref[slot]
-            mine_ref[k:, at] = fold3(mxu(ps_ref[...], dh, NT) + mxu(ps_ref[...], dl, NT))
+            ps = ps_ref[:, to]
+            part = fold3(mxu(ps, dh, NT)) + mxu(ps[:k], dl, NT)
+            a = part if c == 0 else a + part
+            if c == across - 1:
+                mine_ref[k:, at] = a
             qb = qs_ref[:, at]
-            pd = pd + fold3(mxu(qb, dh) + mxu(qb, dl))
-            pt = pt + fold3(mxu(qb, th) + mxu(qb, tl))
+            pd[c] = pd[c] + (fold3(mxu(qb, dh)) + mxu(qb[:k], dl))
+            pt[c] = pt[c] + (fold3(mxu(qb, th)) + mxu(qb[:k], tl))
+    pd = jnp.concatenate(pd, axis=1)
+    pt = jnp.concatenate(pt, axis=1)
     a = mine_ref[k:, :]
     one = pd + pt
 
@@ -132,7 +140,7 @@
         mine_ref[:k] = jnp.zeros_like(a)
 
 
-def em_step(first, snps_all, core, half, q, keep, got):
+def em_step(first, snps_all, half, q, keep, got):
     individuals, snps = half.shape
     k = q.shape[0]
     f32, bf16 = jnp.float32, jnp.bfloat16
@@ -144,7 +152,7 @@
             jax.ShapeDtypeStruct((k, individuals), f32),
             jax.ShapeDtypeStruct((k, snps), f32),
         ),
-        in_specs=[SMEM] + [VMEM] * 4,
+        in_specs=[VMEM] * 4,
         out_specs=(VMEM,) * 4,
         scratch_shapes=[
             pltpu.VMEM((3 * k, individuals), bf16),
@@ -152,10 +160,10 @@
             pltpu.VMEM((3 * k, snps), bf16),
             pltpu.VMEM((6 * k, snps), bf16),
         ]
-        + [pltpu.VMEM((2, ROWS, snps), bf16)] * 4,
+        + [pltpu.VMEM((2, ROWS, COLS), bf16)] * 4,
         compiler_params=pltpu.CompilerParams(vmem_limit_bytes=32 * 1024 * 1024),
         cost_estimate=pl.CostEstimate(flops=2 * 20 * k * individuals * snps, bytes_accessed=4 * individuals * snps, transcendentals=individuals * snps),
-    )(core, half, q, keep, got)
+    )(half, q, keep, got)
 
 
 def swap_cores(x, n_ind):
@@ -194,9 +202,8 @@
     return lax.dynamic_update_slice_in_dim(full, shard, index * width, axis=1)
 
 
-def gather_small(core_id, index, genotypes, ancestry, freqs, n_ind, n_snp):
+def gather_small(first_core, index, genotypes, ancestry, freqs, n_ind, n_snp):
     k = ancestry.shape[0]
-    first_core = core_id[0] == 0
     none = jnp.zeros_like(freqs)
     recv = swap_cores(jnp.where(first_core, ancestry, jnp.concatenate([none, freqs], axis=1)), n_ind)
     zeros = jnp.zeros_like(ancestry)
@@ -217,22 +224,23 @@
     return half, keep, swap_cores(full[:k], n_ind)
 
 
-def close_kernel(snps_all, at_ref, q_ref, p_ref, keep_ref, got_ref, q_out, p_out):
-    core = at_ref[0]
+def close_kernel(snps_all, q_ref, p_ref, keep_ref, got_ref, q_out, p_out):
+    ind = lax.axis_index("ind")
+    core = lax.rem(ind, 2)
     keep, got = keep_ref[...], got_ref[...]
     sums = jnp.where(core == 0, keep, got)
     a_sum = jnp.where(core == 0, got, keep)
     k, wide = q_out.shape
     width = p_out.shape[1]
     a_sum = jnp.concatenate([a_sum[:k], a_sum[k:]], axis=1)
-    q = q_ref[:, pl.ds(pl.multiple_of(at_ref[1], 128), wide)]
-    p = p_ref[:, pl.ds(pl.multiple_of(at_ref[2], 128), width)]
+    q = q_ref[:, pl.ds(pl.multiple_of(lax.axis_index("snp") * wide, 128), wide)]
+    p = p_ref[:, pl.ds(pl.multiple_of(ind * width, 128), width)]
     q_out[...] = new_ancestry(q, a_sum, snps_all)
     up = p * sums[:k]
     p_out[...] = up / (up + (1.0 - p) * sums[k:])
 
 
-def finish_small(snps_all, core_id, index, at, mine, send, q, p, n_ind, n_snp, shapes):
+def finish_small(snps_all, first_core, index, mine, send, q, p, n_ind, n_snp, shapes):
     k = q.shape[0]
     buf = mine + swap_cores(send, n_ind)
     wide = shapes[0][1]
@@ -242,17 +250,16 @@
     total = chunk(0)
     for part in parts[::-1]:
         total = total + part
-    first_core = core_id[0] == 0
     fold = lambda x: jnp.concatenate([x[:, :half], x[:, half:]])
     keep = jnp.where(first_core, total[:, :half], fold(total[k:]))
     got = swap_cores(jnp.where(first_core, total[:, half:], fold(total[:k])), n_ind)
     return pl.pallas_call(
         functools.partial(close_kernel, snps_all),
         out_shape=tuple(jax.ShapeDtypeStruct(s, jnp.float32) for s in shapes),
-        in_specs=[SMEM] + [VMEM] * 4,
+        in_specs=[VMEM] * 4,
         out_specs=(VMEM, VMEM),
         compiler_params=pltpu.CompilerParams(vmem_limit_bytes=1024 * 1024),
-    )(at, q, p, keep, got)
+    )(q, p, keep, got)
 
 
 def body(genotypes, ancestry, freqs):
@@ -263,12 +270,10 @@
     index = jnp.where(first_core, ind // 2, snp)
     k = ancestry.shape[0]
     snps_all = genotypes.shape[1] * n_snp
-    core_id = core.reshape(1).astype(jnp.int32)
-    at = jnp.stack([core, snp * ancestry.shape[1], ind * freqs.shape[1]]).astype(jnp.int32)
     small = n_ind == 2 * n_snp and ancestry.shape[1] == 2 * freqs.shape[1] and freqs.shape[1] % 128 == 0
 
     if small:
-        half, keep, got = gather_small(core_id, index, genotypes, ancestry, freqs, n_ind, n_snp)
+        half, keep, got = gather_small(first_core, index, genotypes, ancestry, freqs, n_ind, n_snp)
         q = keep
     else:
         half = load_counts(genotypes)
@@ -281,9 +286,9 @@
         keep = jnp.where(first_core, buf[:k], buf[k:])
         got = swap_cores(buf[:k], n_ind)
     for step in range(ITERS):
-        mine, send, q, p = em_step(step == 0, snps_all, core_id, half, q, keep, got)
+        mine, send, q, p = em_step(step == 0, snps_all, half, q, keep, got)
         if small and step == ITERS - 1:
-            return finish_small(snps_all, core_id, index, at, mine, send, q, p, n_ind, n_snp, (ancestry.shape, freqs.shape))
+            return finish_small(snps_all, first_core, index, mine, send, q, p, n_ind, n_snp, (ancestry.shape, freqs.shape))
         buf = sum_groups(mine + swap_cores(send, n_ind), n_ind, n_snp)
         up = p * buf[:k]
         p_new = up / (up + (1.0 - p) * buf[k:])

time: 75.3 us -> 71.2 us (0.946)
  Pallas kernels: 18.1 us -> 14 us
  starting transfers between devices: 24.4 us -> 25.9 us
  waiting for transfers between devices: 27.4 us -> 26.1 us
    pallas_call x4, Pallas kernels: 16.3 us -> 12.8 us  [em_step(): pl.pallas_call(functools.partial(em_kernel, first, snps_all), out_shape=(...]
    ppermute x15, waiting for transfers between devices: 19 us -> 17.3 us  [exchange(): return lax.ppermute(x, AXES, pairs) if pairs else None]
    ppermute x10, starting transfers between devices: 5.78 us -> 7.2 us  [swap_cores(): return lax.ppermute(x, 'ind', [(i, i ^ 1) for i in range(n_ind)])]
where the time goes in v3:
time: 71.2 us; the launch traced here: 70.8 us
  waiting for transfers between devices  26.1 us (37%)
  starting transfers between devices  25.9 us (36%)
  Pallas kernels  14 us (20%)
  local copies, waits for them, and re-layouts  2.21 us (3%)
  other arithmetic  1.78 us (2%)
  between operations  0.8 us (1%)
    ppermute x15, starting transfers between devices, exchange(): return lax.ppermute(x, AXES, pairs) if pairs else None  18.7 us
    ppermute x15, waiting for transfers between devices, exchange(): return lax.ppermute(x, AXES, pairs) if pairs else None  17.3 us
    pallas_call x4, Pallas kernels, em_step(): pl.pallas_call(functools.partial(em_kernel, first, snps_all), out_shape=(...  12.8 us
    ppermute x10, waiting for transfers between devices, swap_cores(): return lax.ppermute(x, 'ind', [(i, i ^ 1) for i in range(n_ind)])  8.82 us
    ppermute x10, starting transfers between devices, swap_cores(): return lax.ppermute(x, 'ind', [(i, i ^ 1) for i in range(n_ind)])  7.2 us
    unnamed x2, local copies, waits for them, and re-layouts  2.19 us
  transfers between devices with their start and end apart: 25, of which 23 were waited for; matrix products, arithmetic and copies ran while one was open for 1% of the time, Pallas kernels for 1%

profile of v3, /device:TPU:0, one launch (start us, length us, event | category | flops | bytes accessed | tf_op | source)
XLA Modules:
  0.0 70.8 jit_solution(9994498558445240805)
XLA Ops:
  2.7 2.9 %collective-permute-start.1 = (f32[32,256]{1,0:T(8,128)S(1)}, f32[32,256]{1,0:T(8,128)S(1)}, u32[]{:S(2)}, u32[]{:S(2)}) collective-permute-start(f32[32,256]{1,0:T(8,128)S(1)} %pad_maximum_fusion.1), channel_id=1, source_target_pairs={{0,8},{1,9},{2,10},{3,11},{4,5},{5,4},{6,7},{7,6},{8,0},{9,1},{10,... | collective-permute-start | bytes 98312 | tf_op jit(solution)/shard_map/ppermute | solution.py:182
  5.6 1.5 %collective-permute-start.2 = (f32[32,256]{1,0:T(8,128)S(1)}, f32[32,256]{1,0:T(8,128)S(1)}, u32[]{:S(2)}, u32[]{:S(2)}) collective-permute-start(f32[32,256]{1,0:T(8,128)S(1)} %pad_maximum_fusion.1), channel_id=1, source_target_pairs={{0,16},{1,17},{2,18},{3,19},{4,6},{5,7},{6,4},{7,5},{8,24},{9,25},... | collective-permute-start | bytes 98312 | tf_op jit(solution)/shard_map/ppermute | solution.py:182
  7.1 2.2 %copy-done = s32[1024,1024]{1,0:T(8,128)S(1)} copy-done((s32[1024,1024]{1,0:T(8,128)S(1)}, s32[1024,1024]{1,0:T(8,128)}, u32[]{:S(2)}) %copy-start) | copy-done | bytes 4194328
  10.0 1.9 %collective-permute-done.3 = f32[32,256]{1,0:T(8,128)S(1)} collective-permute-done((f32[32,256]{1,0:T(8,128)S(1)}, f32[32,256]{1,0:T(8,128)S(1)}, u32[]{:S(2)}, u32[]{:S(2)}) %collective-permute-start.3) | collective-permute-done | bytes 32800 | tf_op jit(solution)/shard_map/ppermute | solution.py:182
  13.4 3.1 %shard_map.51 = (f32[32,1024]{1,0:T(8,128)S(1)}, f32[32,1024]{1,0:T(8,128)S(1)}, f32[16,1024]{1,0:T(8,128)S(1)}, f32[16,1024]{1,0:T(8,128)S(1)}) custom-call(f32[1024,1024]{1,0:T(8,128)S(1)} %shard_map.50.g_ref, f32[16,1024]{1,0:T(8,128)S(1)} %get-tuple-element.58.q_ref.keep_ref, f32[16,1024]{1,0:T(8,128)S(1)} %get-tuple-element.58.q_ref.keep_ref, ...), custom_call_target="tpu_custom_call" | custom-call | flops 671088640 | bytes 4194304 | tf_op jit(solution)/shard_map/pallas_call | solution.py:147
  17.1 1.0 %collective-permute-done.5 = f32[32,1024]{1,0:T(8,128)S(1)} collective-permute-done((f32[32,1024]{1,0:T(8,128)S(1)}, f32[32,1024]{1,0:T(8,128)S(1)}, u32[]{:S(2)}, u32[]{:S(2)}) %collective-permute-start.5) | collective-permute-done | bytes 131104 | tf_op jit(solution)/shard_map/ppermute | solution.py:170
  18.1 2.5 %collective-permute-start.6 = (f32[32,1024]{1,0:T(8,128)S(1)}, f32[32,1024]{1,0:T(8,128)S(1)}, u32[]{:S(2)}, u32[]{:S(2)}) collective-permute-start(f32[32,1024]{1,0:T(8,128)S(1)} %add.87), channel_id=1, source_target_pairs={{0,24},{1,25},{2,26},{3,27},{4,7},{5,6},{6,5},{7,4},{8,16},{9,17},... | collective-permute-start | bytes 393224 | tf_op jit(solution)/shard_map/ppermute | solution.py:182
  21.6 2.4 %collective-permute-done.6 = f32[32,1024]{1,0:T(8,128)S(1)} collective-permute-done((f32[32,1024]{1,0:T(8,128)S(1)}, f32[32,1024]{1,0:T(8,128)S(1)}, u32[]{:S(2)}, u32[]{:S(2)}) %collective-permute-start.6) | collective-permute-done | bytes 131104 | tf_op jit(solution)/shard_map/ppermute | solution.py:182
  24.0 1.5 %collective-permute-done.7 = f32[32,1024]{1,0:T(8,128)S(1)} collective-permute-done((f32[32,1024]{1,0:T(8,128)S(1)}, f32[32,1024]{1,0:T(8,128)S(1)}, u32[]{:S(2)}, u32[]{:S(2)}) %collective-permute-start.7) | collective-permute-done | bytes 131104 | tf_op jit(solution)/shard_map/ppermute | solution.py:182
  26.1 1.2 %collective-permute-start.9 = (f32[16,1024]{1,0:T(8,128)S(1)}, f32[16,1024]{1,0:T(8,128)S(1)}, u32[]{:S(2)}, u32[]{:S(2)}) collective-permute-start(f32[16,1024]{1,0:T(8,128)S(1)} %get-tuple-element.52), channel_id=1, source_target_pairs={{0,4},{4,0},{8,12},{12,8},{16,20},{20,16},{24,28},{28,24},{1,5},{5... | collective-permute-start | bytes 196616 | tf_op jit(solution)/shard_map/ppermute | solution.py:170
  27.3 0.9 %collective-permute-done.9.got_ref = f32[16,1024]{1,0:T(8,128)S(1)} collective-permute-done((f32[16,1024]{1,0:T(8,128)S(1)}, f32[16,1024]{1,0:T(8,128)S(1)}, u32[]{:S(2)}, u32[]{:S(2)}) %collective-permute-start.9) | collective-permute-done | bytes 65568 | tf_op jit(solution)/shard_map/ppermute | solution.py:170
  28.2 3.2 %shard_map.52 = (f32[32,1024]{1,0:T(8,128)S(1)}, f32[32,1024]{1,0:T(8,128)S(1)}, f32[16,1024]{1,0:T(8,128)S(1)}, f32[16,1024]{1,0:T(8,128)S(1)}) custom-call(f32[1024,1024]{1,0:T(8,128)S(1)} %shard_map.50.g_ref, f32[16,1024]{1,0:T(8,128)S(1)} %get-tuple-element.32.q_ref, f32[16,1024]{1,0:T(8,128)S(1)} %get-tuple-element.53.keep_ref, ...), custom_call_target="tpu_custom_call" | custom-call | flops 671088640 | bytes 4194304 | tf_op jit(solution)/shard_map/pallas_call | solution.py:147
  31.9 1.0 %collective-permute-done.10 = f32[32,1024]{1,0:T(8,128)S(1)} collective-permute-done((f32[32,1024]{1,0:T(8,128)S(1)}, f32[32,1024]{1,0:T(8,128)S(1)}, u32[]{:S(2)}, u32[]{:S(2)}) %collective-permute-start.10) | collective-permute-done | bytes 131104 | tf_op jit(solution)/shard_map/ppermute | solution.py:170
  32.9 2.2 %collective-permute-start.11 = (f32[32,1024]{1,0:T(8,128)S(1)}, f32[32,1024]{1,0:T(8,128)S(1)}, u32[]{:S(2)}, u32[]{:S(2)}) collective-permute-start(f32[32,1024]{1,0:T(8,128)S(1)} %add.92), channel_id=1, source_target_pairs={{0,24},{1,25},{2,26},{3,27},{4,7},{5,6},{6,5},{7,4},{8,16},{9,17},... | collective-permute-start | bytes 393224 | tf_op jit(solution)/shard_map/ppermute | solution.py:182
  36.4 2.4 %collective-permute-done.11 = f32[32,1024]{1,0:T(8,128)S(1)} collective-permute-done((f32[32,1024]{1,0:T(8,128)S(1)}, f32[32,1024]{1,0:T(8,128)S(1)}, u32[]{:S(2)}, u32[]{:S(2)}) %collective-permute-start.11) | collective-permute-done | bytes 131104 | tf_op jit(solution)/shard_map/ppermute | solution.py:182
  38.8 1.4 %collective-permute-done.12 = f32[32,1024]{1,0:T(8,128)S(1)} collective-permute-done((f32[32,1024]{1,0:T(8,128)S(1)}, f32[32,1024]{1,0:T(8,128)S(1)}, u32[]{:S(2)}, u32[]{:S(2)}) %collective-permute-start.12) | collective-permute-done | bytes 131104 | tf_op jit(solution)/shard_map/ppermute | solution.py:182
  40.7 1.5 %collective-permute-start.14 = (f32[16,1024]{1,0:T(8,128)S(1)}, f32[16,1024]{1,0:T(8,128)S(1)}, u32[]{:S(2)}, u32[]{:S(2)}) collective-permute-start(f32[16,1024]{1,0:T(8,128)S(1)} %get-tuple-element.50), channel_id=1, source_target_pairs={{0,4},{4,0},{8,12},{12,8},{16,20},{20,16},{24,28},{28,24},{1,5},{5... | collective-permute-start | bytes 196616 | tf_op jit(solution)/shard_map/ppermute | solution.py:170
  42.2 0.9 %collective-permute-done.14.got_ref = f32[16,1024]{1,0:T(8,128)S(1)} collective-permute-done((f32[16,1024]{1,0:T(8,128)S(1)}, f32[16,1024]{1,0:T(8,128)S(1)}, u32[]{:S(2)}, u32[]{:S(2)}) %collective-permute-start.14) | collective-permute-done | bytes 65568 | tf_op jit(solution)/shard_map/ppermute | solution.py:170
  43.1 3.3 %shard_map.53 = (f32[32,1024]{1,0:T(8,128)S(1)}, f32[32,1024]{1,0:T(8,128)S(1)}, f32[16,1024]{1,0:T(8,128)S(1)}, f32[16,1024]{1,0:T(8,128)S(1)}) custom-call(f32[1024,1024]{1,0:T(8,128)S(1)} %shard_map.50.g_ref, f32[16,1024]{1,0:T(8,128)S(1)} %get-tuple-element.36.q_ref, f32[16,1024]{1,0:T(8,128)S(1)} %get-tuple-element.51.keep_ref, ...), custom_call_target="tpu_custom_call" | custom-call | flops 671088640 | bytes 4194304 | tf_op jit(solution)/shard_map/pallas_call | solution.py:147
  46.9 1.0 %collective-permute-done.15 = f32[32,1024]{1,0:T(8,128)S(1)} collective-permute-done((f32[32,1024]{1,0:T(8,128)S(1)}, f32[32,1024]{1,0:T(8,128)S(1)}, u32[]{:S(2)}, u32[]{:S(2)}) %collective-permute-start.15) | collective-permute-done | bytes 131104 | tf_op jit(solution)/shard_map/ppermute | solution.py:170
  47.9 2.0 %collective-permute-start.16 = (f32[32,1024]{1,0:T(8,128)S(1)}, f32[32,1024]{1,0:T(8,128)S(1)}, u32[]{:S(2)}, u32[]{:S(2)}) collective-permute-start(f32[32,1024]{1,0:T(8,128)S(1)} %add.97), channel_id=1, source_target_pairs={{0,24},{1,25},{2,26},{3,27},{4,7},{5,6},{6,5},{7,4},{8,16},{9,17},... | collective-permute-start | bytes 393224 | tf_op jit(solution)/shard_map/ppermute | solution.py:182
  50.4 1.1 %collective-permute-start.18 = (f32[32,1024]{1,0:T(8,128)S(1)}, f32[32,1024]{1,0:T(8,128)S(1)}, u32[]{:S(2)}, u32[]{:S(2)}) collective-permute-start(f32[32,1024]{1,0:T(8,128)S(1)} %add.97), channel_id=1, source_target_pairs={{0,8},{1,9},{2,10},{3,11},{4,5},{5,4},{6,7},{7,6},{8,0},{9,1},{10,... | collective-permute-start | bytes 393224 | tf_op jit(solution)/shard_map/ppermute | solution.py:182
  51.4 2.4 %collective-permute-done.16 = f32[32,1024]{1,0:T(8,128)S(1)} collective-permute-done((f32[32,1024]{1,0:T(8,128)S(1)}, f32[32,1024]{1,0:T(8,128)S(1)}, u32[]{:S(2)}, u32[]{:S(2)}) %collective-permute-start.16) | collective-permute-done | bytes 131104 | tf_op jit(solution)/shard_map/ppermute | solution.py:182
  53.9 1.4 %collective-permute-done.17 = f32[32,1024]{1,0:T(8,128)S(1)} collective-permute-done((f32[32,1024]{1,0:T(8,128)S(1)}, f32[32,1024]{1,0:T(8,128)S(1)}, u32[]{:S(2)}, u32[]{:S(2)}) %collective-permute-start.17) | collective-permute-done | bytes 131104 | tf_op jit(solution)/shard_map/ppermute | solution.py:182
  55.4 1.5 %collective-permute-start.19 = (f32[16,1024]{1,0:T(8,128)S(1)}, f32[16,1024]{1,0:T(8,128)S(1)}, u32[]{:S(2)}, u32[]{:S(2)}) collective-permute-start(f32[16,1024]{1,0:T(8,128)S(1)} %get-tuple-element.48), channel_id=1, source_target_pairs={{0,4},{4,0},{8,12},{12,8},{16,20},{20,16},{24,28},{28,24},{1,5},{5... | collective-permute-start | bytes 196616 | tf_op jit(solution)/shard_map/ppermute | solution.py:170
  57.8 3.2 %shard_map.54 = (f32[32,1024]{1,0:T(8,128)S(1)}, f32[32,1024]{1,0:T(8,128)S(1)}, f32[16,1024]{1,0:T(8,128)S(1)}, f32[16,1024]{1,0:T(8,128)S(1)}) custom-call(f32[1024,1024]{1,0:T(8,128)S(1)} %shard_map.50.g_ref, f32[16,1024]{1,0:T(8,128)S(1)} %get-tuple-element.40.q_ref, f32[16,1024]{1,0:T(8,128)S(1)} %get-tuple-element.49.keep_ref, ...), custom_call_target="tpu_custom_call" | custom-call | flops 671088640 | bytes 4194304 | tf_op jit(solution)/shard_map/pallas_call | solution.py:147
  61.4 1.0 %collective-permute-done.20 = f32[32,1024]{1,0:T(8,128)S(1)} collective-permute-done((f32[32,1024]{1,0:T(8,128)S(1)}, f32[32,1024]{1,0:T(8,128)S(1)}, u32[]{:S(2)}, u32[]{:S(2)}) %collective-permute-start.20) | collective-permute-done | bytes 131104 | tf_op jit(solution)/shard_map/ppermute | solution.py:170
  62.5 2.0 %collective-permute-start.21 = (f32[32,256]{1,0:T(8,128)S(1)}, f32[32,256]{1,0:T(8,128)S(1)}, u32[]{:S(2)}, u32[]{:S(2)}) collective-permute-start(f32[32,256]{1,0:T(8,128)S(1)} %get-tuple-element.54), channel_id=1, source_target_pairs={{0,24},{1,25},{2,26},{3,27},{4,7},{5,6},{6,5},{7,4},{8,16},{9,17},... | collective-permute-start | bytes 98312 | tf_op jit(solution)/shard_map/ppermute | solution.py:182
  65.0 1.1 %collective-permute-start.23 = (f32[32,256]{1,0:T(8,128)S(1)}, f32[32,256]{1,0:T(8,128)S(1)}, u32[]{:S(2)}, u32[]{:S(2)}) collective-permute-start(f32[32,256]{1,0:T(8,128)S(1)} %get-tuple-element.55), channel_id=1, source_target_pairs={{0,8},{1,9},{2,10},{3,11},{4,5},{5,4},{6,7},{7,6},{8,0},{9,1},{10,... | collective-permute-start | bytes 98312 | tf_op jit(solution)/shard_map/ppermute | solution.py:182
  66.0 1.3 %collective-permute-done.21 = f32[32,256]{1,0:T(8,128)S(1)} collective-permute-done((f32[32,256]{1,0:T(8,128)S(1)}, f32[32,256]{1,0:T(8,128)S(1)}, u32[]{:S(2)}, u32[]{:S(2)}) %collective-permute-start.21) | collective-permute-done | bytes 32800 | tf_op jit(solution)/shard_map/ppermute | solution.py:182
  67.3 1.0 %collective-permute-done.22 = f32[32,256]{1,0:T(8,128)S(1)} collective-permute-done((f32[32,256]{1,0:T(8,128)S(1)}, f32[32,256]{1,0:T(8,128)S(1)}, u32[]{:S(2)}, u32[]{:S(2)}) %collective-permute-start.22) | collective-permute-done | bytes 32800 | tf_op jit(solution)/shard_map/ppermute | solution.py:182
  69.0 1.2 %collective-permute-done.24.got_ref = f32[32,128]{1,0:T(8,128)S(1)} collective-permute-done((f32[32,128]{1,0:T(8,128)S(1)}, f32[32,128]{1,0:T(8,128)S(1)}, u32[]{:S(2)}, u32[]{:S(2)}) %collective-permute-start.24) | collective-permute-done | bytes 16416 | tf_op jit(solution)/shard_map/ppermute | solution.py:170
  (47 shorter events, 13.0 us)
Async XLA Ops:
  1.4 1.3 %collective-permute-start = (f32[16,256]{1,0:T(8,128)S(1)}, f32[16,256]{1,0:T(8,128)S(1)}, u32[]{:S(2)}, u32[]{:S(2)}) collective-permute-start(f32[16,256]{1,0:T(8,128)S(1)} %pad_select_fusion.1), channel_id=1, source_target_pairs={{0,4},{4,0},{8,12},{12,8},{16,20},{20,16},{24,28},{28,24},{1,5},{5... | collective-permute-start | bytes 49160 | tf_op jit(solution)/shard_map/ppermute | solution.py:170
  2.7 7.3 %collective-permute-start.1 = (f32[32,256]{1,0:T(8,128)S(1)}, f32[32,256]{1,0:T(8,128)S(1)}, u32[]{:S(2)}, u32[]{:S(2)}) collective-permute-start(f32[32,256]{1,0:T(8,128)S(1)} %pad_maximum_fusion.1), channel_id=1, source_target_pairs={{0,8},{1,9},{2,10},{3,11},{4,5},{5,4},{6,7},{7,6},{8,0},{9,1},{10,... | collective-permute-start | bytes 98312 | tf_op jit(solution)/shard_map/ppermute | solution.py:182
  5.6 4.4 %collective-permute-start.2 = (f32[32,256]{1,0:T(8,128)S(1)}, f32[32,256]{1,0:T(8,128)S(1)}, u32[]{:S(2)}, u32[]{:S(2)}) collective-permute-start(f32[32,256]{1,0:T(8,128)S(1)} %pad_maximum_fusion.1), channel_id=1, source_target_pairs={{0,16},{1,17},{2,18},{3,19},{4,6},{5,7},{6,4},{7,5},{8,24},{9,25},... | collective-permute-start | bytes 98312 | tf_op jit(solution)/shard_map/ppermute | solution.py:182
  7.1 4.8 %collective-permute-start.3 = (f32[32,256]{1,0:T(8,128)S(1)}, f32[32,256]{1,0:T(8,128)S(1)}, u32[]{:S(2)}, u32[]{:S(2)}) collective-permute-start(f32[32,256]{1,0:T(8,128)S(1)} %pad_maximum_fusion.1), channel_id=1, source_target_pairs={{0,24},{1,25},{2,26},{3,27},{4,7},{5,6},{6,5},{7,4},{8,16},{9,17},... | collective-permute-start | bytes 98312 | tf_op jit(solution)/shard_map/ppermute | solution.py:182
  7.1 2.2 %copy-start = (s32[1024,1024]{1,0:T(8,128)S(1)}, s32[1024,1024]{1,0:T(8,128)}, u32[]{:S(2)}) copy-start(s32[1024,1024]{1,0:T(8,128)} %g_hbm) | copy-start | bytes 12582916
  12.0 1.5 %collective-permute-start.4 = (f32[16,1024]{1,0:T(8,128)S(1)}, f32[16,1024]{1,0:T(8,128)S(1)}, u32[]{:S(2)}, u32[]{:S(2)}) collective-permute-start(f32[16,1024]{1,0:T(8,128)S(1)} %get-tuple-element.57), channel_id=1, source_target_pairs={{0,4},{4,0},{8,12},{12,8},{16,20},{20,16},{24,28},{28,24},{1,5},{5... | collective-permute-start | bytes 196616 | tf_op jit(solution)/shard_map/ppermute | solution.py:170
  16.6 1.5 %collective-permute-start.5 = (f32[32,1024]{1,0:T(8,128)S(1)}, f32[32,1024]{1,0:T(8,128)S(1)}, u32[]{:S(2)}, u32[]{:S(2)}) collective-permute-start(f32[32,1024]{1,0:T(8,128)S(1)} %get-tuple-element.35), channel_id=1, source_target_pairs={{0,4},{4,0},{8,12},{12,8},{16,20},{20,16},{24,28},{28,24},{1,5},{5... | collective-permute-start | bytes 393224 | tf_op jit(solution)/shard_map/ppermute | solution.py:170
  18.1 5.9 %collective-permute-start.6 = (f32[32,1024]{1,0:T(8,128)S(1)}, f32[32,1024]{1,0:T(8,128)S(1)}, u32[]{:S(2)}, u32[]{:S(2)}) collective-permute-start(f32[32,1024]{1,0:T(8,128)S(1)} %add.87), channel_id=1, source_target_pairs={{0,24},{1,25},{2,26},{3,27},{4,7},{5,6},{6,5},{7,4},{8,16},{9,17},... | collective-permute-start | bytes 393224 | tf_op jit(solution)/shard_map/ppermute | solution.py:182
  20.6 5.0 %collective-permute-start.7 = (f32[32,1024]{1,0:T(8,128)S(1)}, f32[32,1024]{1,0:T(8,128)S(1)}, u32[]{:S(2)}, u32[]{:S(2)}) collective-permute-start(f32[32,1024]{1,0:T(8,128)S(1)} %add.87), channel_id=1, source_target_pairs={{0,16},{1,17},{2,18},{3,19},{4,6},{5,7},{6,4},{7,5},{8,24},{9,25},... | collective-permute-start | bytes 393224 | tf_op jit(solution)/shard_map/ppermute | solution.py:182
  21.1 5.0 %collective-permute-start.8 = (f32[32,1024]{1,0:T(8,128)S(1)}, f32[32,1024]{1,0:T(8,128)S(1)}, u32[]{:S(2)}, u32[]{:S(2)}) collective-permute-start(f32[32,1024]{1,0:T(8,128)S(1)} %add.87), channel_id=1, source_target_pairs={{0,8},{1,9},{2,10},{3,11},{4,5},{5,4},{6,7},{7,6},{8,0},{9,1},{10,... | collective-permute-start | bytes 393224 | tf_op jit(solution)/shard_map/ppermute | solution.py:182
  26.1 2.1 %collective-permute-start.9 = (f32[16,1024]{1,0:T(8,128)S(1)}, f32[16,1024]{1,0:T(8,128)S(1)}, u32[]{:S(2)}, u32[]{:S(2)}) collective-permute-start(f32[16,1024]{1,0:T(8,128)S(1)} %get-tuple-element.52), channel_id=1, source_target_pairs={{0,4},{4,0},{8,12},{12,8},{16,20},{20,16},{24,28},{28,24},{1,5},{5... | collective-permute-start | bytes 196616 | tf_op jit(solution)/shard_map/ppermute | solution.py:170
  31.4 1.5 %collective-permute-start.10 = (f32[32,1024]{1,0:T(8,128)S(1)}, f32[32,1024]{1,0:T(8,128)S(1)}, u32[]{:S(2)}, u32[]{:S(2)}) collective-permute-start(f32[32,1024]{1,0:T(8,128)S(1)} %get-tuple-element.39), channel_id=1, source_target_pairs={{0,4},{4,0},{8,12},{12,8},{16,20},{20,16},{24,28},{28,24},{1,5},{5... | collective-permute-start | bytes 393224 | tf_op jit(solution)/shard_map/ppermute | solution.py:170
  32.9 5.9 %collective-permute-start.11 = (f32[32,1024]{1,0:T(8,128)S(1)}, f32[32,1024]{1,0:T(8,128)S(1)}, u32[]{:S(2)}, u32[]{:S(2)}) collective-permute-start(f32[32,1024]{1,0:T(8,128)S(1)} %add.92), channel_id=1, source_target_pairs={{0,24},{1,25},{2,26},{3,27},{4,7},{5,6},{6,5},{7,4},{8,16},{9,17},... | collective-permute-start | bytes 393224 | tf_op jit(solution)/shard_map/ppermute | solution.py:182
  35.1 5.1 %collective-permute-start.12 = (f32[32,1024]{1,0:T(8,128)S(1)}, f32[32,1024]{1,0:T(8,128)S(1)}, u32[]{:S(2)}, u32[]{:S(2)}) collective-permute-start(f32[32,1024]{1,0:T(8,128)S(1)} %add.92), channel_id=1, source_target_pairs={{0,16},{1,17},{2,18},{3,19},{4,6},{5,7},{6,4},{7,5},{8,24},{9,25},... | collective-permute-start | bytes 393224 | tf_op jit(solution)/shard_map/ppermute | solution.py:182
  35.6 5.0 %collective-permute-start.13 = (f32[32,1024]{1,0:T(8,128)S(1)}, f32[32,1024]{1,0:T(8,128)S(1)}, u32[]{:S(2)}, u32[]{:S(2)}) collective-permute-start(f32[32,1024]{1,0:T(8,128)S(1)} %add.92), channel_id=1, source_target_pairs={{0,8},{1,9},{2,10},{3,11},{4,5},{5,4},{6,7},{7,6},{8,0},{9,1},{10,... | collective-permute-start | bytes 393224 | tf_op jit(solution)/shard_map/ppermute | solution.py:182
  40.7 2.4 %collective-permute-start.14 = (f32[16,1024]{1,0:T(8,128)S(1)}, f32[16,1024]{1,0:T(8,128)S(1)}, u32[]{:S(2)}, u32[]{:S(2)}) collective-permute-start(f32[16,1024]{1,0:T(8,128)S(1)} %get-tuple-element.50), channel_id=1, source_target_pairs={{0,4},{4,0},{8,12},{12,8},{16,20},{20,16},{24,28},{28,24},{1,5},{5... | collective-permute-start | bytes 196616 | tf_op jit(solution)/shard_map/ppermute | solution.py:170
  46.4 1.5 %collective-permute-start.15 = (f32[32,1024]{1,0:T(8,128)S(1)}, f32[32,1024]{1,0:T(8,128)S(1)}, u32[]{:S(2)}, u32[]{:S(2)}) collective-permute-start(f32[32,1024]{1,0:T(8,128)S(1)} %get-tuple-element.43), channel_id=1, source_target_pairs={{0,4},{4,0},{8,12},{12,8},{16,20},{20,16},{24,28},{28,24},{1,5},{5... | collective-permute-start | bytes 393224 | tf_op jit(solution)/shard_map/ppermute | solution.py:170
  47.9 6.0 %collective-permute-start.16 = (f32[32,1024]{1,0:T(8,128)S(1)}, f32[32,1024]{1,0:T(8,128)S(1)}, u32[]{:S(2)}, u32[]{:S(2)}) collective-permute-start(f32[32,1024]{1,0:T(8,128)S(1)} %add.97), channel_id=1, source_target_pairs={{0,24},{1,25},{2,26},{3,27},{4,7},{5,6},{6,5},{7,4},{8,16},{9,17},... | collective-permute-start | bytes 393224 | tf_op jit(solution)/shard_map/ppermute | solution.py:182
  49.9 5.4 %collective-permute-start.17 = (f32[32,1024]{1,0:T(8,128)S(1)}, f32[32,1024]{1,0:T(8,128)S(1)}, u32[]{:S(2)}, u32[]{:S(2)}) collective-permute-start(f32[32,1024]{1,0:T(8,128)S(1)} %add.97), channel_id=1, source_target_pairs={{0,16},{1,17},{2,18},{3,19},{4,6},{5,7},{6,4},{7,5},{8,24},{9,25},... | collective-permute-start | bytes 393224 | tf_op jit(solution)/shard_map/ppermute | solution.py:182
  50.4 5.0 %collective-permute-start.18 = (f32[32,1024]{1,0:T(8,128)S(1)}, f32[32,1024]{1,0:T(8,128)S(1)}, u32[]{:S(2)}, u32[]{:S(2)}) collective-permute-start(f32[32,1024]{1,0:T(8,128)S(1)} %add.97), channel_id=1, source_target_pairs={{0,8},{1,9},{2,10},{3,11},{4,5},{5,4},{6,7},{7,6},{8,0},{9,1},{10,... | collective-permute-start | bytes 393224 | tf_op jit(solution)/shard_map/ppermute | solution.py:182
  55.4 2.4 %collective-permute-start.19 = (f32[16,1024]{1,0:T(8,128)S(1)}, f32[16,1024]{1,0:T(8,128)S(1)}, u32[]{:S(2)}, u32[]{:S(2)}) collective-permute-start(f32[16,1024]{1,0:T(8,128)S(1)} %get-tuple-element.48), channel_id=1, source_target_pairs={{0,4},{4,0},{8,12},{12,8},{16,20},{20,16},{24,28},{28,24},{1,5},{5... | collective-permute-start | bytes 196616 | tf_op jit(solution)/shard_map/ppermute | solution.py:170
  61.0 1.5 %collective-permute-start.20 = (f32[32,1024]{1,0:T(8,128)S(1)}, f32[32,1024]{1,0:T(8,128)S(1)}, u32[]{:S(2)}, u32[]{:S(2)}) collective-permute-start(f32[32,1024]{1,0:T(8,128)S(1)} %get-tuple-element.47), channel_id=1, source_target_pairs={{0,4},{4,0},{8,12},{12,8},{16,20},{20,16},{24,28},{28,24},{1,5},{5... | collective-permute-start | bytes 393224 | tf_op jit(solution)/shard_map/ppermute | solution.py:170
  62.5 4.9 %collective-permute-start.21 = (f32[32,256]{1,0:T(8,128)S(1)}, f32[32,256]{1,0:T(8,128)S(1)}, u32[]{:S(2)}, u32[]{:S(2)}) collective-permute-start(f32[32,256]{1,0:T(8,128)S(1)} %get-tuple-element.54), channel_id=1, source_target_pairs={{0,24},{1,25},{2,26},{3,27},{4,7},{5,6},{6,5},{7,4},{8,16},{9,17},... | collective-permute-start | bytes 98312 | tf_op jit(solution)/shard_map/ppermute | solution.py:182
  64.4 3.9 %collective-permute-start.22 = (f32[32,256]{1,0:T(8,128)S(1)}, f32[32,256]{1,0:T(8,128)S(1)}, u32[]{:S(2)}, u32[]{:S(2)}) collective-permute-start(f32[32,256]{1,0:T(8,128)S(1)} %get-tuple-element.56), channel_id=1, source_target_pairs={{0,16},{1,17},{2,18},{3,19},{4,6},{5,7},{6,4},{7,5},{8,24},{9,25},... | collective-permute-start | bytes 98312 | tf_op jit(solution)/shard_map/ppermute | solution.py:182
  65.0 3.9 %collective-permute-start.23 = (f32[32,256]{1,0:T(8,128)S(1)}, f32[32,256]{1,0:T(8,128)S(1)}, u32[]{:S(2)}, u32[]{:S(2)}) collective-permute-start(f32[32,256]{1,0:T(8,128)S(1)} %get-tuple-element.55), channel_id=1, source_target_pairs={{0,8},{1,9},{2,10},{3,11},{4,5},{5,4},{6,7},{7,6},{8,0},{9,1},{10,... | collective-permute-start | bytes 98312 | tf_op jit(solution)/shard_map/ppermute | solution.py:182
  68.9 1.2 %collective-permute-start.24 = (f32[32,128]{1,0:T(8,128)S(1)}, f32[32,128]{1,0:T(8,128)S(1)}, u32[]{:S(2)}, u32[]{:S(2)}) collective-permute-start(f32[32,128]{1,0:T(8,128)S(1)} %get-tuple-element.63), channel_id=1, source_target_pairs={{0,4},{4,0},{8,12},{12,8},{16,20},{20,16},{24,28},{28,24},{1,5},{5... | collective-permute-start | bytes 49160 | tf_op jit(solution)/shard_map/ppermute | solution.py:170

commit v4 on v3

--- a/solution.py
+++ b/solution.py
@@ -64,7 +64,7 @@
         in_specs=[HBM],
         out_specs=VMEM,
         scratch_shapes=[pltpu.VMEM((n, rows, snps), jnp.int32), pltpu.SemaphoreType.DMA((n,))],
-        compiler_params=pltpu.CompilerParams(vmem_limit_bytes=16 * 1024 * 1024),
+        compiler_params=pltpu.CompilerParams(vmem_limit_bytes=46 * 1024 * 1024),
         cost_estimate=pl.CostEstimate(flops=individuals * snps, bytes_accessed=4 * individuals * snps, transcendentals=0),
     )(genotypes)
 
@@ -92,11 +92,8 @@
         slot = t % 2
         e = mxu(ql_ref[at, :], pr_ref[:, to])
         half = g_ref[at, to]
-        d = e * (1.0 - e)
-        inv = pltpu.reciprocal(d, approx=True)
-        inv = inv * (2.0 - d * inv)
-        diff = (half - e) * inv
-        two = ((1.0 - half) * e) * inv
+        two = (1.0 - half) * pltpu.reciprocal(1.0 - e)
+        diff = half * pltpu.reciprocal(e) - two
         dh_ref[slot], dl_ref[slot] = split2(diff)
         th_ref[slot], tl_ref[slot] = split2(two)
 
@@ -185,7 +182,7 @@
 def sum_groups(buf, n_ind, n_snp):
     base = 1
     while base < max(n_ind // 2, n_snp):
-        parts = [exchange(buf, m * base, n_ind, n_snp) for m in (1, 2, 3)]
+        parts = [exchange(buf, m * base, n_ind, n_snp) for m in (2, 1, 3)]
         parts = [part for part in parts if part is not None]
         if len(parts) == 3:
             buf = (buf + parts[2]) + (parts[1] + parts[0])

time: 71.2 us -> 70 us (0.983)
  local copies, waits for them, and re-layouts: 2.21 us -> 0.02 us
  Pallas kernels: 14 us -> 14.8 us
    unnamed x2 -> x0, local copies, waits for them, and re-layouts: 2.19 us -> none
    pallas_call x1, Pallas kernels: 0.66 us -> 2.25 us  [load_counts(): pl.pallas_call(load_kernel, out_shape=jax.ShapeDtypeStruct((individuals,...]
    pallas_call x4, Pallas kernels: 12.8 us -> 11.9 us  [em_step(): pl.pallas_call(functools.partial(em_kernel, first, snps_all), out_shape=(...]
  transfers between devices with their start and end apart: 25 -> 25, of which waited for: 23 -> 24; matrix products, arithmetic and copies ran while one was open for 1% -> 1% of each run, Pallas kernels for 1% -> 3%
where the time goes in v4:
time: 70 us; the launch traced here: 69.6 us
  waiting for transfers between devices  26.5 us (38%)
  starting transfers between devices  25.8 us (37%)
  Pallas kernels  14.8 us (21%)
  other arithmetic  1.77 us (3%)
  between operations  0.8 us (1%)
    ppermute x15, starting transfers between devices, exchange(): return lax.ppermute(x, AXES, pairs) if pairs else None  18.7 us
    ppermute x15, waiting for transfers between devices, exchange(): return lax.ppermute(x, AXES, pairs) if pairs else None  17.7 us
    pallas_call x4, Pallas kernels, em_step(): pl.pallas_call(functools.partial(em_kernel, first, snps_all), out_shape=(...  11.9 us
    ppermute x10, waiting for transfers between devices, swap_cores(): return lax.ppermute(x, 'ind', [(i, i ^ 1) for i in range(n_ind)])  8.82 us
    ppermute x10, starting transfers between devices, swap_cores(): return lax.ppermute(x, 'ind', [(i, i ^ 1) for i in range(n_ind)])  7.09 us
    pallas_call x1, Pallas kernels, load_counts(): pl.pallas_call(load_kernel, out_shape=jax.ShapeDtypeStruct((individuals,...  2.25 us
  transfers between devices with their start and end apart: 25, of which 24 were waited for; matrix products, arithmetic and copies ran while one was open for 1% of the time, Pallas kernels for 3%

profile of v4, /device:TPU:0, one launch (start us, length us, event | category | flops | bytes accessed | tf_op | source)
XLA Modules:
  0.0 69.6 jit_solution(13694338162233944341)
XLA Ops:
  2.7 2.9 %collective-permute-start.1 = (f32[32,256]{1,0:T(8,128)S(1)}, f32[32,256]{1,0:T(8,128)S(1)}, u32[]{:S(2)}, u32[]{:S(2)}) collective-permute-start(f32[32,256]{1,0:T(8,128)S(1)} %pad_maximum_fusion.1), channel_id=1, source_target_pairs={{0,8},{1,9},{2,10},{3,11},{4,5},{5,4},{6,7},{7,6},{8,0},{9,1},{10,... | collective-permute-start | bytes 98312 | tf_op jit(solution)/shard_map/ppermute | solution.py:179
  5.6 1.5 %collective-permute-start.2 = (f32[32,256]{1,0:T(8,128)S(1)}, f32[32,256]{1,0:T(8,128)S(1)}, u32[]{:S(2)}, u32[]{:S(2)}) collective-permute-start(f32[32,256]{1,0:T(8,128)S(1)} %pad_maximum_fusion.1), channel_id=1, source_target_pairs={{0,16},{1,17},{2,18},{3,19},{4,6},{5,7},{6,4},{7,5},{8,24},{9,25},... | collective-permute-start | bytes 98312 | tf_op jit(solution)/shard_map/ppermute | solution.py:179
  7.1 2.2 %shard_map.50.g_ref = f32[1024,1024]{1,0:T(8,128)S(1)} custom-call(s32[1024,1024]{1,0:T(8,128)} %g_hbm), custom_call_target="tpu_custom_call" | custom-call | flops 1048576 | bytes 4194304 | tf_op jit(solution)/shard_map/pallas_call | solution.py:61
  9.5 2.4 %collective-permute-done.3 = f32[32,256]{1,0:T(8,128)S(1)} collective-permute-done((f32[32,256]{1,0:T(8,128)S(1)}, f32[32,256]{1,0:T(8,128)S(1)}, u32[]{:S(2)}, u32[]{:S(2)}) %collective-permute-start.3) | collective-permute-done | bytes 32800 | tf_op jit(solution)/shard_map/ppermute | solution.py:179
  13.4 2.9 %shard_map.51 = (f32[32,1024]{1,0:T(8,128)S(1)}, f32[32,1024]{1,0:T(8,128)S(1)}, f32[16,1024]{1,0:T(8,128)S(1)}, f32[16,1024]{1,0:T(8,128)S(1)}) custom-call(f32[1024,1024]{1,0:T(8,128)S(1)} %shard_map.50.g_ref, f32[16,1024]{1,0:T(8,128)S(1)} %get-tuple-element.58.q_ref.keep_ref, f32[16,1024]{1,0:T(8,128)S(1)} %get-tuple-element.58.q_ref.keep_ref, ...), custom_call_target="tpu_custom_call" | custom-call | flops 671088640 | bytes 4194304 | tf_op jit(solution)/shard_map/pallas_call | solution.py:144
  16.9 1.0 %collective-permute-done.5 = f32[32,1024]{1,0:T(8,128)S(1)} collective-permute-done((f32[32,1024]{1,0:T(8,128)S(1)}, f32[32,1024]{1,0:T(8,128)S(1)}, u32[]{:S(2)}, u32[]{:S(2)}) %collective-permute-start.5) | collective-permute-done | bytes 131104 | tf_op jit(solution)/shard_map/ppermute | solution.py:167
  17.9 2.5 %collective-permute-start.6 = (f32[32,1024]{1,0:T(8,128)S(1)}, f32[32,1024]{1,0:T(8,128)S(1)}, u32[]{:S(2)}, u32[]{:S(2)}) collective-permute-start(f32[32,1024]{1,0:T(8,128)S(1)} %add.87), channel_id=1, source_target_pairs={{0,24},{1,25},{2,26},{3,27},{4,7},{5,6},{6,5},{7,4},{8,16},{9,17},... | collective-permute-start | bytes 393224 | tf_op jit(solution)/shard_map/ppermute | solution.py:179
  21.4 2.4 %collective-permute-done.6 = f32[32,1024]{1,0:T(8,128)S(1)} collective-permute-done((f32[32,1024]{1,0:T(8,128)S(1)}, f32[32,1024]{1,0:T(8,128)S(1)}, u32[]{:S(2)}, u32[]{:S(2)}) %collective-permute-start.6) | collective-permute-done | bytes 131104 | tf_op jit(solution)/shard_map/ppermute | solution.py:179
  23.8 1.5 %collective-permute-done.7 = f32[32,1024]{1,0:T(8,128)S(1)} collective-permute-done((f32[32,1024]{1,0:T(8,128)S(1)}, f32[32,1024]{1,0:T(8,128)S(1)}, u32[]{:S(2)}, u32[]{:S(2)}) %collective-permute-start.7) | collective-permute-done | bytes 131104 | tf_op jit(solution)/shard_map/ppermute | solution.py:179
  25.9 1.6 %collective-permute-start.9 = (f32[16,1024]{1,0:T(8,128)S(1)}, f32[16,1024]{1,0:T(8,128)S(1)}, u32[]{:S(2)}, u32[]{:S(2)}) collective-permute-start(f32[16,1024]{1,0:T(8,128)S(1)} %get-tuple-element.52), channel_id=1, source_target_pairs={{0,4},{4,0},{8,12},{12,8},{16,20},{20,16},{24,28},{28,24},{1,5},{5... | collective-permute-start | bytes 196616 | tf_op jit(solution)/shard_map/ppermute | solution.py:167
  27.6 0.9 %collective-permute-done.9.got_ref = f32[16,1024]{1,0:T(8,128)S(1)} collective-permute-done((f32[16,1024]{1,0:T(8,128)S(1)}, f32[16,1024]{1,0:T(8,128)S(1)}, u32[]{:S(2)}, u32[]{:S(2)}) %collective-permute-start.9) | collective-permute-done | bytes 65568 | tf_op jit(solution)/shard_map/ppermute | solution.py:167
  28.5 2.9 %shard_map.52 = (f32[32,1024]{1,0:T(8,128)S(1)}, f32[32,1024]{1,0:T(8,128)S(1)}, f32[16,1024]{1,0:T(8,128)S(1)}, f32[16,1024]{1,0:T(8,128)S(1)}) custom-call(f32[1024,1024]{1,0:T(8,128)S(1)} %shard_map.50.g_ref, f32[16,1024]{1,0:T(8,128)S(1)} %get-tuple-element.32.q_ref, f32[16,1024]{1,0:T(8,128)S(1)} %get-tuple-element.53.keep_ref, ...), custom_call_target="tpu_custom_call" | custom-call | flops 671088640 | bytes 4194304 | tf_op jit(solution)/shard_map/pallas_call | solution.py:144
  31.9 1.0 %collective-permute-done.10 = f32[32,1024]{1,0:T(8,128)S(1)} collective-permute-done((f32[32,1024]{1,0:T(8,128)S(1)}, f32[32,1024]{1,0:T(8,128)S(1)}, u32[]{:S(2)}, u32[]{:S(2)}) %collective-permute-start.10) | collective-permute-done | bytes 131104 | tf_op jit(solution)/shard_map/ppermute | solution.py:167
  32.9 1.0 %collective-permute-start.11 = (f32[32,1024]{1,0:T(8,128)S(1)}, f32[32,1024]{1,0:T(8,128)S(1)}, u32[]{:S(2)}, u32[]{:S(2)}) collective-permute-start(f32[32,1024]{1,0:T(8,128)S(1)} %add.92), channel_id=1, source_target_pairs={{0,24},{1,25},{2,26},{3,27},{4,7},{5,6},{6,5},{7,4},{8,16},{9,17},... | collective-permute-start | bytes 393224 | tf_op jit(solution)/shard_map/ppermute | solution.py:179
  33.9 1.3 %collective-permute-start.12 = (f32[32,1024]{1,0:T(8,128)S(1)}, f32[32,1024]{1,0:T(8,128)S(1)}, u32[]{:S(2)}, u32[]{:S(2)}) collective-permute-start(f32[32,1024]{1,0:T(8,128)S(1)} %add.92), channel_id=1, source_target_pairs={{0,8},{1,9},{2,10},{3,11},{4,5},{5,4},{6,7},{7,6},{8,0},{9,1},{10,... | collective-permute-start | bytes 393224 | tf_op jit(solution)/shard_map/ppermute | solution.py:179
  35.2 1.2 %collective-permute-start.13 = (f32[32,1024]{1,0:T(8,128)S(1)}, f32[32,1024]{1,0:T(8,128)S(1)}, u32[]{:S(2)}, u32[]{:S(2)}) collective-permute-start(f32[32,1024]{1,0:T(8,128)S(1)} %add.92), channel_id=1, source_target_pairs={{0,16},{1,17},{2,18},{3,19},{4,6},{5,7},{6,4},{7,5},{8,24},{9,25},... | collective-permute-start | bytes 393224 | tf_op jit(solution)/shard_map/ppermute | solution.py:179
  36.5 2.4 %collective-permute-done.11 = f32[32,1024]{1,0:T(8,128)S(1)} collective-permute-done((f32[32,1024]{1,0:T(8,128)S(1)}, f32[32,1024]{1,0:T(8,128)S(1)}, u32[]{:S(2)}, u32[]{:S(2)}) %collective-permute-start.11) | collective-permute-done | bytes 131104 | tf_op jit(solution)/shard_map/ppermute | solution.py:179
  42.0 3.1 %shard_map.53 = (f32[32,1024]{1,0:T(8,128)S(1)}, f32[32,1024]{1,0:T(8,128)S(1)}, f32[16,1024]{1,0:T(8,128)S(1)}, f32[16,1024]{1,0:T(8,128)S(1)}) custom-call(f32[1024,1024]{1,0:T(8,128)S(1)} %shard_map.50.g_ref, f32[16,1024]{1,0:T(8,128)S(1)} %get-tuple-element.36.q_ref, f32[16,1024]{1,0:T(8,128)S(1)} %get-tuple-element.51.keep_ref, ...), custom_call_target="tpu_custom_call" | custom-call | flops 671088640 | bytes 4194304 | tf_op jit(solution)/shard_map/pallas_call | solution.py:144
  45.6 1.0 %collective-permute-done.15 = f32[32,1024]{1,0:T(8,128)S(1)} collective-permute-done((f32[32,1024]{1,0:T(8,128)S(1)}, f32[32,1024]{1,0:T(8,128)S(1)}, u32[]{:S(2)}, u32[]{:S(2)}) %collective-permute-start.15) | collective-permute-done | bytes 131104 | tf_op jit(solution)/shard_map/ppermute | solution.py:167
  46.6 2.2 %collective-permute-start.16 = (f32[32,1024]{1,0:T(8,128)S(1)}, f32[32,1024]{1,0:T(8,128)S(1)}, u32[]{:S(2)}, u32[]{:S(2)}) collective-permute-start(f32[32,1024]{1,0:T(8,128)S(1)} %add.97), channel_id=1, source_target_pairs={{0,24},{1,25},{2,26},{3,27},{4,7},{5,6},{6,5},{7,4},{8,16},{9,17},... | collective-permute-start | bytes 393224 | tf_op jit(solution)/shard_map/ppermute | solution.py:179
  50.2 2.4 %collective-permute-done.16 = f32[32,1024]{1,0:T(8,128)S(1)} collective-permute-done((f32[32,1024]{1,0:T(8,128)S(1)}, f32[32,1024]{1,0:T(8,128)S(1)}, u32[]{:S(2)}, u32[]{:S(2)}) %collective-permute-start.16) | collective-permute-done | bytes 131104 | tf_op jit(solution)/shard_map/ppermute | solution.py:179
  52.6 1.3 %collective-permute-done.17 = f32[32,1024]{1,0:T(8,128)S(1)} collective-permute-done((f32[32,1024]{1,0:T(8,128)S(1)}, f32[32,1024]{1,0:T(8,128)S(1)}, u32[]{:S(2)}, u32[]{:S(2)}) %collective-permute-start.17) | collective-permute-done | bytes 131104 | tf_op jit(solution)/shard_map/ppermute | solution.py:179
  54.5 1.6 %collective-permute-start.19 = (f32[16,1024]{1,0:T(8,128)S(1)}, f32[16,1024]{1,0:T(8,128)S(1)}, u32[]{:S(2)}, u32[]{:S(2)}) collective-permute-start(f32[16,1024]{1,0:T(8,128)S(1)} %get-tuple-element.48), channel_id=1, source_target_pairs={{0,4},{4,0},{8,12},{12,8},{16,20},{20,16},{24,28},{28,24},{1,5},{5... | collective-permute-start | bytes 196616 | tf_op jit(solution)/shard_map/ppermute | solution.py:167
  56.0 0.9 %collective-permute-done.19.got_ref = f32[16,1024]{1,0:T(8,128)S(1)} collective-permute-done((f32[16,1024]{1,0:T(8,128)S(1)}, f32[16,1024]{1,0:T(8,128)S(1)}, u32[]{:S(2)}, u32[]{:S(2)}) %collective-permute-start.19) | collective-permute-done | bytes 65568 | tf_op jit(solution)/shard_map/ppermute | solution.py:167
  57.0 2.9 %shard_map.54 = (f32[32,1024]{1,0:T(8,128)S(1)}, f32[32,1024]{1,0:T(8,128)S(1)}, f32[16,1024]{1,0:T(8,128)S(1)}, f32[16,1024]{1,0:T(8,128)S(1)}) custom-call(f32[1024,1024]{1,0:T(8,128)S(1)} %shard_map.50.g_ref, f32[16,1024]{1,0:T(8,128)S(1)} %get-tuple-element.40.q_ref, f32[16,1024]{1,0:T(8,128)S(1)} %get-tuple-element.49.keep_ref, ...), custom_call_target="tpu_custom_call" | custom-call | flops 671088640 | bytes 4194304 | tf_op jit(solution)/shard_map/pallas_call | solution.py:144
  60.4 1.0 %collective-permute-done.20 = f32[32,1024]{1,0:T(8,128)S(1)} collective-permute-done((f32[32,1024]{1,0:T(8,128)S(1)}, f32[32,1024]{1,0:T(8,128)S(1)}, u32[]{:S(2)}, u32[]{:S(2)}) %collective-permute-start.20) | collective-permute-done | bytes 131104 | tf_op jit(solution)/shard_map/ppermute | solution.py:167
  61.4 1.0 %collective-permute-start.21 = (f32[32,256]{1,0:T(8,128)S(1)}, f32[32,256]{1,0:T(8,128)S(1)}, u32[]{:S(2)}, u32[]{:S(2)}) collective-permute-start(f32[32,256]{1,0:T(8,128)S(1)} %get-tuple-element.54), channel_id=1, source_target_pairs={{0,24},{1,25},{2,26},{3,27},{4,7},{5,6},{6,5},{7,4},{8,16},{9,17},... | collective-permute-start | bytes 98312 | tf_op jit(solution)/shard_map/ppermute | solution.py:179
  62.4 1.3 %collective-permute-start.22 = (f32[32,256]{1,0:T(8,128)S(1)}, f32[32,256]{1,0:T(8,128)S(1)}, u32[]{:S(2)}, u32[]{:S(2)}) collective-permute-start(f32[32,256]{1,0:T(8,128)S(1)} %get-tuple-element.56), channel_id=1, source_target_pairs={{0,16},{1,17},{2,18},{3,19},{4,6},{5,7},{6,4},{7,5},{8,24},{9,25},... | collective-permute-start | bytes 98312 | tf_op jit(solution)/shard_map/ppermute | solution.py:179
  63.7 1.2 %collective-permute-start.23 = (f32[32,256]{1,0:T(8,128)S(1)}, f32[32,256]{1,0:T(8,128)S(1)}, u32[]{:S(2)}, u32[]{:S(2)}) collective-permute-start(f32[32,256]{1,0:T(8,128)S(1)} %get-tuple-element.55), channel_id=1, source_target_pairs={{0,8},{1,9},{2,10},{3,11},{4,5},{5,4},{6,7},{7,6},{8,0},{9,1},{10,... | collective-permute-start | bytes 98312 | tf_op jit(solution)/shard_map/ppermute | solution.py:179
  65.0 1.4 %collective-permute-done.21 = f32[32,256]{1,0:T(8,128)S(1)} collective-permute-done((f32[32,256]{1,0:T(8,128)S(1)}, f32[32,256]{1,0:T(8,128)S(1)}, u32[]{:S(2)}, u32[]{:S(2)}) %collective-permute-start.21) | collective-permute-done | bytes 32800 | tf_op jit(solution)/shard_map/ppermute | solution.py:179
  66.6 1.0 %collective-permute-done.23 = f32[32,256]{1,0:T(8,128)S(1)} collective-permute-done((f32[32,256]{1,0:T(8,128)S(1)}, f32[32,256]{1,0:T(8,128)S(1)}, u32[]{:S(2)}, u32[]{:S(2)}) %collective-permute-start.23) | collective-permute-done | bytes 32800 | tf_op jit(solution)/shard_map/ppermute | solution.py:179
  67.8 1.2 %collective-permute-done.24.got_ref = f32[32,128]{1,0:T(8,128)S(1)} collective-permute-done((f32[32,128]{1,0:T(8,128)S(1)}, f32[32,128]{1,0:T(8,128)S(1)}, u32[]{:S(2)}, u32[]{:S(2)}) %collective-permute-start.24) | collective-permute-done | bytes 16416 | tf_op jit(solution)/shard_map/ppermute | solution.py:167
  (45 shorter events, 13.5 us)
Async XLA Ops:
  1.4 1.3 %collective-permute-start = (f32[16,256]{1,0:T(8,128)S(1)}, f32[16,256]{1,0:T(8,128)S(1)}, u32[]{:S(2)}, u32[]{:S(2)}) collective-permute-start(f32[16,256]{1,0:T(8,128)S(1)} %pad_select_fusion.1), channel_id=1, source_target_pairs={{0,4},{4,0},{8,12},{12,8},{16,20},{20,16},{24,28},{28,24},{1,5},{5... | collective-permute-start | bytes 49160 | tf_op jit(solution)/shard_map/ppermute | solution.py:167
  2.7 6.7 %collective-permute-start.1 = (f32[32,256]{1,0:T(8,128)S(1)}, f32[32,256]{1,0:T(8,128)S(1)}, u32[]{:S(2)}, u32[]{:S(2)}) collective-permute-start(f32[32,256]{1,0:T(8,128)S(1)} %pad_maximum_fusion.1), channel_id=1, source_target_pairs={{0,8},{1,9},{2,10},{3,11},{4,5},{5,4},{6,7},{7,6},{8,0},{9,1},{10,... | collective-permute-start | bytes 98312 | tf_op jit(solution)/shard_map/ppermute | solution.py:179
  5.6 3.9 %collective-permute-start.2 = (f32[32,256]{1,0:T(8,128)S(1)}, f32[32,256]{1,0:T(8,128)S(1)}, u32[]{:S(2)}, u32[]{:S(2)}) collective-permute-start(f32[32,256]{1,0:T(8,128)S(1)} %pad_maximum_fusion.1), channel_id=1, source_target_pairs={{0,16},{1,17},{2,18},{3,19},{4,6},{5,7},{6,4},{7,5},{8,24},{9,25},... | collective-permute-start | bytes 98312 | tf_op jit(solution)/shard_map/ppermute | solution.py:179
  7.1 4.8 %collective-permute-start.3 = (f32[32,256]{1,0:T(8,128)S(1)}, f32[32,256]{1,0:T(8,128)S(1)}, u32[]{:S(2)}, u32[]{:S(2)}) collective-permute-start(f32[32,256]{1,0:T(8,128)S(1)} %pad_maximum_fusion.1), channel_id=1, source_target_pairs={{0,24},{1,25},{2,26},{3,27},{4,7},{5,6},{6,5},{7,4},{8,16},{9,17},... | collective-permute-start | bytes 98312 | tf_op jit(solution)/shard_map/ppermute | solution.py:179
  12.0 1.5 %collective-permute-start.4 = (f32[16,1024]{1,0:T(8,128)S(1)}, f32[16,1024]{1,0:T(8,128)S(1)}, u32[]{:S(2)}, u32[]{:S(2)}) collective-permute-start(f32[16,1024]{1,0:T(8,128)S(1)} %get-tuple-element.57), channel_id=1, source_target_pairs={{0,4},{4,0},{8,12},{12,8},{16,20},{20,16},{24,28},{28,24},{1,5},{5... | collective-permute-start | bytes 196616 | tf_op jit(solution)/shard_map/ppermute | solution.py:167
  16.4 1.5 %collective-permute-start.5 = (f32[32,1024]{1,0:T(8,128)S(1)}, f32[32,1024]{1,0:T(8,128)S(1)}, u32[]{:S(2)}, u32[]{:S(2)}) collective-permute-start(f32[32,1024]{1,0:T(8,128)S(1)} %get-tuple-element.35), channel_id=1, source_target_pairs={{0,4},{4,0},{8,12},{12,8},{16,20},{20,16},{24,28},{28,24},{1,5},{5... | collective-permute-start | bytes 393224 | tf_op jit(solution)/shard_map/ppermute | solution.py:167
  17.9 5.9 %collective-permute-start.6 = (f32[32,1024]{1,0:T(8,128)S(1)}, f32[32,1024]{1,0:T(8,128)S(1)}, u32[]{:S(2)}, u32[]{:S(2)}) collective-permute-start(f32[32,1024]{1,0:T(8,128)S(1)} %add.87), channel_id=1, source_target_pairs={{0,24},{1,25},{2,26},{3,27},{4,7},{5,6},{6,5},{7,4},{8,16},{9,17},... | collective-permute-start | bytes 393224 | tf_op jit(solution)/shard_map/ppermute | solution.py:179
  20.4 5.0 %collective-permute-start.7 = (f32[32,1024]{1,0:T(8,128)S(1)}, f32[32,1024]{1,0:T(8,128)S(1)}, u32[]{:S(2)}, u32[]{:S(2)}) collective-permute-start(f32[32,1024]{1,0:T(8,128)S(1)} %add.87), channel_id=1, source_target_pairs={{0,8},{1,9},{2,10},{3,11},{4,5},{5,4},{6,7},{7,6},{8,0},{9,1},{10,... | collective-permute-start | bytes 393224 | tf_op jit(solution)/shard_map/ppermute | solution.py:179
  20.9 5.0 %collective-permute-start.8 = (f32[32,1024]{1,0:T(8,128)S(1)}, f32[32,1024]{1,0:T(8,128)S(1)}, u32[]{:S(2)}, u32[]{:S(2)}) collective-permute-start(f32[32,1024]{1,0:T(8,128)S(1)} %add.87), channel_id=1, source_target_pairs={{0,16},{1,17},{2,18},{3,19},{4,6},{5,7},{6,4},{7,5},{8,24},{9,25},... | collective-permute-start | bytes 393224 | tf_op jit(solution)/shard_map/ppermute | solution.py:179
  25.9 2.5 %collective-permute-start.9 = (f32[16,1024]{1,0:T(8,128)S(1)}, f32[16,1024]{1,0:T(8,128)S(1)}, u32[]{:S(2)}, u32[]{:S(2)}) collective-permute-start(f32[16,1024]{1,0:T(8,128)S(1)} %get-tuple-element.52), channel_id=1, source_target_pairs={{0,4},{4,0},{8,12},{12,8},{16,20},{20,16},{24,28},{28,24},{1,5},{5... | collective-permute-start | bytes 196616 | tf_op jit(solution)/shard_map/ppermute | solution.py:167
  31.4 1.5 %collective-permute-start.10 = (f32[32,1024]{1,0:T(8,128)S(1)}, f32[32,1024]{1,0:T(8,128)S(1)}, u32[]{:S(2)}, u32[]{:S(2)}) collective-permute-start(f32[32,1024]{1,0:T(8,128)S(1)} %get-tuple-element.39), channel_id=1, source_target_pairs={{0,4},{4,0},{8,12},{12,8},{16,20},{20,16},{24,28},{28,24},{1,5},{5... | collective-permute-start | bytes 393224 | tf_op jit(solution)/shard_map/ppermute | solution.py:167
  32.9 5.9 %collective-permute-start.11 = (f32[32,1024]{1,0:T(8,128)S(1)}, f32[32,1024]{1,0:T(8,128)S(1)}, u32[]{:S(2)}, u32[]{:S(2)}) collective-permute-start(f32[32,1024]{1,0:T(8,128)S(1)} %add.92), channel_id=1, source_target_pairs={{0,24},{1,25},{2,26},{3,27},{4,7},{5,6},{6,5},{7,4},{8,16},{9,17},... | collective-permute-start | bytes 393224 | tf_op jit(solution)/shard_map/ppermute | solution.py:179
  33.9 5.7 %collective-permute-start.12 = (f32[32,1024]{1,0:T(8,128)S(1)}, f32[32,1024]{1,0:T(8,128)S(1)}, u32[]{:S(2)}, u32[]{:S(2)}) collective-permute-start(f32[32,1024]{1,0:T(8,128)S(1)} %add.92), channel_id=1, source_target_pairs={{0,8},{1,9},{2,10},{3,11},{4,5},{5,4},{6,7},{7,6},{8,0},{9,1},{10,... | collective-permute-start | bytes 393224 | tf_op jit(solution)/shard_map/ppermute | solution.py:179
  35.2 5.0 %collective-permute-start.13 = (f32[32,1024]{1,0:T(8,128)S(1)}, f32[32,1024]{1,0:T(8,128)S(1)}, u32[]{:S(2)}, u32[]{:S(2)}) collective-permute-start(f32[32,1024]{1,0:T(8,128)S(1)} %add.92), channel_id=1, source_target_pairs={{0,16},{1,17},{2,18},{3,19},{4,6},{5,7},{6,4},{7,5},{8,24},{9,25},... | collective-permute-start | bytes 393224 | tf_op jit(solution)/shard_map/ppermute | solution.py:179
  40.3 1.7 %collective-permute-start.14 = (f32[16,1024]{1,0:T(8,128)S(1)}, f32[16,1024]{1,0:T(8,128)S(1)}, u32[]{:S(2)}, u32[]{:S(2)}) collective-permute-start(f32[16,1024]{1,0:T(8,128)S(1)} %get-tuple-element.50), channel_id=1, source_target_pairs={{0,4},{4,0},{8,12},{12,8},{16,20},{20,16},{24,28},{28,24},{1,5},{5... | collective-permute-start | bytes 196616 | tf_op jit(solution)/shard_map/ppermute | solution.py:167
  45.1 1.5 %collective-permute-start.15 = (f32[32,1024]{1,0:T(8,128)S(1)}, f32[32,1024]{1,0:T(8,128)S(1)}, u32[]{:S(2)}, u32[]{:S(2)}) collective-permute-start(f32[32,1024]{1,0:T(8,128)S(1)} %get-tuple-element.43), channel_id=1, source_target_pairs={{0,4},{4,0},{8,12},{12,8},{16,20},{20,16},{24,28},{28,24},{1,5},{5... | collective-permute-start | bytes 393224 | tf_op jit(solution)/shard_map/ppermute | solution.py:167
  46.6 5.9 %collective-permute-start.16 = (f32[32,1024]{1,0:T(8,128)S(1)}, f32[32,1024]{1,0:T(8,128)S(1)}, u32[]{:S(2)}, u32[]{:S(2)}) collective-permute-start(f32[32,1024]{1,0:T(8,128)S(1)} %add.97), channel_id=1, source_target_pairs={{0,24},{1,25},{2,26},{3,27},{4,7},{5,6},{6,5},{7,4},{8,16},{9,17},... | collective-permute-start | bytes 393224 | tf_op jit(solution)/shard_map/ppermute | solution.py:179
  48.9 5.0 %collective-permute-start.17 = (f32[32,1024]{1,0:T(8,128)S(1)}, f32[32,1024]{1,0:T(8,128)S(1)}, u32[]{:S(2)}, u32[]{:S(2)}) collective-permute-start(f32[32,1024]{1,0:T(8,128)S(1)} %add.97), channel_id=1, source_target_pairs={{0,8},{1,9},{2,10},{3,11},{4,5},{5,4},{6,7},{7,6},{8,0},{9,1},{10,... | collective-permute-start | bytes 393224 | tf_op jit(solution)/shard_map/ppermute | solution.py:179
  49.4 5.0 %collective-permute-start.18 = (f32[32,1024]{1,0:T(8,128)S(1)}, f32[32,1024]{1,0:T(8,128)S(1)}, u32[]{:S(2)}, u32[]{:S(2)}) collective-permute-start(f32[32,1024]{1,0:T(8,128)S(1)} %add.97), channel_id=1, source_target_pairs={{0,16},{1,17},{2,18},{3,19},{4,6},{5,7},{6,4},{7,5},{8,24},{9,25},... | collective-permute-start | bytes 393224 | tf_op jit(solution)/shard_map/ppermute | solution.py:179
  54.5 2.5 %collective-permute-start.19 = (f32[16,1024]{1,0:T(8,128)S(1)}, f32[16,1024]{1,0:T(8,128)S(1)}, u32[]{:S(2)}, u32[]{:S(2)}) collective-permute-start(f32[16,1024]{1,0:T(8,128)S(1)} %get-tuple-element.48), channel_id=1, source_target_pairs={{0,4},{4,0},{8,12},{12,8},{16,20},{20,16},{24,28},{28,24},{1,5},{5... | collective-permute-start | bytes 196616 | tf_op jit(solution)/shard_map/ppermute | solution.py:167
  59.9 1.5 %collective-permute-start.20 = (f32[32,1024]{1,0:T(8,128)S(1)}, f32[32,1024]{1,0:T(8,128)S(1)}, u32[]{:S(2)}, u32[]{:S(2)}) collective-permute-start(f32[32,1024]{1,0:T(8,128)S(1)} %get-tuple-element.47), channel_id=1, source_target_pairs={{0,4},{4,0},{8,12},{12,8},{16,20},{20,16},{24,28},{28,24},{1,5},{5... | collective-permute-start | bytes 393224 | tf_op jit(solution)/shard_map/ppermute | solution.py:167
  61.4 4.9 %collective-permute-start.21 = (f32[32,256]{1,0:T(8,128)S(1)}, f32[32,256]{1,0:T(8,128)S(1)}, u32[]{:S(2)}, u32[]{:S(2)}) collective-permute-start(f32[32,256]{1,0:T(8,128)S(1)} %get-tuple-element.54), channel_id=1, source_target_pairs={{0,24},{1,25},{2,26},{3,27},{4,7},{5,6},{6,5},{7,4},{8,16},{9,17},... | collective-permute-start | bytes 98312 | tf_op jit(solution)/shard_map/ppermute | solution.py:179
  62.4 4.2 %collective-permute-start.22 = (f32[32,256]{1,0:T(8,128)S(1)}, f32[32,256]{1,0:T(8,128)S(1)}, u32[]{:S(2)}, u32[]{:S(2)}) collective-permute-start(f32[32,256]{1,0:T(8,128)S(1)} %get-tuple-element.56), channel_id=1, source_target_pairs={{0,16},{1,17},{2,18},{3,19},{4,6},{5,7},{6,4},{7,5},{8,24},{9,25},... | collective-permute-start | bytes 98312 | tf_op jit(solution)/shard_map/ppermute | solution.py:179
  63.7 3.9 %collective-permute-start.23 = (f32[32,256]{1,0:T(8,128)S(1)}, f32[32,256]{1,0:T(8,128)S(1)}, u32[]{:S(2)}, u32[]{:S(2)}) collective-permute-start(f32[32,256]{1,0:T(8,128)S(1)} %get-tuple-element.55), channel_id=1, source_target_pairs={{0,8},{1,9},{2,10},{3,11},{4,5},{5,4},{6,7},{7,6},{8,0},{9,1},{10,... | collective-permute-start | bytes 98312 | tf_op jit(solution)/shard_map/ppermute | solution.py:179
  67.7 1.2 %collective-permute-start.24 = (f32[32,128]{1,0:T(8,128)S(1)}, f32[32,128]{1,0:T(8,128)S(1)}, u32[]{:S(2)}, u32[]{:S(2)}) collective-permute-start(f32[32,128]{1,0:T(8,128)S(1)} %get-tuple-element.63), channel_id=1, source_target_pairs={{0,4},{4,0},{8,12},{12,8},{16,20},{20,16},{24,28},{28,24},{1,5},{5... | collective-permute-start | bytes 49160 | tf_op jit(solution)/shard_map/ppermute | solution.py:167

commit v5 on v4

--- a/solution.py
+++ b/solution.py
@@ -210,7 +210,7 @@
     own, genotypes = lax.optimization_barrier((own, genotypes))
     half = load_counts(genotypes)
     chunks = [own] + [exchange(own, m, n_ind, n_snp) for m in range(1, n_snp)]
-    *chunks, half = lax.optimization_barrier((*chunks, half))
+    chunks[3], half = lax.optimization_barrier((chunks[3], half))
     bit = 1
     while bit < n_snp:
         flip = (index & bit) != 0

time: 70 us -> 69.1 us (0.987)
  waiting for transfers between devices: 26.5 us -> 25.5 us
    ppermute x15, waiting for transfers between devices: 17.7 us -> 16.6 us  [exchange(): return lax.ppermute(x, AXES, pairs) if pairs else None]
where the time goes in v5:
time: 69.1 us; the launch traced here: 68.6 us
  starting transfers between devices  25.7 us (37%)
  waiting for transfers between devices  25.5 us (37%)
  Pallas kernels  14.8 us (21%)
  other arithmetic  1.77 us (3%)
  between operations  0.8 us (1%)
    ppermute x15, starting transfers between devices, exchange(): return lax.ppermute(x, AXES, pairs) if pairs else None  18.7 us
    ppermute x15, waiting for transfers between devices, exchange(): return lax.ppermute(x, AXES, pairs) if pairs else None  16.6 us
    pallas_call x4, Pallas kernels, em_step(): pl.pallas_call(functools.partial(em_kernel, first, snps_all), out_shape=(...  11.9 us
    ppermute x10, waiting for transfers between devices, swap_cores(): return lax.ppermute(x, 'ind', [(i, i ^ 1) for i in range(n_ind)])  8.89 us
    ppermute x10, starting transfers between devices, swap_cores(): return lax.ppermute(x, 'ind', [(i, i ^ 1) for i in range(n_ind)])  7.01 us
    pallas_call x1, Pallas kernels, load_counts(): pl.pallas_call(load_kernel, out_shape=jax.ShapeDtypeStruct((individuals,...  2.25 us
  transfers between devices with their start and end apart: 25, of which 24 were waited for; matrix products, arithmetic and copies ran while one was open for 1% of the time, Pallas kernels for 3%

profile of v5, /device:TPU:0, one launch (start us, length us, event | category | flops | bytes accessed | tf_op | source)
XLA Modules:
  0.0 68.6 jit_solution(15893915263458007265)
XLA Ops:
  2.7 3.9 %collective-permute-start.1 = (f32[32,256]{1,0:T(8,128)S(1)}, f32[32,256]{1,0:T(8,128)S(1)}, u32[]{:S(2)}, u32[]{:S(2)}) collective-permute-start(f32[32,256]{1,0:T(8,128)S(1)} %pad_maximum_fusion.1), channel_id=1, source_target_pairs={{0,24},{1,25},{2,26},{3,27},{4,7},{5,6},{6,5},{7,4},{8,16},{9,17},... | collective-permute-start | bytes 98312 | tf_op jit(solution)/shard_map/ppermute | solution.py:179
  7.2 2.2 %shard_map.50.g_ref = f32[1024,1024]{1,0:T(8,128)S(1)} custom-call(s32[1024,1024]{1,0:T(8,128)} %g_hbm), custom_call_target="tpu_custom_call" | custom-call | flops 1048576 | bytes 4194304 | tf_op jit(solution)/shard_map/pallas_call | solution.py:61
  9.4 1.0 %collective-permute-done.2 = f32[32,256]{1,0:T(8,128)S(1)} collective-permute-done((f32[32,256]{1,0:T(8,128)S(1)}, f32[32,256]{1,0:T(8,128)S(1)}, u32[]{:S(2)}, u32[]{:S(2)}) %collective-permute-start.2) | collective-permute-done | bytes 32800 | tf_op jit(solution)/shard_map/ppermute | solution.py:179
  11.4 1.0 %collective-permute-done.4.got_ref = f32[16,1024]{1,0:T(8,128)S(1)} collective-permute-done((f32[16,1024]{1,0:T(8,128)S(1)}, f32[16,1024]{1,0:T(8,128)S(1)}, u32[]{:S(2)}, u32[]{:S(2)}) %collective-permute-start.4) | collective-permute-done | bytes 65568 | tf_op jit(solution)/shard_map/ppermute | solution.py:167
  12.3 2.9 %shard_map.51 = (f32[32,1024]{1,0:T(8,128)S(1)}, f32[32,1024]{1,0:T(8,128)S(1)}, f32[16,1024]{1,0:T(8,128)S(1)}, f32[16,1024]{1,0:T(8,128)S(1)}) custom-call(f32[1024,1024]{1,0:T(8,128)S(1)} %shard_map.50.g_ref, f32[16,1024]{1,0:T(8,128)S(1)} %get-tuple-element.52.q_ref.keep_ref, f32[16,1024]{1,0:T(8,128)S(1)} %get-tuple-element.52.q_ref.keep_ref, ...), custom_call_target="tpu_custom_call" | custom-call | flops 671088640 | bytes 4194304 | tf_op jit(solution)/shard_map/pallas_call | solution.py:144
  15.7 1.0 %collective-permute-done.5 = f32[32,1024]{1,0:T(8,128)S(1)} collective-permute-done((f32[32,1024]{1,0:T(8,128)S(1)}, f32[32,1024]{1,0:T(8,128)S(1)}, u32[]{:S(2)}, u32[]{:S(2)}) %collective-permute-start.5) | collective-permute-done | bytes 131104 | tf_op jit(solution)/shard_map/ppermute | solution.py:167
  16.7 2.5 %collective-permute-start.6 = (f32[32,1024]{1,0:T(8,128)S(1)}, f32[32,1024]{1,0:T(8,128)S(1)}, u32[]{:S(2)}, u32[]{:S(2)}) collective-permute-start(f32[32,1024]{1,0:T(8,128)S(1)} %add.87), channel_id=1, source_target_pairs={{0,24},{1,25},{2,26},{3,27},{4,7},{5,6},{6,5},{7,4},{8,16},{9,17},... | collective-permute-start | bytes 393224 | tf_op jit(solution)/shard_map/ppermute | solution.py:179
  20.2 2.4 %collective-permute-done.6 = f32[32,1024]{1,0:T(8,128)S(1)} collective-permute-done((f32[32,1024]{1,0:T(8,128)S(1)}, f32[32,1024]{1,0:T(8,128)S(1)}, u32[]{:S(2)}, u32[]{:S(2)}) %collective-permute-start.6) | collective-permute-done | bytes 131104 | tf_op jit(solution)/shard_map/ppermute | solution.py:179
  22.6 1.5 %collective-permute-done.7 = f32[32,1024]{1,0:T(8,128)S(1)} collective-permute-done((f32[32,1024]{1,0:T(8,128)S(1)}, f32[32,1024]{1,0:T(8,128)S(1)}, u32[]{:S(2)}, u32[]{:S(2)}) %collective-permute-start.7) | collective-permute-done | bytes 131104 | tf_op jit(solution)/shard_map/ppermute | solution.py:179
  24.8 1.8 %collective-permute-start.9 = (f32[16,1024]{1,0:T(8,128)S(1)}, f32[16,1024]{1,0:T(8,128)S(1)}, u32[]{:S(2)}, u32[]{:S(2)}) collective-permute-start(f32[16,1024]{1,0:T(8,128)S(1)} %get-tuple-element.46), channel_id=1, source_target_pairs={{0,4},{4,0},{8,12},{12,8},{16,20},{20,16},{24,28},{28,24},{1,5},{5... | collective-permute-start | bytes 196616 | tf_op jit(solution)/shard_map/ppermute | solution.py:167
  26.6 0.9 %collective-permute-done.9.got_ref = f32[16,1024]{1,0:T(8,128)S(1)} collective-permute-done((f32[16,1024]{1,0:T(8,128)S(1)}, f32[16,1024]{1,0:T(8,128)S(1)}, u32[]{:S(2)}, u32[]{:S(2)}) %collective-permute-start.9) | collective-permute-done | bytes 65568 | tf_op jit(solution)/shard_map/ppermute | solution.py:167
  27.5 2.9 %shard_map.52 = (f32[32,1024]{1,0:T(8,128)S(1)}, f32[32,1024]{1,0:T(8,128)S(1)}, f32[16,1024]{1,0:T(8,128)S(1)}, f32[16,1024]{1,0:T(8,128)S(1)}) custom-call(f32[1024,1024]{1,0:T(8,128)S(1)} %shard_map.50.g_ref, f32[16,1024]{1,0:T(8,128)S(1)} %get-tuple-element.26.q_ref, f32[16,1024]{1,0:T(8,128)S(1)} %get-tuple-element.47.keep_ref, ...), custom_call_target="tpu_custom_call" | custom-call | flops 671088640 | bytes 4194304 | tf_op jit(solution)/shard_map/pallas_call | solution.py:144
  30.9 1.0 %collective-permute-done.10 = f32[32,1024]{1,0:T(8,128)S(1)} collective-permute-done((f32[32,1024]{1,0:T(8,128)S(1)}, f32[32,1024]{1,0:T(8,128)S(1)}, u32[]{:S(2)}, u32[]{:S(2)}) %collective-permute-start.10) | collective-permute-done | bytes 131104 | tf_op jit(solution)/shard_map/ppermute | solution.py:167
  31.9 1.6 %collective-permute-start.11 = (f32[32,1024]{1,0:T(8,128)S(1)}, f32[32,1024]{1,0:T(8,128)S(1)}, u32[]{:S(2)}, u32[]{:S(2)}) collective-permute-start(f32[32,1024]{1,0:T(8,128)S(1)} %add.92), channel_id=1, source_target_pairs={{0,24},{1,25},{2,26},{3,27},{4,7},{5,6},{6,5},{7,4},{8,16},{9,17},... | collective-permute-start | bytes 393224 | tf_op jit(solution)/shard_map/ppermute | solution.py:179
  33.5 1.5 %collective-permute-start.12 = (f32[32,1024]{1,0:T(8,128)S(1)}, f32[32,1024]{1,0:T(8,128)S(1)}, u32[]{:S(2)}, u32[]{:S(2)}) collective-permute-start(f32[32,1024]{1,0:T(8,128)S(1)} %add.92), channel_id=1, source_target_pairs={{0,8},{1,9},{2,10},{3,11},{4,5},{5,4},{6,7},{7,6},{8,0},{9,1},{10,... | collective-permute-start | bytes 393224 | tf_op jit(solution)/shard_map/ppermute | solution.py:179
  35.5 2.4 %collective-permute-done.11 = f32[32,1024]{1,0:T(8,128)S(1)} collective-permute-done((f32[32,1024]{1,0:T(8,128)S(1)}, f32[32,1024]{1,0:T(8,128)S(1)}, u32[]{:S(2)}, u32[]{:S(2)}) %collective-permute-start.11) | collective-permute-done | bytes 131104 | tf_op jit(solution)/shard_map/ppermute | solution.py:179
  37.9 1.5 %collective-permute-done.12 = f32[32,1024]{1,0:T(8,128)S(1)} collective-permute-done((f32[32,1024]{1,0:T(8,128)S(1)}, f32[32,1024]{1,0:T(8,128)S(1)}, u32[]{:S(2)}, u32[]{:S(2)}) %collective-permute-start.12) | collective-permute-done | bytes 131104 | tf_op jit(solution)/shard_map/ppermute | solution.py:179
  40.8 0.9 %collective-permute-done.14.got_ref = f32[16,1024]{1,0:T(8,128)S(1)} collective-permute-done((f32[16,1024]{1,0:T(8,128)S(1)}, f32[16,1024]{1,0:T(8,128)S(1)}, u32[]{:S(2)}, u32[]{:S(2)}) %collective-permute-start.14) | collective-permute-done | bytes 65568 | tf_op jit(solution)/shard_map/ppermute | solution.py:167
  41.7 3.1 %shard_map.53 = (f32[32,1024]{1,0:T(8,128)S(1)}, f32[32,1024]{1,0:T(8,128)S(1)}, f32[16,1024]{1,0:T(8,128)S(1)}, f32[16,1024]{1,0:T(8,128)S(1)}) custom-call(f32[1024,1024]{1,0:T(8,128)S(1)} %shard_map.50.g_ref, f32[16,1024]{1,0:T(8,128)S(1)} %get-tuple-element.30.q_ref, f32[16,1024]{1,0:T(8,128)S(1)} %get-tuple-element.45.keep_ref, ...), custom_call_target="tpu_custom_call" | custom-call | flops 671088640 | bytes 4194304 | tf_op jit(solution)/shard_map/pallas_call | solution.py:144
  45.4 1.0 %collective-permute-done.15 = f32[32,1024]{1,0:T(8,128)S(1)} collective-permute-done((f32[32,1024]{1,0:T(8,128)S(1)}, f32[32,1024]{1,0:T(8,128)S(1)}, u32[]{:S(2)}, u32[]{:S(2)}) %collective-permute-start.15) | collective-permute-done | bytes 131104 | tf_op jit(solution)/shard_map/ppermute | solution.py:167
  46.4 1.3 %collective-permute-start.16 = (f32[32,1024]{1,0:T(8,128)S(1)}, f32[32,1024]{1,0:T(8,128)S(1)}, u32[]{:S(2)}, u32[]{:S(2)}) collective-permute-start(f32[32,1024]{1,0:T(8,128)S(1)} %add.97), channel_id=1, source_target_pairs={{0,24},{1,25},{2,26},{3,27},{4,7},{5,6},{6,5},{7,4},{8,16},{9,17},... | collective-permute-start | bytes 393224 | tf_op jit(solution)/shard_map/ppermute | solution.py:179
  47.7 1.0 %collective-permute-start.17 = (f32[32,1024]{1,0:T(8,128)S(1)}, f32[32,1024]{1,0:T(8,128)S(1)}, u32[]{:S(2)}, u32[]{:S(2)}) collective-permute-start(f32[32,1024]{1,0:T(8,128)S(1)} %add.97), channel_id=1, source_target_pairs={{0,8},{1,9},{2,10},{3,11},{4,5},{5,4},{6,7},{7,6},{8,0},{9,1},{10,... | collective-permute-start | bytes 393224 | tf_op jit(solution)/shard_map/ppermute | solution.py:179
  48.7 1.2 %collective-permute-start.18 = (f32[32,1024]{1,0:T(8,128)S(1)}, f32[32,1024]{1,0:T(8,128)S(1)}, u32[]{:S(2)}, u32[]{:S(2)}) collective-permute-start(f32[32,1024]{1,0:T(8,128)S(1)} %add.97), channel_id=1, source_target_pairs={{0,16},{1,17},{2,18},{3,19},{4,6},{5,7},{6,4},{7,5},{8,24},{9,25},... | collective-permute-start | bytes 393224 | tf_op jit(solution)/shard_map/ppermute | solution.py:179
  49.9 2.4 %collective-permute-done.16 = f32[32,1024]{1,0:T(8,128)S(1)} collective-permute-done((f32[32,1024]{1,0:T(8,128)S(1)}, f32[32,1024]{1,0:T(8,128)S(1)}, u32[]{:S(2)}, u32[]{:S(2)}) %collective-permute-start.16) | collective-permute-done | bytes 131104 | tf_op jit(solution)/shard_map/ppermute | solution.py:179
  53.8 1.6 %collective-permute-start.19 = (f32[16,1024]{1,0:T(8,128)S(1)}, f32[16,1024]{1,0:T(8,128)S(1)}, u32[]{:S(2)}, u32[]{:S(2)}) collective-permute-start(f32[16,1024]{1,0:T(8,128)S(1)} %get-tuple-element.42), channel_id=1, source_target_pairs={{0,4},{4,0},{8,12},{12,8},{16,20},{20,16},{24,28},{28,24},{1,5},{5... | collective-permute-start | bytes 196616 | tf_op jit(solution)/shard_map/ppermute | solution.py:167
  55.3 0.9 %collective-permute-done.19.got_ref = f32[16,1024]{1,0:T(8,128)S(1)} collective-permute-done((f32[16,1024]{1,0:T(8,128)S(1)}, f32[16,1024]{1,0:T(8,128)S(1)}, u32[]{:S(2)}, u32[]{:S(2)}) %collective-permute-start.19) | collective-permute-done | bytes 65568 | tf_op jit(solution)/shard_map/ppermute | solution.py:167
  56.2 2.9 %shard_map.54 = (f32[32,1024]{1,0:T(8,128)S(1)}, f32[32,1024]{1,0:T(8,128)S(1)}, f32[16,1024]{1,0:T(8,128)S(1)}, f32[16,1024]{1,0:T(8,128)S(1)}) custom-call(f32[1024,1024]{1,0:T(8,128)S(1)} %shard_map.50.g_ref, f32[16,1024]{1,0:T(8,128)S(1)} %get-tuple-element.34.q_ref, f32[16,1024]{1,0:T(8,128)S(1)} %get-tuple-element.43.keep_ref, ...), custom_call_target="tpu_custom_call" | custom-call | flops 671088640 | bytes 4194304 | tf_op jit(solution)/shard_map/pallas_call | solution.py:144
  59.7 1.0 %collective-permute-done.20 = f32[32,1024]{1,0:T(8,128)S(1)} collective-permute-done((f32[32,1024]{1,0:T(8,128)S(1)}, f32[32,1024]{1,0:T(8,128)S(1)}, u32[]{:S(2)}, u32[]{:S(2)}) %collective-permute-start.20) | collective-permute-done | bytes 131104 | tf_op jit(solution)/shard_map/ppermute | solution.py:167
  60.7 1.3 %collective-permute-start.21 = (f32[32,256]{1,0:T(8,128)S(1)}, f32[32,256]{1,0:T(8,128)S(1)}, u32[]{:S(2)}, u32[]{:S(2)}) collective-permute-start(f32[32,256]{1,0:T(8,128)S(1)} %get-tuple-element.48), channel_id=1, source_target_pairs={{0,24},{1,25},{2,26},{3,27},{4,7},{5,6},{6,5},{7,4},{8,16},{9,17},... | collective-permute-start | bytes 98312 | tf_op jit(solution)/shard_map/ppermute | solution.py:179
  62.8 1.5 %collective-permute-start.23 = (f32[32,256]{1,0:T(8,128)S(1)}, f32[32,256]{1,0:T(8,128)S(1)}, u32[]{:S(2)}, u32[]{:S(2)}) collective-permute-start(f32[32,256]{1,0:T(8,128)S(1)} %get-tuple-element.49), channel_id=1, source_target_pairs={{0,8},{1,9},{2,10},{3,11},{4,5},{5,4},{6,7},{7,6},{8,0},{9,1},{10,... | collective-permute-start | bytes 98312 | tf_op jit(solution)/shard_map/ppermute | solution.py:179
  64.3 1.3 %collective-permute-done.21 = f32[32,256]{1,0:T(8,128)S(1)} collective-permute-done((f32[32,256]{1,0:T(8,128)S(1)}, f32[32,256]{1,0:T(8,128)S(1)}, u32[]{:S(2)}, u32[]{:S(2)}) %collective-permute-start.21) | collective-permute-done | bytes 32800 | tf_op jit(solution)/shard_map/ppermute | solution.py:179
  66.8 1.2 %collective-permute-done.24.got_ref = f32[32,128]{1,0:T(8,128)S(1)} collective-permute-done((f32[32,128]{1,0:T(8,128)S(1)}, f32[32,128]{1,0:T(8,128)S(1)}, u32[]{:S(2)}, u32[]{:S(2)}) %collective-permute-start.24) | collective-permute-done | bytes 16416 | tf_op jit(solution)/shard_map/ppermute | solution.py:167
  (45 shorter events, 13.2 us)
Async XLA Ops:
  1.4 1.3 %collective-permute-start = (f32[16,256]{1,0:T(8,128)S(1)}, f32[16,256]{1,0:T(8,128)S(1)}, u32[]{:S(2)}, u32[]{:S(2)}) collective-permute-start(f32[16,256]{1,0:T(8,128)S(1)} %pad_select_fusion.1), channel_id=1, source_target_pairs={{0,4},{4,0},{8,12},{12,8},{16,20},{20,16},{24,28},{28,24},{1,5},{5... | collective-permute-start | bytes 49160 | tf_op jit(solution)/shard_map/ppermute | solution.py:167
  2.7 6.8 %collective-permute-start.1 = (f32[32,256]{1,0:T(8,128)S(1)}, f32[32,256]{1,0:T(8,128)S(1)}, u32[]{:S(2)}, u32[]{:S(2)}) collective-permute-start(f32[32,256]{1,0:T(8,128)S(1)} %pad_maximum_fusion.1), channel_id=1, source_target_pairs={{0,24},{1,25},{2,26},{3,27},{4,7},{5,6},{6,5},{7,4},{8,16},{9,17},... | collective-permute-start | bytes 98312 | tf_op jit(solution)/shard_map/ppermute | solution.py:179
  6.5 3.9 %collective-permute-start.2 = (f32[32,256]{1,0:T(8,128)S(1)}, f32[32,256]{1,0:T(8,128)S(1)}, u32[]{:S(2)}, u32[]{:S(2)}) collective-permute-start(f32[32,256]{1,0:T(8,128)S(1)} %pad_maximum_fusion.1), channel_id=1, source_target_pairs={{0,16},{1,17},{2,18},{3,19},{4,6},{5,7},{6,4},{7,5},{8,24},{9,25},... | collective-permute-start | bytes 98312 | tf_op jit(solution)/shard_map/ppermute | solution.py:179
  7.0 3.9 %collective-permute-start.3 = (f32[32,256]{1,0:T(8,128)S(1)}, f32[32,256]{1,0:T(8,128)S(1)}, u32[]{:S(2)}, u32[]{:S(2)}) collective-permute-start(f32[32,256]{1,0:T(8,128)S(1)} %pad_maximum_fusion.1), channel_id=1, source_target_pairs={{0,8},{1,9},{2,10},{3,11},{4,5},{5,4},{6,7},{7,6},{8,0},{9,1},{10,... | collective-permute-start | bytes 98312 | tf_op jit(solution)/shard_map/ppermute | solution.py:179
  11.0 1.3 %collective-permute-start.4 = (f32[16,1024]{1,0:T(8,128)S(1)}, f32[16,1024]{1,0:T(8,128)S(1)}, u32[]{:S(2)}, u32[]{:S(2)}) collective-permute-start(f32[16,1024]{1,0:T(8,128)S(1)} %get-tuple-element.51), channel_id=1, source_target_pairs={{0,4},{4,0},{8,12},{12,8},{16,20},{20,16},{24,28},{28,24},{1,5},{5... | collective-permute-start | bytes 196616 | tf_op jit(solution)/shard_map/ppermute | solution.py:167
  15.3 1.4 %collective-permute-start.5 = (f32[32,1024]{1,0:T(8,128)S(1)}, f32[32,1024]{1,0:T(8,128)S(1)}, u32[]{:S(2)}, u32[]{:S(2)}) collective-permute-start(f32[32,1024]{1,0:T(8,128)S(1)} %get-tuple-element.29), channel_id=1, source_target_pairs={{0,4},{4,0},{8,12},{12,8},{16,20},{20,16},{24,28},{28,24},{1,5},{5... | collective-permute-start | bytes 393224 | tf_op jit(solution)/shard_map/ppermute | solution.py:167
  16.7 5.9 %collective-permute-start.6 = (f32[32,1024]{1,0:T(8,128)S(1)}, f32[32,1024]{1,0:T(8,128)S(1)}, u32[]{:S(2)}, u32[]{:S(2)}) collective-permute-start(f32[32,1024]{1,0:T(8,128)S(1)} %add.87), channel_id=1, source_target_pairs={{0,24},{1,25},{2,26},{3,27},{4,7},{5,6},{6,5},{7,4},{8,16},{9,17},... | collective-permute-start | bytes 393224 | tf_op jit(solution)/shard_map/ppermute | solution.py:179
  19.2 5.0 %collective-permute-start.7 = (f32[32,1024]{1,0:T(8,128)S(1)}, f32[32,1024]{1,0:T(8,128)S(1)}, u32[]{:S(2)}, u32[]{:S(2)}) collective-permute-start(f32[32,1024]{1,0:T(8,128)S(1)} %add.87), channel_id=1, source_target_pairs={{0,8},{1,9},{2,10},{3,11},{4,5},{5,4},{6,7},{7,6},{8,0},{9,1},{10,... | collective-permute-start | bytes 393224 | tf_op jit(solution)/shard_map/ppermute | solution.py:179
  19.7 5.0 %collective-permute-start.8 = (f32[32,1024]{1,0:T(8,128)S(1)}, f32[32,1024]{1,0:T(8,128)S(1)}, u32[]{:S(2)}, u32[]{:S(2)}) collective-permute-start(f32[32,1024]{1,0:T(8,128)S(1)} %add.87), channel_id=1, source_target_pairs={{0,16},{1,17},{2,18},{3,19},{4,6},{5,7},{6,4},{7,5},{8,24},{9,25},... | collective-permute-start | bytes 393224 | tf_op jit(solution)/shard_map/ppermute | solution.py:179
  24.8 2.7 %collective-permute-start.9 = (f32[16,1024]{1,0:T(8,128)S(1)}, f32[16,1024]{1,0:T(8,128)S(1)}, u32[]{:S(2)}, u32[]{:S(2)}) collective-permute-start(f32[16,1024]{1,0:T(8,128)S(1)} %get-tuple-element.46), channel_id=1, source_target_pairs={{0,4},{4,0},{8,12},{12,8},{16,20},{20,16},{24,28},{28,24},{1,5},{5... | collective-permute-start | bytes 196616 | tf_op jit(solution)/shard_map/ppermute | solution.py:167
  30.5 1.5 %collective-permute-start.10 = (f32[32,1024]{1,0:T(8,128)S(1)}, f32[32,1024]{1,0:T(8,128)S(1)}, u32[]{:S(2)}, u32[]{:S(2)}) collective-permute-start(f32[32,1024]{1,0:T(8,128)S(1)} %get-tuple-element.33), channel_id=1, source_target_pairs={{0,4},{4,0},{8,12},{12,8},{16,20},{20,16},{24,28},{28,24},{1,5},{5... | collective-permute-start | bytes 393224 | tf_op jit(solution)/shard_map/ppermute | solution.py:167
  31.9 5.9 %collective-permute-start.11 = (f32[32,1024]{1,0:T(8,128)S(1)}, f32[32,1024]{1,0:T(8,128)S(1)}, u32[]{:S(2)}, u32[]{:S(2)}) collective-permute-start(f32[32,1024]{1,0:T(8,128)S(1)} %add.92), channel_id=1, source_target_pairs={{0,24},{1,25},{2,26},{3,27},{4,7},{5,6},{6,5},{7,4},{8,16},{9,17},... | collective-permute-start | bytes 393224 | tf_op jit(solution)/shard_map/ppermute | solution.py:179
  33.5 5.8 %collective-permute-start.12 = (f32[32,1024]{1,0:T(8,128)S(1)}, f32[32,1024]{1,0:T(8,128)S(1)}, u32[]{:S(2)}, u32[]{:S(2)}) collective-permute-start(f32[32,1024]{1,0:T(8,128)S(1)} %add.92), channel_id=1, source_target_pairs={{0,8},{1,9},{2,10},{3,11},{4,5},{5,4},{6,7},{7,6},{8,0},{9,1},{10,... | collective-permute-start | bytes 393224 | tf_op jit(solution)/shard_map/ppermute | solution.py:179
  35.0 5.0 %collective-permute-start.13 = (f32[32,1024]{1,0:T(8,128)S(1)}, f32[32,1024]{1,0:T(8,128)S(1)}, u32[]{:S(2)}, u32[]{:S(2)}) collective-permute-start(f32[32,1024]{1,0:T(8,128)S(1)} %add.92), channel_id=1, source_target_pairs={{0,16},{1,17},{2,18},{3,19},{4,6},{5,7},{6,4},{7,5},{8,24},{9,25},... | collective-permute-start | bytes 393224 | tf_op jit(solution)/shard_map/ppermute | solution.py:179
  40.0 1.7 %collective-permute-start.14 = (f32[16,1024]{1,0:T(8,128)S(1)}, f32[16,1024]{1,0:T(8,128)S(1)}, u32[]{:S(2)}, u32[]{:S(2)}) collective-permute-start(f32[16,1024]{1,0:T(8,128)S(1)} %get-tuple-element.44), channel_id=1, source_target_pairs={{0,4},{4,0},{8,12},{12,8},{16,20},{20,16},{24,28},{28,24},{1,5},{5... | collective-permute-start | bytes 196616 | tf_op jit(solution)/shard_map/ppermute | solution.py:167
  44.8 1.5 %collective-permute-start.15 = (f32[32,1024]{1,0:T(8,128)S(1)}, f32[32,1024]{1,0:T(8,128)S(1)}, u32[]{:S(2)}, u32[]{:S(2)}) collective-permute-start(f32[32,1024]{1,0:T(8,128)S(1)} %get-tuple-element.37), channel_id=1, source_target_pairs={{0,4},{4,0},{8,12},{12,8},{16,20},{20,16},{24,28},{28,24},{1,5},{5... | collective-permute-start | bytes 393224 | tf_op jit(solution)/shard_map/ppermute | solution.py:167
  46.4 5.9 %collective-permute-start.16 = (f32[32,1024]{1,0:T(8,128)S(1)}, f32[32,1024]{1,0:T(8,128)S(1)}, u32[]{:S(2)}, u32[]{:S(2)}) collective-permute-start(f32[32,1024]{1,0:T(8,128)S(1)} %add.97), channel_id=1, source_target_pairs={{0,24},{1,25},{2,26},{3,27},{4,7},{5,6},{6,5},{7,4},{8,16},{9,17},... | collective-permute-start | bytes 393224 | tf_op jit(solution)/shard_map/ppermute | solution.py:179
  47.7 5.4 %collective-permute-start.17 = (f32[32,1024]{1,0:T(8,128)S(1)}, f32[32,1024]{1,0:T(8,128)S(1)}, u32[]{:S(2)}, u32[]{:S(2)}) collective-permute-start(f32[32,1024]{1,0:T(8,128)S(1)} %add.97), channel_id=1, source_target_pairs={{0,8},{1,9},{2,10},{3,11},{4,5},{5,4},{6,7},{7,6},{8,0},{9,1},{10,... | collective-permute-start | bytes 393224 | tf_op jit(solution)/shard_map/ppermute | solution.py:179
  48.7 5.0 %collective-permute-start.18 = (f32[32,1024]{1,0:T(8,128)S(1)}, f32[32,1024]{1,0:T(8,128)S(1)}, u32[]{:S(2)}, u32[]{:S(2)}) collective-permute-start(f32[32,1024]{1,0:T(8,128)S(1)} %add.97), channel_id=1, source_target_pairs={{0,16},{1,17},{2,18},{3,19},{4,6},{5,7},{6,4},{7,5},{8,24},{9,25},... | collective-permute-start | bytes 393224 | tf_op jit(solution)/shard_map/ppermute | solution.py:179
  53.8 2.5 %collective-permute-start.19 = (f32[16,1024]{1,0:T(8,128)S(1)}, f32[16,1024]{1,0:T(8,128)S(1)}, u32[]{:S(2)}, u32[]{:S(2)}) collective-permute-start(f32[16,1024]{1,0:T(8,128)S(1)} %get-tuple-element.42), channel_id=1, source_target_pairs={{0,4},{4,0},{8,12},{12,8},{16,20},{20,16},{24,28},{28,24},{1,5},{5... | collective-permute-start | bytes 196616 | tf_op jit(solution)/shard_map/ppermute | solution.py:167
  59.2 1.5 %collective-permute-start.20 = (f32[32,1024]{1,0:T(8,128)S(1)}, f32[32,1024]{1,0:T(8,128)S(1)}, u32[]{:S(2)}, u32[]{:S(2)}) collective-permute-start(f32[32,1024]{1,0:T(8,128)S(1)} %get-tuple-element.41), channel_id=1, source_target_pairs={{0,4},{4,0},{8,12},{12,8},{16,20},{20,16},{24,28},{28,24},{1,5},{5... | collective-permute-start | bytes 393224 | tf_op jit(solution)/shard_map/ppermute | solution.py:167
  60.7 4.9 %collective-permute-start.21 = (f32[32,256]{1,0:T(8,128)S(1)}, f32[32,256]{1,0:T(8,128)S(1)}, u32[]{:S(2)}, u32[]{:S(2)}) collective-permute-start(f32[32,256]{1,0:T(8,128)S(1)} %get-tuple-element.48), channel_id=1, source_target_pairs={{0,24},{1,25},{2,26},{3,27},{4,7},{5,6},{6,5},{7,4},{8,16},{9,17},... | collective-permute-start | bytes 98312 | tf_op jit(solution)/shard_map/ppermute | solution.py:179
  62.1 3.9 %collective-permute-start.22 = (f32[32,256]{1,0:T(8,128)S(1)}, f32[32,256]{1,0:T(8,128)S(1)}, u32[]{:S(2)}, u32[]{:S(2)}) collective-permute-start(f32[32,256]{1,0:T(8,128)S(1)} %get-tuple-element.50), channel_id=1, source_target_pairs={{0,16},{1,17},{2,18},{3,19},{4,6},{5,7},{6,4},{7,5},{8,24},{9,25},... | collective-permute-start | bytes 98312 | tf_op jit(solution)/shard_map/ppermute | solution.py:179
  62.8 3.9 %collective-permute-start.23 = (f32[32,256]{1,0:T(8,128)S(1)}, f32[32,256]{1,0:T(8,128)S(1)}, u32[]{:S(2)}, u32[]{:S(2)}) collective-permute-start(f32[32,256]{1,0:T(8,128)S(1)} %get-tuple-element.49), channel_id=1, source_target_pairs={{0,8},{1,9},{2,10},{3,11},{4,5},{5,4},{6,7},{7,6},{8,0},{9,1},{10,... | collective-permute-start | bytes 98312 | tf_op jit(solution)/shard_map/ppermute | solution.py:179
  66.7 1.2 %collective-permute-start.24 = (f32[32,128]{1,0:T(8,128)S(1)}, f32[32,128]{1,0:T(8,128)S(1)}, u32[]{:S(2)}, u32[]{:S(2)}) collective-permute-start(f32[32,128]{1,0:T(8,128)S(1)} %get-tuple-element.57), channel_id=1, source_target_pairs={{0,4},{4,0},{8,12},{12,8},{16,20},{20,16},{24,28},{28,24},{1,5},{5... | collective-permute-start | bytes 49160 | tf_op jit(solution)/shard_map/ppermute | solution.py:167
